TPU v7x, 128 devices: a whole 4x4x4 slice. The times are simulated.
128 devices in a mesh: dp: 4 (over z), expert: 32 (over y, x, core).
Axes of the slice: x: 4, y: 4, z: 4, core: 2. Of those that a mesh axis runs over, the one named last changes fastest.
Arguments:
- grad_parts: bfloat16 [4, 8192, 7168], P('dp', 'expert'), may hold values from -3 to 3
- owner_slot: int32 [224], replicated, may hold values from 0 to 383, as said below
- stat_left: float32 [384, 512, 512], P(('dp', 'expert')), may hold values from -1 to 3, as said below
- stat_right: float32 [384, 512, 512], P(('dp', 'expert')), may hold values from -1 to 3, as said below
- root_left: bfloat16 [384, 512, 512], P(('dp', 'expert')), may hold values from -1 to 2, as said below
- root_right: bfloat16 [384, 512, 512], P(('dp', 'expert')), may hold values from -1 to 2, as said below
Outputs:
- new_left: float32 [384, 512, 512], P(('dp', 'expert'))
- new_right: float32 [384, 512, 512], P(('dp', 'expert'))
- updates: bfloat16 [8192, 7168], P('expert')
Inputs may be any that keep to these rules, and one draw needn't show every extreme that they name: `owner_slot`: the entries are distinct; slot t lies on device t // 3 with devices counted dp first, then expert. No device holds more than 3 blocks and some device of every index along expert holds exactly 3. The devices of each index along expert hold 7 blocks together. Of the blocks that meet the rows of one device along expert, at most 1 lie on devices of one index along expert, and some index gets exactly 1. `stat_left`: each slot is symmetric with its diagonal in 0.3 to 3. `stat_right`: each slot is symmetric with its diagonal in 0.3 to 3. `root_left`: each slot is symmetric with its diagonal in 0.5 to 2. `root_right`: each slot is symmetric with its diagonal in 0.5 to 2.
All inputs are finite; a program needn't handle non-finite values.
Results may differ from a plain program's by a relative error of at most 0.017.
Values may be sent and summed in bfloat16 or wider, within the bound.
No kernel may reach another device: no remote copies, remote signals or barrier semaphores. Data moves between devices by JAX's collectives and lax.ppermute only.
A program may use at most 128 MiB of HBM per device.

v0:
```python
import jax
import jax.numpy as jnp
from jax import lax
from jax.sharding import PartitionSpec as P

BLOCK = 512


DECAY_RATE = 0.999


def shards(grad_parts, owner_slot, stat_left, stat_right, root_left, root_right):
    dp_count = lax.axis_size("dp")
    expert_count = lax.axis_size("expert")
    shard_rows = grad_parts.shape[1]
    row_width = grad_parts.shape[2]
    slot_count = stat_left.shape[0]
    wide_count = row_width // BLOCK
    piece_rows = min(shard_rows, BLOCK)
    pieces = shard_rows // piece_rows * wide_count
    capacity = -(-pieces // expert_count)
    quarters = BLOCK // piece_rows
    block_count = owner_slot.shape[0]
    all_count = slot_count * dp_count * expert_count
    blocks = jnp.arange(block_count, dtype=jnp.int32)
    row_block = blocks // wide_count
    block_group = row_block * BLOCK // max(shard_rows, BLOCK)
    column = owner_slot // slot_count % expert_count
    same_col = (column[None, :] == column[:, None]) & (block_group[None, :] == block_group[:, None])
    col_rank = jnp.sum(same_col & (blocks[None, :] < blocks[:, None]), axis=1)
    my_expert = lax.axis_index("expert")
    local_piece = jnp.arange(pieces, dtype=jnp.int32)
    piece_block = (
        my_expert * shard_rows // BLOCK + local_piece // wide_count
    ) * wide_count + local_piece % wide_count
    flat_pos = column[piece_block] * capacity + col_rank[piece_block]
    send_index = jnp.zeros((expert_count * capacity,), jnp.int32).at[flat_pos].set(local_piece)
    send_valid = jnp.zeros((expert_count * capacity,), jnp.bfloat16).at[flat_pos].set(1.0)
    send_index = send_index.reshape(expert_count, capacity)
    send_valid = send_valid.reshape(expert_count, capacity)
    layout = grad_parts[0].reshape(shard_rows // piece_rows, piece_rows, wide_count, BLOCK)
    outgoing = (
        layout[send_index // wide_count, :, send_index % wide_count, :]
        * send_valid[:, :, None, None]
    )
    slot_block = jnp.full((all_count,), -1, jnp.int32).at[owner_slot].set(blocks)
    slot_ids = (
        jnp.arange(dp_count, dtype=jnp.int32)[:, None] * expert_count + my_expert
    ) * slot_count + jnp.arange(slot_count, dtype=jnp.int32)[None, :]
    held_block = slot_block[slot_ids]
    used_slot = held_block >= 0
    held_safe = jnp.maximum(held_block, 0)
    part_index = jnp.arange(quarters, dtype=jnp.int32)
    source_idx = (row_block[held_safe][:, :, None] * BLOCK + part_index * piece_rows) // shard_rows
    rank_index = jnp.broadcast_to(col_rank[held_safe][:, :, None], source_idx.shape)
    incoming = lax.all_to_all(outgoing, "expert", split_axis=0, concat_axis=0, tiled=True)
    assembled = incoming[source_idx, rank_index].reshape(dp_count, slot_count, BLOCK, BLOCK)
    block_terms = jnp.where(used_slot[:, :, None, None], assembled.astype(jnp.float32), 0.0)
    grad_low = (
        lax.psum_scatter(block_terms.astype(jnp.bfloat16), "dp", scatter_dimension=0, tiled=True)
        .astype(jnp.float32)[0]
        .astype(jnp.bfloat16)
    )
    left_gram = jnp.einsum("sij,skj->sik", grad_low, grad_low, preferred_element_type=jnp.float32)
    right_gram = jnp.einsum("sji,sjk->sik", grad_low, grad_low, preferred_element_type=jnp.float32)
    new_left = DECAY_RATE * stat_left + (1.0 - DECAY_RATE) * left_gram
    new_right = DECAY_RATE * stat_right + (1.0 - DECAY_RATE) * right_gram
    left_part = jnp.einsum(
        "sij,sjk->sik", root_left, grad_low, preferred_element_type=jnp.float32
    ).astype(jnp.bfloat16)
    update = jnp.einsum(
        "sij,sjk->sik", left_part, root_right, preferred_element_type=jnp.float32
    ).astype(jnp.bfloat16)
    column_updates = lax.all_gather(update, "dp", axis=0, tiled=True)
    dest_index = jnp.arange(expert_count, dtype=jnp.int32)[:, None]
    piece_index = jnp.arange(pieces, dtype=jnp.int32)[None, :]
    back_block = (
        dest_index * shard_rows // BLOCK + piece_index // wide_count
    ) * wide_count + piece_index % wide_count
    is_mine = column[back_block] == my_expert
    back_slot = owner_slot[back_block]
    owner_pos = back_slot // (slot_count * expert_count) * slot_count + back_slot % slot_count
    row_part = jnp.maximum(dest_index * shard_rows - row_block[back_block] * BLOCK, 0) // piece_rows
    target = jnp.where(
        is_mine, dest_index * capacity + col_rank[back_block], expert_count * capacity
    )
    back_index = (
        jnp.zeros((expert_count * capacity,), jnp.int32)
        .at[target]
        .set(owner_pos * quarters + row_part, mode="drop")
    )
    back_valid = (
        jnp.zeros((expert_count * capacity,), jnp.bfloat16).at[target].set(1.0, mode="drop")
    )
    source_view = column_updates.reshape(dp_count * slot_count * quarters, piece_rows, BLOCK)
    outgoing_back = source_view[back_index] * back_valid[:, None, None]
    outgoing_back = outgoing_back.reshape(expert_count, capacity, piece_rows, BLOCK)
    returned = lax.all_to_all(outgoing_back, "expert", split_axis=0, concat_axis=0, tiled=True)
    fetched = returned[column[piece_block], col_rank[piece_block]]
    result = fetched.reshape(shard_rows // piece_rows, wide_count, piece_rows, BLOCK).transpose(
        0, 2, 1, 3
    )
    return (new_left, new_right, result.reshape(shard_rows, row_width))


def solution(mesh):
    return jax.shard_map(
        shards,
        mesh=mesh,
        in_specs=(
            P("dp", "expert", None),
            P(),
            P(("dp", "expert"), None, None),
            P(("dp", "expert"), None, None),
            P(("dp", "expert"), None, None),
            P(("dp", "expert"), None, None),
        ),
        out_specs=(
            P(("dp", "expert"), None, None),
            P(("dp", "expert"), None, None),
            P("expert", None),
        ),
        check_vma=False,
    )
```

profile of v0, /device:TPU:0, one launch (start us, length us, event | category | flops | bytes accessed | tf_op | source)
XLA Modules:
  0.0 450.7 jit_solution(15695909711104956676)
XLA Ops:
  7.2 0.8 compare_select_fusion.4
  8.3 0.7 gather_fusion.1
  8.9 0.7 gather_fusion.2
  10.3 5.9 %copy.34 = bf16[1,256,7168]{1,2,0:T(8,128)(2,1)} copy(bf16[1,256,7168]{2,1,0:T(8,128)(2,1)} %param.6) | data formatting | bytes 7340032 | tf_op args[0]
  16.2 5.9 %copy.35 = bf16[1,256,14,512]{3,1,2,0:T(8,128)(2,1)} copy(bf16[1,256,14,512]{1,3,2,0:T(8,128)(2,1)} %bitcast.68) | data formatting | bytes 7340032 | tf_op jit(solution)/shard_map/reshape;squeeze | solution.py:41
  22.8 7.0 %gather_fusion.3 = bf16[32,256,512]{2,1,0:T(8,128)(2,1)} fusion(bf16[1,256,14,512]{3,1,2,0:T(8,128)(2,1)} %copy.35, s32[32]{0:T(128)S(1)} %or_bitcast_fusion), kind=kCustom, calls=%fused_computation.3 | custom fusion | bytes 16777472 | tf_op jit(solution)/shard_map/gather | solution.py:43
  29.8 7.2 %fusion.1 = bf16[32,1,256,512]{3,2,1,0:T(8,128)(2,1)} fusion(bf16[32,256,512]{2,1,0:T(8,128)(2,1)} %gather_fusion.3, bf16[32]{0:T(256)(128)(2,1)S(1)} %scatter_custom_fusion.2), kind=kLoop, calls=%fused_computation.22 | loop fusion | flops 4194304 | bytes 16777280 | tf_op jit(solution)/shard_map/mul | solution.py:43
  37.0 7.5 %all-to-all-start = ((bf16[32,1,256,512]{3,2,1,0:T(8,128)(2,1)}), bf16[32,1,256,512]{3,2,1,0:T(8,128)(2,1)}, u32[]{:S(2)}, u32[]{:S(2)}) async-start(bf16[32,1,256,512]{3,2,1,0:T(8,128)(2,1)} %fusion.1), calls=%async_computation | async-start | bytes 16777216 | tf_op jit(solution)/shard_map/all_to_all | solution.py:56
  44.7 1.3 scatter_custom_fusion
  46.0 0.7 gather_fusion
  47.5 0.7 gather_fusion.4
  48.5 101.8 %all-to-all-done = bf16[32,1,256,512]{3,2,1,0:T(8,128)(2,1)} async-done(((bf16[32,1,256,512]{3,2,1,0:T(8,128)(2,1)}), bf16[32,1,256,512]{3,2,1,0:T(8,128)(2,1)}, u32[]{:S(2)}, u32[]{:S(2)}) %all-to-all-start) | async-done | bytes 8388640 | tf_op jit(solution)/shard_map/all_to_all | solution.py:56
  150.4 7.9 %gather_fusion.6 = bf16[24,256,512]{2,1,0:T(8,128)(2,1)} fusion(bf16[32,1,256,512]{3,2,1,0:T(8,128)(2,1)} %all-to-all-done, s32[24]{0:T(128)S(1)} %reshape.571), kind=kCustom, calls=%fused_computation.6 | custom fusion | bytes 12583104 | tf_op jit(solution)/shard_map/gather | solution.py:57
  158.3 7.1 %fusion = bf16[4,3,512,512]{3,2,1,0:T(8,128)(2,1)} fusion(bf16[4,3,512,512]{3,2,1,0:T(8,128)(2,1)} %bitcast.66, pred[4,3]{1,0:T(4,128)(4,1)S(1)} %reshape.678), kind=kLoop, calls=%fused_computation.19 | loop fusion | flops 9437184 | bytes 12582924 | tf_op jit(solution)/shard_map/convert_element_type | solution.py:60
  165.6 61.8 %reduce-scatter.2.cloned.1.call-done = bf16[1,3,512,512]{3,2,1,0:T(8,128)(2,1)} async-done(((bf16[4,3,512,512]{3,2,1,0:T(8,128)(2,1)}), bf16[1,3,512,512]{3,2,1,0:T(8,128)(2,1)}) %reduce-scatter.2.cloned.1.call-update) | async-done | bytes 1572880 | tf_op jit(solution)/shard_map/reduce_scatter | solution.py:60
  227.5 4.6 %convolution_convert_fusion = bf16[3,512,512]{2,1,0:T(8,128)(2,1)} fusion(bf16[3,512,512]{2,1,0:T(8,128)(2,1)S(1)} %copy-done, bf16[3,512,512]{2,1,0:T(8,128)(2,1)S(1)} %copy-done.5, bf16[1,3,512,512]{3,2,1,0:T(8,128)(2,1)} %reduce-scatter.2.cloned.1.call-done), kind=kOutput, calls=%fused_computation.25 | convolution fusion | flops 1612185600 | bytes 6291456 | tf_op jit(solution)/shard_map/sij,sjk->sik/dot_general | solution.py:71
  232.3 3.2 gather_fusion.10
  235.5 3.2 gather_fusion.8
  238.7 3.2 gather_fusion.7
  241.9 3.2 gather_fusion.9
  246.1 3.4 scatter_custom_fusion.4
  249.5 2.9 scatter_custom_fusion.3
  252.4 45.3 %all-gather.2.cloned.1.call-done = bf16[12,512,512]{2,1,0:T(8,128)(2,1)} async-done(((bf16[3,512,512]{2,1,0:T(8,128)(2,1)}), bf16[12,512,512]{2,1,0:T(8,128)(2,1)}) %all-gather.2.cloned.1.call-update) | async-done | bytes 6291472 | tf_op jit(solution)/shard_map/all_gather | solution.py:74
  297.7 7.7 %gather_fusion.11 = bf16[32,256,512]{2,1,0:T(8,128)(2,1)} fusion(bf16[24,256,512]{2,1,0:T(8,128)(2,1)} %bitcast.70, s32[1024]{0:T(1024)S(1)} %pad_clamp_fusion), kind=kCustom, calls=%fused_computation.11 | custom fusion | bytes 16777344 | tf_op jit(solution)/shard_map/gather | solution.py:96
  305.5 7.2 %bitcast_multiply_fusion = bf16[32,1,256,512]{3,2,1,0:T(8,128)(2,1)} fusion(bf16[32,256,512]{2,1,0:T(8,128)(2,1)} %gather_fusion.11, bf16[32]{0:T(256)(128)(2,1)S(1)} %scatter_custom_fusion.4), kind=kLoop, calls=%fused_computation.20 | loop fusion | flops 4194304 | bytes 16777280 | tf_op jit(solution)/shard_map/mul | solution.py:96
  312.7 7.6 %all-to-all-start.1 = ((bf16[32,1,256,512]{3,2,1,0:T(8,128)(2,1)}), bf16[32,1,256,512]{3,2,1,0:T(8,128)(2,1)}, u32[]{:S(2)}, u32[]{:S(2)}) async-start(bf16[32,1,256,512]{3,2,1,0:T(8,128)(2,1)} %bitcast_multiply_fusion), calls=%async_computation.2 | async-start | bytes 16777216 | tf_op jit(solution)/shard_map/all_to_all | solution.py:98
  320.3 4.9 %multiply_add_fusion = f32[3,512,512]{2,1,0:T(8,128)} fusion(f32[3,512,512]{2,1,0:T(8,128)} %param.9, bf16[1,3,512,512]{3,2,1,0:T(8,128)(2,1)S(1)} %copy-done.3), kind=kOutput, calls=%fused_computation.23 | convolution fusion | flops 807665664 | bytes 7864320 | tf_op jit(solution)/shard_map/sji,sjk->sik/dot_general | solution.py:65
  325.2 2.8 multiply_add_fusion.1
  327.9 98.0 %all-to-all-done.1 = bf16[32,1,256,512]{3,2,1,0:T(8,128)(2,1)} async-done(((bf16[32,1,256,512]{3,2,1,0:T(8,128)(2,1)}), bf16[32,1,256,512]{3,2,1,0:T(8,128)(2,1)}, u32[]{:S(2)}, u32[]{:S(2)}) %all-to-all-start.1) | async-done | bytes 8388640 | tf_op jit(solution)/shard_map/all_to_all | solution.py:98
  425.9 6.0 %gather_fusion.12 = bf16[14,256,512]{2,1,0:T(8,128)(2,1)} fusion(bf16[32,1,256,512]{3,2,1,0:T(8,128)(2,1)} %all-to-all-done.1, s32[14]{0:T(128)S(1)} %get-tuple-element.17), kind=kCustom, calls=%fused_computation.12 | custom fusion | bytes 7340144 | tf_op jit(solution)/shard_map/gather | solution.py:99
  431.9 5.9 %copy.40 = bf16[1,256,14,512]{1,3,2,0:T(8,128)(2,1)} copy(bf16[1,256,14,512]{3,1,2,0:T(8,128)(2,1)} %bitcast.69) | data formatting | bytes 7340032 | tf_op jit(solution)/shard_map/transpose | solution.py:100
  437.8 6.0 %copy.41 = bf16[256,7168]{1,0:T(8,128)(2,1)} copy(bf16[256,7168]{0,1:T(8,128)(2,1)} %bitcast.67) | data formatting | bytes 7340032
  (69 shorter events, 4.4 us)
Async XLA Ops:
  7.2 220.3 %copy-start = (bf16[3,512,512]{2,1,0:T(8,128)(2,1)S(1)}, bf16[3,512,512]{2,1,0:T(8,128)(2,1)}, u32[]{:S(2)}) copy-start(bf16[3,512,512]{2,1,0:T(8,128)(2,1)} %param.11) | copy-start | bytes 4718596
  37.0 113.4 %all-to-all-start = ((bf16[32,1,256,512]{3,2,1,0:T(8,128)(2,1)}), bf16[32,1,256,512]{3,2,1,0:T(8,128)(2,1)}, u32[]{:S(2)}, u32[]{:S(2)}) async-start(bf16[32,1,256,512]{3,2,1,0:T(8,128)(2,1)} %fusion.1), calls=%async_computation | async-start | bytes 16777216 | tf_op jit(solution)/shard_map/all_to_all | solution.py:56
  44.5 183.0 %reduce-scatter.2.cloned.1.call-start = ((), (), s32[]{:S(2)}) async-start(), calls=%async_computation.3 | async-start | bytes 7864320 | tf_op jit(solution)/shard_map/reduce_scatter | solution.py:60
  165.4 62.1 %copy-start.5 = (bf16[3,512,512]{2,1,0:T(8,128)(2,1)S(1)}, bf16[3,512,512]{2,1,0:T(8,128)(2,1)}, u32[]{:S(2)}) copy-start(bf16[3,512,512]{2,1,0:T(8,128)(2,1)} %param.10) | copy-start | bytes 4718596
  165.4 132.3 %all-gather.2.cloned.1.call-start = ((), (), s32[]{:S(2)}) async-start(), calls=%async_computation.4 | async-start | bytes 7864320 | tf_op jit(solution)/shard_map/all_gather | solution.py:74
  238.7 3.2 copy-start.2
  312.7 7.6 %copy-start.3 = (bf16[1,3,512,512]{3,2,1,0:T(8,128)(2,1)S(1)}, bf16[1,3,512,512]{3,2,1,0:T(8,128)(2,1)}, u32[]{:S(2)}) copy-start(bf16[1,3,512,512]{3,2,1,0:T(8,128)(2,1)} %reduce-scatter.2.cloned.1.call-done) | copy-start | bytes 4718596
  312.7 113.2 %all-to-all-start.1 = ((bf16[32,1,256,512]{3,2,1,0:T(8,128)(2,1)}), bf16[32,1,256,512]{3,2,1,0:T(8,128)(2,1)}, u32[]{:S(2)}, u32[]{:S(2)}) async-start(bf16[32,1,256,512]{3,2,1,0:T(8,128)(2,1)} %bitcast_multiply_fusion), calls=%async_computation.2 | async-start | bytes 16777216 | tf_op jit(solution)/shard_map/all_to_all | solution.py:98
  320.3 4.9 %copy-start.4 = (f32[3,512,512]{2,1,0:T(8,128)S(1)}, f32[3,512,512]{2,1,0:T(8,128)}, u32[]{:S(2)}) copy-start(f32[3,512,512]{2,1,0:T(8,128)} %param.8) | copy-start | bytes 9437188
  437.8 6.0 %copy-start.1 = (bf16[3,512,512]{2,1,0:T(8,128)(2,1)S(1)}, bf16[3,512,512]{2,1,0:T(8,128)(2,1)}, u32[]{:S(2)}) copy-start(bf16[3,512,512]{2,1,0:T(8,128)(2,1)} %param.11) | copy-start | bytes 4718596
Sparse Core Ops, SparseCore 0:
  165.5 61.8 reduce-scatter.1
  232.2 65.4 all-gather.1
where the time goes:
time: 452 us; the launch traced here: 451 us
  waiting for transfers between devices  307 us (68%)
  local copies, waits for them, and re-layouts  78.6 us (17%)
  other arithmetic  23.1 us (5%)
  starting transfers between devices  15.4 us (3%)
  between operations  14.4 us (3%)
  matrix products  12.2 us (3%)
    all_to_all x1, waiting for transfers between devices, shards(): lax.all_to_all(outgoing, 'expert', split_axis=0, concat_axis=0, tiled=True)  102 us
    all_to_all x1, waiting for transfers between devices, shards(): lax.all_to_all(outgoing_back, 'expert', split_axis=0, concat_axis=0, tile...  98 us
    reduce_scatter x1, waiting for transfers between devices, shards(): lax.psum_scatter(block_terms.astype(jnp.bfloat16), 'dp', scatter_dimensio...  61.8 us
    all_gather x1, waiting for transfers between devices, shards(): column_updates = lax.all_gather(update, 'dp', axis=0, tiled=True)  45.3 us
    unnamed x14, local copies, waits for them, and re-layouts  12 us
  transfers between devices with their start and end apart: 4, of which 4 were waited for; matrix products, arithmetic and copies ran while one was open for 7% of the time, Pallas kernels for 0%

commit v1 on v0

v1 whole, which is shorter than its diff:
```python
import jax
import jax.numpy as jnp
from jax import lax
from jax.sharding import PartitionSpec as P

DECAY_RATE = 0.999
CHUNKS = 2


def shards(grad_parts, owner_slot, stat_left, stat_right, root_left, root_right):
    dp_count = lax.axis_size("dp")
    expert_count = lax.axis_size("expert")
    shard_rows = grad_parts.shape[1]
    row_width = grad_parts.shape[2]
    slot_count, block_rows, block_cols = stat_left.shape
    wide_count = row_width // block_cols
    halves = block_rows // shard_rows
    row_blocks = expert_count // halves
    block_count = owner_slot.shape[0]
    chunk_rows = shard_rows // CHUNKS
    part_rows = chunk_rows // dp_count
    held_count = dp_count * slot_count

    my_expert = lax.axis_index("expert")
    blocks = jnp.arange(block_count, dtype=jnp.int32)
    column = owner_slot // slot_count % expert_count

    my_column = lax.dynamic_slice(column, (my_expert // halves * wide_count,), (wide_count,))
    to_column = my_column[None, :] == jnp.arange(expert_count, dtype=jnp.int32)[:, None]
    pieces = jnp.arange(wide_count, dtype=jnp.int32)
    send_piece = jnp.sum(jnp.where(to_column, pieces[None, :], 0), axis=1)

    held = jnp.arange(held_count, dtype=jnp.int32)
    slot_ids = (held // slot_count * expert_count + my_expert) * slot_count + held % slot_count
    holds = owner_slot[None, :] == slot_ids[:, None]
    held_row = jnp.sum(jnp.where(holds, blocks[None, :] // wide_count, 0), axis=1)
    held_used = jnp.any(holds, axis=1)
    row_ids = jnp.arange(row_blocks, dtype=jnp.int32)
    from_held = (held_row[None, :] == row_ids[:, None]) & held_used[None, :]
    back_held = jnp.sum(jnp.where(from_held, held[None, :], 0), axis=1)
    my_used = lax.dynamic_slice(held_used, (lax.axis_index("dp") * slot_count,), (slot_count,))

    gathered = []
    for chunk in range(CHUNKS):
        rows = grad_parts[0, chunk * chunk_rows : (chunk + 1) * chunk_rows]
        part = lax.psum_scatter(rows, "dp", scatter_dimension=0, tiled=True)
        layout = part.reshape(part_rows, wide_count, block_cols).transpose(1, 0, 2)
        incoming = lax.all_to_all(layout[send_piece], "expert", split_axis=0, concat_axis=0, tiled=True)
        by_row = incoming.reshape(row_blocks, halves, part_rows, block_cols)
        to_owner = by_row[held_row].reshape(dp_count, slot_count, halves, part_rows, block_cols)
        gathered.append(lax.all_to_all(to_owner, "dp", split_axis=0, concat_axis=0, tiled=True))
    grad = jnp.stack(gathered).transpose(2, 3, 0, 1, 4, 5)
    grad = grad.reshape(slot_count, block_rows, block_cols)
    grad = jnp.where(my_used[:, None, None], grad, jnp.zeros_like(grad))

    left_part = jnp.einsum("sij,sjk->sik", root_left, grad, preferred_element_type=jnp.float32).astype(jnp.bfloat16)
    update = jnp.einsum("sij,sjk->sik", left_part, root_right, preferred_element_type=jnp.float32).astype(jnp.bfloat16)
    update = update.reshape(slot_count, halves, CHUNKS, dp_count, part_rows, block_cols)

    out = []
    for chunk in range(CHUNKS):
        to_replica = update[:, :, chunk].transpose(2, 0, 1, 3, 4)
        column_part = lax.all_to_all(to_replica, "dp", split_axis=0, concat_axis=0, tiled=True)
        column_part = column_part.reshape(held_count, halves, part_rows, block_cols)
        to_rows = column_part[back_held].reshape(expert_count, part_rows, block_cols)
        returned = lax.all_to_all(to_rows, "expert", split_axis=0, concat_axis=0, tiled=True)
        part = returned[my_column].transpose(1, 0, 2).reshape(part_rows, row_width)
        out.append(lax.all_gather(part, "dp", axis=0, tiled=True))
    updates = jnp.concatenate(out, axis=0)

    left_gram = jnp.einsum("sij,skj->sik", grad, grad, preferred_element_type=jnp.float32)
    right_gram = jnp.einsum("sji,sjk->sik", grad, grad, preferred_element_type=jnp.float32)
    new_left = DECAY_RATE * stat_left + (1.0 - DECAY_RATE) * left_gram
    new_right = DECAY_RATE * stat_right + (1.0 - DECAY_RATE) * right_gram
    return new_left, new_right, updates


def solution(mesh):
    owned = P(("dp", "expert"), None, None)
    return jax.shard_map(
        shards,
        mesh=mesh,
        in_specs=(P("dp", "expert", None), P(), owned, owned, owned, owned),
        out_specs=(owned, owned, P("expert", None)),
        check_vma=False,
    )
```

time: 452 us -> 277 us (0.61)
  waiting for transfers between devices: 307 us -> 133 us
  blocking collectives: 0 us -> 46 us
  local copies, waits for them, and re-layouts: 78.6 us -> 32.7 us
  other arithmetic: 23.1 us -> 5.23 us
  starting transfers between devices: 15.4 us -> 31.2 us
    all_to_all x2 -> x6, waiting for transfers between devices: 200 us -> 65.6 us  [the longest x2 21.8 us: shards(): lax.all_to_all(to_owner, 'dp', split_axis=0, concat_axis=0, tiled=True)]
    all_to_all x0 -> x2, blocking collectives: none -> 46 us  [the longest x1 24 us: shards(): lax.all_to_all(to_replica, 'dp', split_axis=0, concat_axis=0, tiled=True)]
    all_gather x1 -> x2, waiting for transfers between devices: 45.3 us -> 17 us  [shards(): out.append(lax.all_gather(part, 'dp', axis=0, tiled=True))]
    gather x15 -> x8, local copies, waits for them, and re-layouts: 44.8 us -> 18 us  [the longest x2 5.43 us: shards(): column_part[back_held].reshape(expert_count, part_rows, block_cols)]
    all_to_all x2 -> x6, starting transfers between devices: 15.1 us -> 31 us  [the longest x2 14.3 us: shards(): lax.all_to_all(layout[send_piece], 'expert', split_axis=0, concat_axis=0,...]
    mul x7 -> x0, other arithmetic: 14.4 us -> none  [the longest x1 7.21 us: shards(): layout[send_index // wide_count, :, send_index % wide_count, :]]
    reduce_scatter x1 -> x2, waiting for transfers between devices: 61.8 us -> 50 us  [shards(): part = lax.psum_scatter(rows, 'dp', scatter_dimension=0, tiled=True)]
    unnamed x14 -> x8, local copies, waits for them, and re-layouts: 12 us -> 2.15 us
  transfers between devices with their start and end apart: 4 -> 10, of which waited for: 4 -> 8; matrix products, arithmetic and copies ran while one was open for 7% -> 10% of each run, Pallas kernels for 0% -> 0%
where the time goes in v1:
time: 277 us; the launch traced here: 275 us
  waiting for transfers between devices  133 us (48%)
  blocking collectives  46 us (17%)
  local copies, waits for them, and re-layouts  32.7 us (12%)
  starting transfers between devices  31.2 us (11%)
  between operations  14 us (5%)
  matrix products  12.2 us (4%)
  other arithmetic  5.23 us (2%)
    reduce_scatter x2, waiting for transfers between devices, shards(): part = lax.psum_scatter(rows, 'dp', scatter_dimension=0, tiled=True)  50 us
    all_to_all x1, blocking collectives, shards(): lax.all_to_all(to_replica, 'dp', split_axis=0, concat_axis=0, tiled=True)  24 us
    all_to_all x1, blocking collectives, shards(): lax.all_to_all(to_rows, 'expert', split_axis=0, concat_axis=0, tiled=True)  22 us
    all_to_all x2, waiting for transfers between devices, shards(): lax.all_to_all(to_owner, 'dp', split_axis=0, concat_axis=0, tiled=True)  21.8 us
    all_to_all x1, waiting for transfers between devices, shards(): lax.all_to_all(to_rows, 'expert', split_axis=0, concat_axis=0, tiled=True)  17.2 us
    all_gather x2, waiting for transfers between devices, shards(): out.append(lax.all_gather(part, 'dp', axis=0, tiled=True))  17 us
    all_to_all x2, waiting for transfers between devices, shards(): lax.all_to_all(layout[send_piece], 'expert', split_axis=0, concat_axis=0,...  15.6 us
    all_to_all x2, starting transfers between devices, shards(): lax.all_to_all(layout[send_piece], 'expert', split_axis=0, concat_axis=0,...  14.3 us
  transfers between devices with their start and end apart: 10, of which 8 were waited for; matrix products, arithmetic and copies ran while one was open for 10% of the time, Pallas kernels for 0%

profile of v1, /device:TPU:0, one launch (start us, length us, event | category | flops | bytes accessed | tf_op | source)
XLA Modules:
  0.0 274.6 jit_solution(6378663892023022560)
XLA Ops:
  7.2 4.2 %slice_bitcast_fusion.1 = (bf16[128,7168]{1,0:T(8,128)(2,1)}, bf16[128,7168]{1,0:T(8,128)(2,1)}) fusion(bf16[1,256,7168]{2,1,0:T(8,128)(2,1)} %param.6), kind=kLoop, calls=%fused_computation.12 | loop fusion | bytes 7340032 | tf_op jit(solution)/shard_map/squeeze | solution.py:45
  12.5 29.4 %reduce-scatter.5.cloned.1.call-done = bf16[32,7168]{1,0:T(8,128)(2,1)} async-done(((bf16[128,7168]{1,0:T(8,128)(2,1)}), bf16[32,7168]{1,0:T(8,128)(2,1)}) %reduce-scatter.5.cloned.1.call-update) | async-done | bytes 458768 | tf_op jit(solution)/shard_map/reduce_scatter | solution.py:46
  43.0 1.6 gather_fusion.2
  44.5 7.1 %all-to-all-start.2 = ((bf16[32,32,512]{2,1,0:T(8,128)(2,1)}), bf16[32,32,512]{2,1,0:T(8,128)(2,1)S(1)}, u32[]{:S(2)}, u32[]{:S(2)}) async-start(bf16[32,32,512]{2,1,0:T(8,128)(2,1)} %gather_fusion.2), calls=%async_computation.4 | async-start | bytes 2097152 | tf_op jit(solution)/shard_map/all_to_all | solution.py:48
  51.6 20.6 %reduce-scatter.3.cloned.1.call-done = bf16[32,7168]{1,0:T(8,128)(2,1)} async-done(((bf16[128,7168]{1,0:T(8,128)(2,1)}), bf16[32,7168]{1,0:T(8,128)(2,1)}) %reduce-scatter.3.cloned.1.call-update) | async-done | bytes 458768 | tf_op jit(solution)/shard_map/reduce_scatter | solution.py:46
  73.3 1.6 gather_fusion
  74.9 7.2 %all-to-all-start = ((bf16[32,32,512]{2,1,0:T(8,128)(2,1)}), bf16[32,32,512]{2,1,0:T(8,128)(2,1)}, u32[]{:S(2)}, u32[]{:S(2)}) async-start(bf16[32,32,512]{2,1,0:T(8,128)(2,1)} %gather_fusion), calls=%async_computation.1 | async-start | bytes 2097152 | tf_op jit(solution)/shard_map/all_to_all | solution.py:48
  82.4 1.5 gather_fusion.3
  83.9 15.6 %all-to-all-done = bf16[32,32,512]{2,1,0:T(8,128)(2,1)} async-done(((bf16[32,32,512]{2,1,0:T(8,128)(2,1)}), bf16[32,32,512]{2,1,0:T(8,128)(2,1)}, u32[]{:S(2)}, u32[]{:S(2)}) %all-to-all-start) | async-done | bytes 1048608 | tf_op jit(solution)/shard_map/all_to_all | solution.py:48
  99.4 3.5 %all-to-all-start.3 = ((bf16[4,3,2,32,512]{4,3,2,1,0:T(8,128)(2,1)}), bf16[4,3,2,32,512]{4,3,2,1,0:T(8,128)(2,1)S(1)}, u32[]{:S(2)}, u32[]{:S(2)}) async-start(bf16[4,3,2,32,512]{4,3,2,1,0:T(8,128)(2,1)} %bitcast.74), calls=%async_computation.5 | async-start | bytes 1572864 | tf_op jit(solution)/shard_map/all_to_all | solution.py:51
  102.9 2.7 gather_fusion.1
  105.7 10.1 %all-to-all-done.3 = bf16[4,3,2,32,512]{4,3,2,1,0:T(8,128)(2,1)S(1)} async-done(((bf16[4,3,2,32,512]{4,3,2,1,0:T(8,128)(2,1)}), bf16[4,3,2,32,512]{4,3,2,1,0:T(8,128)(2,1)S(1)}, u32[]{:S(2)}, u32[]{:S(2)}) %all-to-all-start.3) | async-done | bytes 786464 | tf_op jit(solution)/shard_map/all_to_all | solution.py:51
  115.7 3.5 %all-to-all-start.1 = ((bf16[4,3,2,32,512]{4,3,2,1,0:T(8,128)(2,1)}), bf16[4,3,2,32,512]{4,3,2,1,0:T(8,128)(2,1)S(1)}, u32[]{:S(2)}, u32[]{:S(2)}) async-start(bf16[4,3,2,32,512]{4,3,2,1,0:T(8,128)(2,1)} %bitcast.7), calls=%async_computation.2 | async-start | bytes 1572864 | tf_op jit(solution)/shard_map/all_to_all | solution.py:51
  119.5 11.7 %all-to-all-done.1 = bf16[4,3,2,32,512]{4,3,2,1,0:T(8,128)(2,1)S(1)} async-done(((bf16[4,3,2,32,512]{4,3,2,1,0:T(8,128)(2,1)}), bf16[4,3,2,32,512]{4,3,2,1,0:T(8,128)(2,1)S(1)}, u32[]{:S(2)}, u32[]{:S(2)}) %all-to-all-start.1) | async-done | bytes 786464 | tf_op jit(solution)/shard_map/all_to_all | solution.py:51
  131.8 4.5 %convolution_convert_fusion = bf16[3,512,512]{2,1,0:T(8,128)(2,1)} fusion(bf16[3,512,512]{2,1,0:T(8,128)(2,1)S(1)} %copy-done, bf16[3,512,512]{2,1,0:T(8,128)(2,1)S(1)} %bitcast_select_fusion, bf16[3,512,512]{2,1,0:T(8,128)(2,1)} %param.10), kind=kOutput, calls=%fused_computation.13 | convolution fusion | flops 1612185600 | bytes 6291456 | tf_op jit(solution)/shard_map/sij,sjk->sik/dot_general | solution.py:57
  136.3 2.4 fusion.10
  139.6 4.2 %all-to-all-start.4 = ((bf16[4,3,2,32,512]{4,3,2,1,0:T(8,128)(2,1)}), bf16[4,3,2,32,512]{4,3,2,1,0:T(8,128)(2,1)}, u32[]{:S(2)}, u32[]{:S(2)}) async-start(bf16[4,3,2,32,512]{4,3,2,1,0:T(8,128)(2,1)} %bitcast.75), calls=%async_computation.6 | async-start | bytes 1572864 | tf_op jit(solution)/shard_map/all_to_all | solution.py:63
  144.0 11.0 %all-to-all-done.4 = bf16[4,3,2,32,512]{4,3,2,1,0:T(8,128)(2,1)} async-done(((bf16[4,3,2,32,512]{4,3,2,1,0:T(8,128)(2,1)}), bf16[4,3,2,32,512]{4,3,2,1,0:T(8,128)(2,1)}, u32[]{:S(2)}, u32[]{:S(2)}) %all-to-all-start.4) | async-done | bytes 786464 | tf_op jit(solution)/shard_map/all_to_all | solution.py:63
  155.0 2.7 gather_fusion.4
  157.7 5.5 %all-to-all-start.5 = ((bf16[32,32,512]{2,1,0:T(8,128)(2,1)}), bf16[32,32,512]{2,1,0:T(8,128)(2,1)}, u32[]{:S(2)}, u32[]{:S(2)}) async-start(bf16[32,32,512]{2,1,0:T(8,128)(2,1)} %bitcast.71), calls=%async_computation.7 | async-start | bytes 2097152 | tf_op jit(solution)/shard_map/all_to_all | solution.py:66
  163.3 17.2 %all-to-all-done.5 = bf16[32,32,512]{2,1,0:T(8,128)(2,1)} async-done(((bf16[32,32,512]{2,1,0:T(8,128)(2,1)}), bf16[32,32,512]{2,1,0:T(8,128)(2,1)}, u32[]{:S(2)}, u32[]{:S(2)}) %all-to-all-start.5) | async-done | bytes 1048608 | tf_op jit(solution)/shard_map/all_to_all | solution.py:66
  180.5 2.6 gather_fusion.5
  183.1 1.8 copy.37
  186.2 24.0 %all_to_all.40 = bf16[4,3,2,32,512]{4,3,2,1,0:T(8,128)(2,1)} all-to-all(bf16[4,3,2,32,512]{4,3,2,1,0:T(8,128)(2,1)S(1)} %bitcast.76), channel_id=1, replica_groups=mesh['dp'=4,'expert'=32] {'dp'}, dimensions={0} | all-to-all | bytes 1572864 | tf_op jit(solution)/shard_map/all_to_all | solution.py:63
  210.2 2.7 gather_fusion.6
  212.9 22.0 %all_to_all.41 = bf16[32,32,512]{2,1,0:T(8,128)(2,1)} all-to-all(bf16[32,32,512]{2,1,0:T(8,128)(2,1)} %bitcast.72), channel_id=1, replica_groups=mesh['dp'=4,'expert'=32] {'expert'}, dimensions={0} | all-to-all | bytes 2097152 | tf_op jit(solution)/shard_map/all_to_all | solution.py:66
  234.9 2.6 gather_fusion.7
  237.5 1.8 copy.38
  239.3 4.9 %multiply_add_fusion = f32[3,512,512]{2,1,0:T(8,128)} fusion(f32[3,512,512]{2,1,0:T(8,128)} %param.9, bf16[3,512,512]{2,1,0:T(8,128)(2,1)S(1)} %bitcast_select_fusion), kind=kOutput, calls=%fused_computation.9 | convolution fusion | flops 807665664 | bytes 7864320 | tf_op jit(solution)/shard_map/sji,sjk->sik/dot_general | solution.py:72
  244.2 2.8 %multiply_add_fusion.1 = f32[3,512,512]{2,1,0:T(8,128)} fusion(f32[3,512,512]{2,1,0:T(8,128)S(1)} %copy-done.1, bf16[3,512,512]{2,1,0:T(8,128)(2,1)S(1)} %bitcast_select_fusion), kind=kOutput, calls=%fused_computation.10 | convolution fusion | flops 807665664 | bytes 7864320 | tf_op jit(solution)/shard_map/sij,skj->sik/dot_general | solution.py:71
  247.0 17.0 %all-gather.5.cloned.1.call-done = bf16[128,7168]{1,0:T(8,128)(2,1)} async-done(((bf16[32,7168]{1,0:T(8,128)(2,1)}), bf16[128,7168]{1,0:T(8,128)(2,1)}) %all-gather.5.cloned.1.call-update) | async-done | bytes 1835024 | tf_op jit(solution)/shard_map/all_gather | solution.py:68
  264.0 4.1 %pad_maximum_fusion = bf16[256,7168]{1,0:T(8,128)(2,1)} fusion(bf16[128,7168]{1,0:T(8,128)(2,1)} %all-gather.5.cloned.1.call-done, bf16[128,7168]{1,0:T(8,128)(2,1)} %all-gather.3.cloned.1.call-done), kind=kLoop, calls=%fused_computation.8 | loop fusion | flops 7340032 | bytes 7340032 | tf_op jit(solution)/shard_map/concatenate | solution.py:69
  (39 shorter events, 6.5 us)
Async XLA Ops:
  7.2 124.6 %copy-start = (bf16[3,512,512]{2,1,0:T(8,128)(2,1)S(1)}, bf16[3,512,512]{2,1,0:T(8,128)(2,1)}, u32[]{:S(2)}) copy-start(bf16[3,512,512]{2,1,0:T(8,128)(2,1)} %param.11) | copy-start | bytes 4718596
  7.2 34.7 %reduce-scatter.5.cloned.1.call-start = ((), (), s32[]{:S(2)}) async-start(), calls=%async_computation.11 | async-start | bytes 2293760 | tf_op jit(solution)/shard_map/reduce_scatter | solution.py:46
  11.5 0.8 copy-start.2
  11.5 60.8 %reduce-scatter.3.cloned.1.call-start = ((), (), s32[]{:S(2)}) async-start(), calls=%async_computation.10 | async-start | bytes 2293760 | tf_op jit(solution)/shard_map/reduce_scatter | solution.py:46
  44.5 30.3 %all-to-all-start.2 = ((bf16[32,32,512]{2,1,0:T(8,128)(2,1)}), bf16[32,32,512]{2,1,0:T(8,128)(2,1)S(1)}, u32[]{:S(2)}, u32[]{:S(2)}) async-start(bf16[32,32,512]{2,1,0:T(8,128)(2,1)} %gather_fusion.2), calls=%async_computation.4 | async-start | bytes 2097152 | tf_op jit(solution)/shard_map/all_to_all | solution.py:48
  74.9 24.5 %all-to-all-start = ((bf16[32,32,512]{2,1,0:T(8,128)(2,1)}), bf16[32,32,512]{2,1,0:T(8,128)(2,1)}, u32[]{:S(2)}, u32[]{:S(2)}) async-start(bf16[32,32,512]{2,1,0:T(8,128)(2,1)} %gather_fusion), calls=%async_computation.1 | async-start | bytes 2097152 | tf_op jit(solution)/shard_map/all_to_all | solution.py:48
  99.4 16.3 %all-to-all-start.3 = ((bf16[4,3,2,32,512]{4,3,2,1,0:T(8,128)(2,1)}), bf16[4,3,2,32,512]{4,3,2,1,0:T(8,128)(2,1)S(1)}, u32[]{:S(2)}, u32[]{:S(2)}) async-start(bf16[4,3,2,32,512]{4,3,2,1,0:T(8,128)(2,1)} %bitcast.74), calls=%async_computation.5 | async-start | bytes 1572864 | tf_op jit(solution)/shard_map/all_to_all | solution.py:51
  115.7 15.5 %all-to-all-start.1 = ((bf16[4,3,2,32,512]{4,3,2,1,0:T(8,128)(2,1)}), bf16[4,3,2,32,512]{4,3,2,1,0:T(8,128)(2,1)S(1)}, u32[]{:S(2)}, u32[]{:S(2)}) async-start(bf16[4,3,2,32,512]{4,3,2,1,0:T(8,128)(2,1)} %bitcast.7), calls=%async_computation.2 | async-start | bytes 1572864 | tf_op jit(solution)/shard_map/all_to_all | solution.py:51
  139.6 15.4 %all-to-all-start.4 = ((bf16[4,3,2,32,512]{4,3,2,1,0:T(8,128)(2,1)}), bf16[4,3,2,32,512]{4,3,2,1,0:T(8,128)(2,1)}, u32[]{:S(2)}, u32[]{:S(2)}) async-start(bf16[4,3,2,32,512]{4,3,2,1,0:T(8,128)(2,1)} %bitcast.75), calls=%async_computation.6 | async-start | bytes 1572864 | tf_op jit(solution)/shard_map/all_to_all | solution.py:63
  157.7 22.8 %all-to-all-start.5 = ((bf16[32,32,512]{2,1,0:T(8,128)(2,1)}), bf16[32,32,512]{2,1,0:T(8,128)(2,1)}, u32[]{:S(2)}, u32[]{:S(2)}) async-start(bf16[32,32,512]{2,1,0:T(8,128)(2,1)} %bitcast.71), calls=%async_computation.7 | async-start | bytes 2097152 | tf_op jit(solution)/shard_map/all_to_all | solution.py:66
  163.2 83.8 %all-gather.3.cloned.1.call-start = ((), (), s32[]{:S(2)}) async-start(), calls=%async_computation.12 | async-start | bytes 2293760 | tf_op jit(solution)/shard_map/all_gather | solution.py:68
  184.9 79.0 %all-gather.5.cloned.1.call-start = ((), (), s32[]{:S(2)}) async-start(), calls=%async_computation.13 | async-start | bytes 2293760 | tf_op jit(solution)/shard_map/all_gather | solution.py:68
  239.3 4.9 %copy-start.1 = (f32[3,512,512]{2,1,0:T(8,128)S(1)}, f32[3,512,512]{2,1,0:T(8,128)}, u32[]{:S(2)}) copy-start(f32[3,512,512]{2,1,0:T(8,128)} %param.8) | copy-start | bytes 9437188
Sparse Core Ops, SparseCore 0:
  11.6 30.2 reduce-scatter.4
  44.9 27.3 reduce-scatter.2
  185.0 31.8 all-gather.2
  239.5 24.4 all-gather.4

commit v2 on v1

--- a/solution.py
+++ b/solution.py
@@ -1,10 +1,125 @@
+import functools
+
 import jax
 import jax.numpy as jnp
 from jax import lax
+from jax.experimental import pallas as pl
+from jax.experimental.pallas import tpu as pltpu
 from jax.sharding import PartitionSpec as P
 
 DECAY_RATE = 0.999
 CHUNKS = 2
+
+
+def ring_shift(count, step):
+    return [(i, (i + step) % count) for i in range(count)]
+
+
+def ahead(x):
+    return lax.ppermute(x, "dp", ring_shift(lax.axis_size("dp"), 1))
+
+
+def behind(x):
+    return lax.ppermute(x, "dp", ring_shift(lax.axis_size("dp"), -1))
+
+
+def add(dtype, *terms):
+    total = terms[0].astype(jnp.float32)
+    for term in terms[1:]:
+        total += term.astype(jnp.float32)
+    return total.astype(dtype)
+
+
+def sum_over_replicas(chunks):
+    count = lax.axis_size("dp")
+    me = lax.axis_index("dp")
+    results = []
+    after = None
+    for rows in chunks:
+        quarter = rows.shape[0] // count
+        half = quarter // 2
+
+        def part(offset, second):
+            start = (me + offset) % count * quarter + second * half
+            return lax.dynamic_slice_in_dim(rows, start, half, axis=0)
+
+        outgoing = part(2, 0), part(2, 1), part(1, 0), part(3, 1)
+        if after is not None:
+            outgoing, after = lax.optimization_barrier((outgoing, after))
+        relay_first = behind(outgoing[0])
+        relay_second = ahead(outgoing[1])
+        near_first = ahead(outgoing[2])
+        near_second = behind(outgoing[3])
+        after = add(rows.dtype, relay_first, part(3, 0)), add(rows.dtype, relay_second, part(1, 1))
+        far_first = behind(after[0])
+        far_second = ahead(after[1])
+        first = add(rows.dtype, part(0, 0), near_first, far_first)
+        second = add(rows.dtype, part(0, 1), near_second, far_second)
+        results.append(jnp.concatenate([first, second], axis=0))
+    return results
+
+
+PLACES = ((0, 0), (0, 1), (1, 0), (1, 1), (2, 0), (2, 1), (3, 0), (3, 1))
+
+
+def place_rows(base, me_ref, *refs):
+    parts = refs[:7]
+    out_ref, stage, in_sems, out_sems = refs[-4:]
+    half = parts[-1].shape[0]
+    me = me_ref[0]
+    loads = []
+    for i in range(7):
+        first = 0 if i == 0 else i + 1
+        width = 2 if i == 0 else 1
+        loads.append(pltpu.make_async_copy(parts[i], stage.at[pl.ds(first * half, width * half)], in_sems.at[i]))
+    for load in loads:
+        load.start()
+    stores = []
+    for i, load in enumerate(loads):
+        load.wait()
+        first = 0 if i == 0 else i + 1
+        width = 2 if i == 0 else 1
+        offset, second = PLACES[first]
+        start = pl.multiple_of(base + (me + offset) % 4 * 2 * half + second * half, half)
+        store = pltpu.make_async_copy(
+            stage.at[pl.ds(first * half, width * half)], out_ref.at[pl.ds(start, width * half)], out_sems.at[i]
+        )
+        store.start()
+        stores.append(store)
+    for store in stores:
+        store.wait()
+
+
+def gather_over_replicas(own, updates, base, total_rows):
+    quarter, width = own.shape
+    half = quarter // 2
+    prev_first = ahead(own[:half])
+    next_second = behind(own[half:])
+    prev_second = ahead(own[half:])
+    next_first = behind(own[:half])
+    far_first = ahead(prev_first)
+    far_second = behind(next_second)
+    me = lax.axis_index("dp").astype(jnp.int32).reshape(1)
+    any_spec = pl.BlockSpec(memory_space=pl.ANY)
+    operands = [me, own, next_first, next_second, far_first, far_second, prev_first, prev_second]
+    aliases = {}
+    if updates is not None:
+        aliases = {len(operands): 0}
+        operands.append(updates)
+    return pl.pallas_call(
+        functools.partial(place_rows, base),
+        out_shape=jax.ShapeDtypeStruct((total_rows, width), own.dtype),
+        in_specs=[pl.BlockSpec(memory_space=pltpu.SMEM)] + [any_spec] * (len(operands) - 1),
+        out_specs=any_spec,
+        scratch_shapes=[
+            pltpu.VMEM((8 * half, width), own.dtype),
+            pltpu.SemaphoreType.DMA((7,)),
+            pltpu.SemaphoreType.DMA((7,)),
+        ],
+        input_output_aliases=aliases,
+        cost_estimate=pl.CostEstimate(flops=0, bytes_accessed=32 * half * width, transcendentals=0),
+        name="place_rows",
+    )(*operands)
 
 
 def shards(grad_parts, owner_slot, stat_left, stat_right, root_left, root_right):
@@ -40,10 +155,9 @@
     back_held = jnp.sum(jnp.where(from_held, held[None, :], 0), axis=1)
     my_used = lax.dynamic_slice(held_used, (lax.axis_index("dp") * slot_count,), (slot_count,))
 
+    chunks = [grad_parts[0, i * chunk_rows : (i + 1) * chunk_rows] for i in range(CHUNKS)]
     gathered = []
-    for chunk in range(CHUNKS):
-        rows = grad_parts[0, chunk * chunk_rows : (chunk + 1) * chunk_rows]
-        part = lax.psum_scatter(rows, "dp", scatter_dimension=0, tiled=True)
+    for part in sum_over_replicas(chunks):
         layout = part.reshape(part_rows, wide_count, block_cols).transpose(1, 0, 2)
         incoming = lax.all_to_all(layout[send_piece], "expert", split_axis=0, concat_axis=0, tiled=True)
         by_row = incoming.reshape(row_blocks, halves, part_rows, block_cols)
@@ -57,16 +171,15 @@
     update = jnp.einsum("sij,sjk->sik", left_part, root_right, preferred_element_type=jnp.float32).astype(jnp.bfloat16)
     update = update.reshape(slot_count, halves, CHUNKS, dp_count, part_rows, block_cols)
 
-    out = []
+    updates = None
     for chunk in range(CHUNKS):
         to_replica = update[:, :, chunk].transpose(2, 0, 1, 3, 4)
         column_part = lax.all_to_all(to_replica, "dp", split_axis=0, concat_axis=0, tiled=True)
         column_part = column_part.reshape(held_count, halves, part_rows, block_cols)
         to_rows = column_part[back_held].reshape(expert_count, part_rows, block_cols)
         returned = lax.all_to_all(to_rows, "expert", split_axis=0, concat_axis=0, tiled=True)
-        part = returned[my_column].transpose(1, 0, 2).reshape(part_rows, row_width)
-        out.append(lax.all_gather(part, "dp", axis=0, tiled=True))
-    updates = jnp.concatenate(out, axis=0)
+        own = returned[my_column].transpose(1, 0, 2).reshape(part_rows, row_width)
+        updates = gather_over_replicas(own, updates, chunk * chunk_rows, shard_rows)
 
     left_gram = jnp.einsum("sij,skj->sik", grad, grad, preferred_element_type=jnp.float32)
     right_gram = jnp.einsum("sji,sjk->sik", grad, grad, preferred_element_type=jnp.float32)

time: 277 us -> 252 us (0.910)
  starting transfers between devices: 31.2 us -> 79.1 us
  blocking collectives: 46 us -> 0 us
  waiting for transfers between devices: 133 us -> 107 us
  between operations: 14 us -> 1.22 us
  local copies, waits for them, and re-layouts: 32.7 us -> 38.3 us
  Pallas kernels: 0 us -> 4.71 us
  other arithmetic: 5.23 us -> 8.63 us
    reduce_scatter x2 -> x0, waiting for transfers between devices: 50 us -> none  [shards(): part = lax.psum_scatter(rows, 'dp', scatter_dimension=0, tiled=True)]
    all_to_all x2 -> x0, blocking collectives: 46 us -> none  [the longest x1 24 us: shards(): lax.all_to_all(to_replica, 'dp', split_axis=0, concat_axis=0, tiled=True)]
    ppermute x0 -> x24, starting transfers between devices: none -> 39.1 us  [the longest x12 33.9 us: behind(): return lax.ppermute(x, 'dp', ring_shift(lax.axis_size('dp'), -1))]
    ppermute x0 -> x24, waiting for transfers between devices: none -> 20.6 us  [the longest x12 16 us: behind(): return lax.ppermute(x, 'dp', ring_shift(lax.axis_size('dp'), -1))]
    all_gather x2 -> x0, waiting for transfers between devices: 17 us -> none  [shards(): out.append(lax.all_gather(part, 'dp', axis=0, tiled=True))]
    all_to_all x2, waiting for transfers between devices: 15.6 us -> 27.9 us  [shards(): lax.all_to_all(layout[send_piece], 'expert', split_axis=0, concat_axis=0,...]
    all_to_all x1 -> x2, starting transfers between devices: 5.5 us -> 12.2 us  [shards(): lax.all_to_all(to_rows, 'expert', split_axis=0, concat_axis=0, tiled=True)]
    convert_element_type x0 -> x6, other arithmetic: none -> 6.54 us  [add(): return total.astype(dtype)]
  transfers between devices with their start and end apart: 10 -> 32, of which waited for: 8 -> 15; matrix products, arithmetic and copies ran while one was open for 10% -> 18% of each run, Pallas kernels for 0% -> 1%
where the time goes in v2:
time: 252 us; the launch traced here: 251 us
  waiting for transfers between devices  107 us (42%)
  starting transfers between devices  79.1 us (31%)
  local copies, waits for them, and re-layouts  38.3 us (15%)
  matrix products  12.2 us (5%)
  other arithmetic  8.63 us (3%)
  Pallas kernels  4.71 us (2%)
    ppermute x12, starting transfers between devices, behind(): return lax.ppermute(x, 'dp', ring_shift(lax.axis_size('dp'), -1))  33.9 us
    all_to_all x2, waiting for transfers between devices, shards(): lax.all_to_all(layout[send_piece], 'expert', split_axis=0, concat_axis=0,...  27.9 us
    all_to_all x2, waiting for transfers between devices, shards(): lax.all_to_all(to_owner, 'dp', split_axis=0, concat_axis=0, tiled=True)  22.5 us
    all_to_all x2, waiting for transfers between devices, shards(): lax.all_to_all(to_rows, 'expert', split_axis=0, concat_axis=0, tiled=True)  20.3 us
    ppermute x12, waiting for transfers between devices, behind(): return lax.ppermute(x, 'dp', ring_shift(lax.axis_size('dp'), -1))  16 us
    all_to_all x2, waiting for transfers between devices, shards(): lax.all_to_all(to_replica, 'dp', split_axis=0, concat_axis=0, tiled=True)  15.5 us
    all_to_all x2, starting transfers between devices, shards(): lax.all_to_all(to_rows, 'expert', split_axis=0, concat_axis=0, tiled=True)  12.2 us
    all_to_all x2, starting transfers between devices, shards(): lax.all_to_all(layout[send_piece], 'expert', split_axis=0, concat_axis=0,...  11.4 us
  transfers between devices with their start and end apart: 32, of which 15 were waited for; matrix products, arithmetic and copies ran while one was open for 18% of the time, Pallas kernels for 1%

profile of v2, /device:TPU:0, one launch (start us, length us, event | category | flops | bytes accessed | tf_op | source)
XLA Modules:
  0.0 251.0 jit_solution(17188329444799783664)
XLA Ops:
  0.7 3.6 %fusion.22 = (bf16[1,128,7168]{2,1,0:T(8,128)(2,1)}, bf16[1,128,7168]{2,1,0:T(8,128)(2,1)S(1)}) fusion(bf16[1,256,7168]{2,1,0:T(8,128)(2,1)} %param.6), kind=kLoop, calls=%fused_computation.89 | loop fusion | bytes 7340032 | tf_op jit(solution)/shard_map/slice | solution.py:158
  13.7 8.8 %collective-permute-done.1 = bf16[16,7168]{1,0:T(8,128)(2,1)} collective-permute-done((bf16[16,7168]{1,0:T(8,128)(2,1)}, bf16[16,7168]{1,0:T(8,128)(2,1)}, u32[]{:S(2)}, u32[]{:S(2)}) %collective-permute-start.1) | collective-permute-done | bytes 229408 | tf_op jit(solution)/shard_map/ppermute | solution.py:23
  27.1 3.6 %collective-permute-done.2 = bf16[16,7168]{1,0:T(8,128)(2,1)} collective-permute-done((bf16[16,7168]{1,0:T(8,128)(2,1)}, bf16[16,7168]{1,0:T(8,128)(2,1)}, u32[]{:S(2)}, u32[]{:S(2)}) %collective-permute-start.2) | collective-permute-done | bytes 229408 | tf_op jit(solution)/shard_map/ppermute | solution.py:23
  32.2 3.8 %collective-permute-start.7 = (bf16[16,7168]{1,0:T(8,128)(2,1)S(1)}, bf16[16,7168]{1,0:T(8,128)(2,1)S(1)}, u32[]{:S(2)}, u32[]{:S(2)}) collective-permute-start(bf16[16,7168]{1,0:T(8,128)(2,1)S(1)} %copy-done.6), channel_id=1, source_target_pairs={{0,96},{32,0},{64,32},{96,64},{1,97},{33,1},{65,33},{97,65},{2,98}... | collective-permute-start | bytes 688136 | tf_op jit(solution)/shard_map/ppermute | solution.py:23
  36.1 3.2 %collective-permute-start.9 = (bf16[16,7168]{1,0:T(8,128)(2,1)}, bf16[16,7168]{1,0:T(8,128)(2,1)}, u32[]{:S(2)}, u32[]{:S(2)}) collective-permute-start(bf16[16,7168]{1,0:T(8,128)(2,1)} %get-tuple-element.9), channel_id=1, source_target_pairs={{0,96},{32,0},{64,32},{96,64},{1,97},{33,1},{65,33},{97,65},{2,98}... | collective-permute-start | bytes 688136 | tf_op jit(solution)/shard_map/ppermute | solution.py:23
  42.0 3.8 %collective-permute-start.8 = (bf16[16,7168]{1,0:T(8,128)(2,1)S(1)}, bf16[16,7168]{1,0:T(8,128)(2,1)S(1)}, u32[]{:S(2)}, u32[]{:S(2)}) collective-permute-start(bf16[16,7168]{1,0:T(8,128)(2,1)S(1)} %fusion.3), channel_id=1, source_target_pairs={{0,96},{32,0},{64,32},{96,64},{1,97},{33,1},{65,33},{97,65},{2,98}... | collective-permute-start | bytes 688136 | tf_op jit(solution)/shard_map/ppermute | solution.py:23
  55.9 7.4 %all-to-all-start = ((bf16[32,32,512]{2,1,0:T(8,128)(2,1)}), bf16[32,32,512]{2,1,0:T(8,128)(2,1)}, u32[]{:S(2)}, u32[]{:S(2)}) async-start(bf16[32,32,512]{2,1,0:T(8,128)(2,1)} %gather_fusion), calls=%async_computation | async-start | bytes 2097152 | tf_op jit(solution)/shard_map/all_to_all | solution.py:162
  67.1 13.5 %all-to-all-done = bf16[32,32,512]{2,1,0:T(8,128)(2,1)} async-done(((bf16[32,32,512]{2,1,0:T(8,128)(2,1)}), bf16[32,32,512]{2,1,0:T(8,128)(2,1)}, u32[]{:S(2)}, u32[]{:S(2)}) %all-to-all-start) | async-done | bytes 1048608 | tf_op jit(solution)/shard_map/all_to_all | solution.py:162
  80.6 3.9 %all-to-all-start.2 = ((bf16[32,32,512]{2,1,0:T(8,128)(2,1)}), bf16[32,32,512]{2,1,0:T(8,128)(2,1)S(1)}, u32[]{:S(2)}, u32[]{:S(2)}) async-start(bf16[32,32,512]{2,1,0:T(8,128)(2,1)} %gather_fusion.2), calls=%async_computation.2 | async-start | bytes 2097152 | tf_op jit(solution)/shard_map/all_to_all | solution.py:162
  84.8 2.7 %gather_fusion.1 = bf16[12,2,32,512]{3,2,1,0:T(8,128)(2,1)} fusion(bf16[16,2,32,512]{3,2,1,0:T(8,128)(2,1)} %bitcast.11, s32[1024]{0:T(1024)S(1)} %pad_clamp_fusion.2), kind=kCustom, calls=%fused_computation.1 | custom fusion | bytes 1572912 | tf_op jit(solution)/shard_map/gather | solution.py:164
  87.5 14.4 %all-to-all-done.2 = bf16[32,32,512]{2,1,0:T(8,128)(2,1)S(1)} async-done(((bf16[32,32,512]{2,1,0:T(8,128)(2,1)}), bf16[32,32,512]{2,1,0:T(8,128)(2,1)S(1)}, u32[]{:S(2)}, u32[]{:S(2)}) %all-to-all-start.2) | async-done | bytes 1048608 | tf_op jit(solution)/shard_map/all_to_all | solution.py:162
  101.9 4.5 %all-to-all-start.1 = ((bf16[4,3,2,32,512]{4,3,2,1,0:T(8,128)(2,1)}), bf16[4,3,2,32,512]{4,3,2,1,0:T(8,128)(2,1)S(1)}, u32[]{:S(2)}, u32[]{:S(2)}) async-start(bf16[4,3,2,32,512]{4,3,2,1,0:T(8,128)(2,1)} %bitcast.14), calls=%async_computation.1 | async-start | bytes 1572864 | tf_op jit(solution)/shard_map/all_to_all | solution.py:165
  107.9 11.1 %all-to-all-done.1 = bf16[4,3,2,32,512]{4,3,2,1,0:T(8,128)(2,1)S(1)} async-done(((bf16[4,3,2,32,512]{4,3,2,1,0:T(8,128)(2,1)}), bf16[4,3,2,32,512]{4,3,2,1,0:T(8,128)(2,1)S(1)}, u32[]{:S(2)}, u32[]{:S(2)}) %all-to-all-start.1) | async-done | bytes 786464 | tf_op jit(solution)/shard_map/all_to_all | solution.py:165
  119.0 3.5 %all-to-all-start.3 = ((bf16[4,3,2,32,512]{4,3,2,1,0:T(8,128)(2,1)}), bf16[4,3,2,32,512]{4,3,2,1,0:T(8,128)(2,1)S(1)}, u32[]{:S(2)}, u32[]{:S(2)}) async-start(bf16[4,3,2,32,512]{4,3,2,1,0:T(8,128)(2,1)} %bitcast.26), calls=%async_computation.3 | async-start | bytes 1572864 | tf_op jit(solution)/shard_map/all_to_all | solution.py:165
  122.8 11.4 %all-to-all-done.3 = bf16[4,3,2,32,512]{4,3,2,1,0:T(8,128)(2,1)S(1)} async-done(((bf16[4,3,2,32,512]{4,3,2,1,0:T(8,128)(2,1)}), bf16[4,3,2,32,512]{4,3,2,1,0:T(8,128)(2,1)S(1)}, u32[]{:S(2)}, u32[]{:S(2)}) %all-to-all-start.3) | async-done | bytes 786464 | tf_op jit(solution)/shard_map/all_to_all | solution.py:165
  134.7 4.5 %convolution_convert_fusion = bf16[3,512,512]{2,1,0:T(8,128)(2,1)} fusion(bf16[3,512,512]{2,1,0:T(8,128)(2,1)S(1)} %copy-done, bf16[3,512,512]{2,1,0:T(8,128)(2,1)S(1)} %bitcast_select_fusion, bf16[3,512,512]{2,1,0:T(8,128)(2,1)} %param.10), kind=kOutput, calls=%fused_computation.10 | convolution fusion | flops 1612185600 | bytes 6291456 | tf_op jit(solution)/shard_map/sij,sjk->sik/dot_general | solution.py:171
  142.5 4.2 %all-to-all-start.6 = ((bf16[4,3,2,32,512]{4,3,2,1,0:T(8,128)(2,1)}), bf16[4,3,2,32,512]{4,3,2,1,0:T(8,128)(2,1)}, u32[]{:S(2)}, u32[]{:S(2)}) async-start(bf16[4,3,2,32,512]{4,3,2,1,0:T(8,128)(2,1)} %bitcast.127), calls=%async_computation.6 | async-start | bytes 1572864 | tf_op jit(solution)/shard_map/all_to_all | solution.py:177
  148.8 8.7 %all-to-all-done.6 = bf16[4,3,2,32,512]{4,3,2,1,0:T(8,128)(2,1)} async-done(((bf16[4,3,2,32,512]{4,3,2,1,0:T(8,128)(2,1)}), bf16[4,3,2,32,512]{4,3,2,1,0:T(8,128)(2,1)}, u32[]{:S(2)}, u32[]{:S(2)}) %all-to-all-start.6) | async-done | bytes 786464 | tf_op jit(solution)/shard_map/all_to_all | solution.py:177
  157.6 4.2 %all-to-all-start.4 = ((bf16[4,3,2,32,512]{4,3,2,1,0:T(8,128)(2,1)}), bf16[4,3,2,32,512]{4,3,2,1,0:T(8,128)(2,1)}, u32[]{:S(2)}, u32[]{:S(2)}) async-start(bf16[4,3,2,32,512]{4,3,2,1,0:T(8,128)(2,1)} %bitcast.126), calls=%async_computation.4 | async-start | bytes 1572864 | tf_op jit(solution)/shard_map/all_to_all | solution.py:177
  161.9 2.7 %gather_fusion.6 = bf16[16,2,32,512]{3,2,1,0:T(8,128)(2,1)} fusion(bf16[12,2,32,512]{3,2,1,0:T(8,128)(2,1)} %bitcast.41, s32[1024]{0:T(1024)S(1)} %pad_clamp_fusion.1), kind=kCustom, calls=%fused_computation.6 | custom fusion | bytes 2097216 | tf_op jit(solution)/shard_map/gather | solution.py:179
  164.6 6.8 %all-to-all-done.4 = bf16[4,3,2,32,512]{4,3,2,1,0:T(8,128)(2,1)} async-done(((bf16[4,3,2,32,512]{4,3,2,1,0:T(8,128)(2,1)}), bf16[4,3,2,32,512]{4,3,2,1,0:T(8,128)(2,1)}, u32[]{:S(2)}, u32[]{:S(2)}) %all-to-all-start.4) | async-done | bytes 786464 | tf_op jit(solution)/shard_map/all_to_all | solution.py:177
  171.4 7.3 %all-to-all-start.7 = ((bf16[32,32,512]{2,1,0:T(8,128)(2,1)}), bf16[32,32,512]{2,1,0:T(8,128)(2,1)}, u32[]{:S(2)}, u32[]{:S(2)}) async-start(bf16[32,32,512]{2,1,0:T(8,128)(2,1)} %bitcast.120), calls=%async_computation.7 | async-start | bytes 2097152 | tf_op jit(solution)/shard_map/all_to_all | solution.py:180
  178.7 2.7 %gather_fusion.4 = bf16[16,2,32,512]{3,2,1,0:T(8,128)(2,1)} fusion(bf16[12,2,32,512]{3,2,1,0:T(8,128)(2,1)} %bitcast.34, s32[1024]{0:T(1024)S(1)} %pad_clamp_fusion.1), kind=kCustom, calls=%fused_computation.4 | custom fusion | bytes 2097216 | tf_op jit(solution)/shard_map/gather | solution.py:179
  181.4 14.6 %all-to-all-done.7 = bf16[32,32,512]{2,1,0:T(8,128)(2,1)} async-done(((bf16[32,32,512]{2,1,0:T(8,128)(2,1)}), bf16[32,32,512]{2,1,0:T(8,128)(2,1)}, u32[]{:S(2)}, u32[]{:S(2)}) %all-to-all-start.7) | async-done | bytes 1048608 | tf_op jit(solution)/shard_map/all_to_all | solution.py:180
  196.0 4.9 %all-to-all-start.5 = ((bf16[32,32,512]{2,1,0:T(8,128)(2,1)}), bf16[32,32,512]{2,1,0:T(8,128)(2,1)}, u32[]{:S(2)}, u32[]{:S(2)}) async-start(bf16[32,32,512]{2,1,0:T(8,128)(2,1)} %bitcast.119), calls=%async_computation.5 | async-start | bytes 2097152 | tf_op jit(solution)/shard_map/all_to_all | solution.py:180
  209.2 3.2 %collective-permute-start.19 = (bf16[16,7168]{1,0:T(8,128)(2,1)}, bf16[16,7168]{1,0:T(8,128)(2,1)}, u32[]{:S(2)}, u32[]{:S(2)}) collective-permute-start(bf16[16,7168]{1,0:T(8,128)(2,1)} %bitcast.69), channel_id=1, source_target_pairs={{0,96},{32,0},{64,32},{96,64},{1,97},{33,1},{65,33},{97,65},{2,98}... | collective-permute-start | bytes 688136 | tf_op jit(solution)/shard_map/ppermute | solution.py:23
  212.5 5.7 %all-to-all-done.5 = bf16[32,32,512]{2,1,0:T(8,128)(2,1)} async-done(((bf16[32,32,512]{2,1,0:T(8,128)(2,1)}), bf16[32,32,512]{2,1,0:T(8,128)(2,1)}, u32[]{:S(2)}, u32[]{:S(2)}) %all-to-all-start.5) | async-done | bytes 1048608 | tf_op jit(solution)/shard_map/all_to_all | solution.py:180
  225.8 4.9 %multiply_add_fusion = f32[3,512,512]{2,1,0:T(8,128)} fusion(f32[3,512,512]{2,1,0:T(8,128)} %param.9, bf16[3,512,512]{2,1,0:T(8,128)(2,1)S(1)} %bitcast_select_fusion), kind=kOutput, calls=%fused_computation.8 | convolution fusion | flops 807665664 | bytes 7864320 | tf_op jit(solution)/shard_map/sji,sjk->sik/dot_general | solution.py:185
  230.7 3.3 %collective-permute-start.12 = (bf16[16,7168]{1,0:T(8,128)(2,1)}, bf16[16,7168]{1,0:T(8,128)(2,1)}, u32[]{:S(2)}, u32[]{:S(2)}) collective-permute-start(bf16[16,7168]{1,0:T(8,128)(2,1)} %bitcast.61), channel_id=1, source_target_pairs={{0,96},{32,0},{64,32},{96,64},{1,97},{33,1},{65,33},{97,65},{2,98}... | collective-permute-start | bytes 688136 | tf_op jit(solution)/shard_map/ppermute | solution.py:23
  234.0 3.2 %collective-permute-start.22 = (bf16[16,7168]{1,0:T(8,128)(2,1)}, bf16[16,7168]{1,0:T(8,128)(2,1)}, u32[]{:S(2)}, u32[]{:S(2)}) collective-permute-start(bf16[16,7168]{1,0:T(8,128)(2,1)} %collective-permute-done.19.refs_2_), channel_id=1, source_target_pairs={{0,96},{32,0},{64,32},{96,64},{1,97},{33,1},{65,33},{97,65},{2,98}... | collective-permute-start | bytes 688136 | tf_op jit(solution)/shard_map/ppermute | solution.py:23
  237.3 3.2 %collective-permute-start.16 = (bf16[16,7168]{1,0:T(8,128)(2,1)}, bf16[16,7168]{1,0:T(8,128)(2,1)}, u32[]{:S(2)}, u32[]{:S(2)}) collective-permute-start(bf16[16,7168]{1,0:T(8,128)(2,1)} %collective-permute-done.13.refs_2_), channel_id=1, source_target_pairs={{0,96},{32,0},{64,32},{96,64},{1,97},{33,1},{65,33},{97,65},{2,98}... | collective-permute-start | bytes 688136 | tf_op jit(solution)/shard_map/ppermute | solution.py:23
  240.5 2.8 %multiply_add_fusion.1 = f32[3,512,512]{2,1,0:T(8,128)} fusion(f32[3,512,512]{2,1,0:T(8,128)S(1)} %copy-done.3, bf16[3,512,512]{2,1,0:T(8,128)(2,1)S(1)} %bitcast_select_fusion), kind=kOutput, calls=%fused_computation.9 | convolution fusion | flops 807665664 | bytes 7864320 | tf_op jit(solution)/shard_map/sij,skj->sik/dot_general | solution.py:184
  (105 shorter events, 63.6 us)
Async XLA Ops:
  6.6 20.5 %collective-permute-start = (bf16[16,7168]{1,0:T(8,128)(2,1)}, bf16[16,7168]{1,0:T(8,128)(2,1)}, u32[]{:S(2)}, u32[]{:S(2)}) collective-permute-start(bf16[16,7168]{1,0:T(8,128)(2,1)} %get-tuple-element.17), channel_id=1, source_target_pairs={{0,32},{32,64},{64,96},{96,0},{1,33},{33,65},{65,97},{97,1},{2,34}... | collective-permute-start | bytes 688136 | tf_op jit(solution)/shard_map/ppermute | solution.py:19
  8.6 18.5 %collective-permute-start.4 = (bf16[16,7168]{1,0:T(8,128)(2,1)}, bf16[16,7168]{1,0:T(8,128)(2,1)}, u32[]{:S(2)}, u32[]{:S(2)}) collective-permute-start(bf16[16,7168]{1,0:T(8,128)(2,1)} %get-tuple-element.18), channel_id=1, source_target_pairs={{0,32},{32,64},{64,96},{96,0},{1,33},{33,65},{65,97},{97,1},{2,34}... | collective-permute-start | bytes 688136 | tf_op jit(solution)/shard_map/ppermute | solution.py:19
  10.5 31.5 %collective-permute-start.3 = (bf16[16,7168]{1,0:T(8,128)(2,1)}, bf16[16,7168]{1,0:T(8,128)(2,1)}, u32[]{:S(2)}, u32[]{:S(2)}) collective-permute-start(bf16[16,7168]{1,0:T(8,128)(2,1)} %get-tuple-element.19), channel_id=1, source_target_pairs={{0,96},{32,0},{64,32},{96,64},{1,97},{33,1},{65,33},{97,65},{2,98}... | collective-permute-start | bytes 688136 | tf_op jit(solution)/shard_map/ppermute | solution.py:23
  11.8 10.7 %collective-permute-start.1 = (bf16[16,7168]{1,0:T(8,128)(2,1)}, bf16[16,7168]{1,0:T(8,128)(2,1)}, u32[]{:S(2)}, u32[]{:S(2)}) collective-permute-start(bf16[16,7168]{1,0:T(8,128)(2,1)} %get-tuple-element.20), channel_id=1, source_target_pairs={{0,96},{32,0},{64,32},{96,64},{1,97},{33,1},{65,33},{97,65},{2,98}... | collective-permute-start | bytes 688136 | tf_op jit(solution)/shard_map/ppermute | solution.py:23
  24.3 6.4 %collective-permute-start.2 = (bf16[16,7168]{1,0:T(8,128)(2,1)}, bf16[16,7168]{1,0:T(8,128)(2,1)}, u32[]{:S(2)}, u32[]{:S(2)}) collective-permute-start(bf16[16,7168]{1,0:T(8,128)(2,1)} %fusion.9), channel_id=1, source_target_pairs={{0,96},{32,0},{64,32},{96,64},{1,97},{33,1},{65,33},{97,65},{2,98}... | collective-permute-start | bytes 688136 | tf_op jit(solution)/shard_map/ppermute | solution.py:23
  32.2 9.7 %collective-permute-start.7 = (bf16[16,7168]{1,0:T(8,128)(2,1)S(1)}, bf16[16,7168]{1,0:T(8,128)(2,1)S(1)}, u32[]{:S(2)}, u32[]{:S(2)}) collective-permute-start(bf16[16,7168]{1,0:T(8,128)(2,1)S(1)} %copy-done.6), channel_id=1, source_target_pairs={{0,96},{32,0},{64,32},{96,64},{1,97},{33,1},{65,33},{97,65},{2,98}... | collective-permute-start | bytes 688136 | tf_op jit(solution)/shard_map/ppermute | solution.py:23
  36.0 9.8 %collective-permute-start.5 = (bf16[16,7168]{1,0:T(8,128)(2,1)S(1)}, bf16[16,7168]{1,0:T(8,128)(2,1)S(1)}, u32[]{:S(2)}, u32[]{:S(2)}) collective-permute-start(bf16[16,7168]{1,0:T(8,128)(2,1)S(1)} %get-tuple-element.16), channel_id=1, source_target_pairs={{0,32},{32,64},{64,96},{96,0},{1,33},{33,65},{65,97},{97,1},{2,34}... | collective-permute-start | bytes 688136 | tf_op jit(solution)/shard_map/ppermute | solution.py:19
  36.1 13.0 %collective-permute-start.6 = (bf16[16,7168]{1,0:T(8,128)(2,1)S(1)}, bf16[16,7168]{1,0:T(8,128)(2,1)S(1)}, u32[]{:S(2)}, u32[]{:S(2)}) collective-permute-start(bf16[16,7168]{1,0:T(8,128)(2,1)S(1)} %copy-done.5), channel_id=1, source_target_pairs={{0,32},{32,64},{64,96},{96,0},{1,33},{33,65},{65,97},{97,1},{2,34}... | collective-permute-start | bytes 688136 | tf_op jit(solution)/shard_map/ppermute | solution.py:19
  36.1 27.2 %collective-permute-start.9 = (bf16[16,7168]{1,0:T(8,128)(2,1)}, bf16[16,7168]{1,0:T(8,128)(2,1)}, u32[]{:S(2)}, u32[]{:S(2)}) collective-permute-start(bf16[16,7168]{1,0:T(8,128)(2,1)} %get-tuple-element.9), channel_id=1, source_target_pairs={{0,96},{32,0},{64,32},{96,64},{1,97},{33,1},{65,33},{97,65},{2,98}... | collective-permute-start | bytes 688136 | tf_op jit(solution)/shard_map/ppermute | solution.py:23
  41.9 9.6 %collective-permute-start.10 = (bf16[16,7168]{1,0:T(8,128)(2,1)S(1)}, bf16[16,7168]{1,0:T(8,128)(2,1)S(1)}, u32[]{:S(2)}, u32[]{:S(2)}) collective-permute-start(bf16[16,7168]{1,0:T(8,128)(2,1)S(1)} %copy-done.4), channel_id=1, source_target_pairs={{0,32},{32,64},{64,96},{96,0},{1,33},{33,65},{65,97},{97,1},{2,34}... | collective-permute-start | bytes 688136 | tf_op jit(solution)/shard_map/ppermute | solution.py:19
  42.0 9.5 %collective-permute-start.8 = (bf16[16,7168]{1,0:T(8,128)(2,1)S(1)}, bf16[16,7168]{1,0:T(8,128)(2,1)S(1)}, u32[]{:S(2)}, u32[]{:S(2)}) collective-permute-start(bf16[16,7168]{1,0:T(8,128)(2,1)S(1)} %fusion.3), channel_id=1, source_target_pairs={{0,96},{32,0},{64,32},{96,64},{1,97},{33,1},{65,33},{97,65},{2,98}... | collective-permute-start | bytes 688136 | tf_op jit(solution)/shard_map/ppermute | solution.py:23
  52.4 10.9 %collective-permute-start.11 = (bf16[16,7168]{1,0:T(8,128)(2,1)}, bf16[16,7168]{1,0:T(8,128)(2,1)}, u32[]{:S(2)}, u32[]{:S(2)}) collective-permute-start(bf16[16,7168]{1,0:T(8,128)(2,1)} %get-tuple-element.22), channel_id=1, source_target_pairs={{0,32},{32,64},{64,96},{96,0},{1,33},{33,65},{65,97},{97,1},{2,34}... | collective-permute-start | bytes 688136 | tf_op jit(solution)/shard_map/ppermute | solution.py:19
  55.9 24.8 %all-to-all-start = ((bf16[32,32,512]{2,1,0:T(8,128)(2,1)}), bf16[32,32,512]{2,1,0:T(8,128)(2,1)}, u32[]{:S(2)}, u32[]{:S(2)}) async-start(bf16[32,32,512]{2,1,0:T(8,128)(2,1)} %gather_fusion), calls=%async_computation | async-start | bytes 2097152 | tf_op jit(solution)/shard_map/all_to_all | solution.py:162
  80.6 21.3 %all-to-all-start.2 = ((bf16[32,32,512]{2,1,0:T(8,128)(2,1)}), bf16[32,32,512]{2,1,0:T(8,128)(2,1)S(1)}, u32[]{:S(2)}, u32[]{:S(2)}) async-start(bf16[32,32,512]{2,1,0:T(8,128)(2,1)} %gather_fusion.2), calls=%async_computation.2 | async-start | bytes 2097152 | tf_op jit(solution)/shard_map/all_to_all | solution.py:162
  101.9 17.1 %all-to-all-start.1 = ((bf16[4,3,2,32,512]{4,3,2,1,0:T(8,128)(2,1)}), bf16[4,3,2,32,512]{4,3,2,1,0:T(8,128)(2,1)S(1)}, u32[]{:S(2)}, u32[]{:S(2)}) async-start(bf16[4,3,2,32,512]{4,3,2,1,0:T(8,128)(2,1)} %bitcast.14), calls=%async_computation.1 | async-start | bytes 1572864 | tf_op jit(solution)/shard_map/all_to_all | solution.py:165
  119.0 15.2 %all-to-all-start.3 = ((bf16[4,3,2,32,512]{4,3,2,1,0:T(8,128)(2,1)}), bf16[4,3,2,32,512]{4,3,2,1,0:T(8,128)(2,1)S(1)}, u32[]{:S(2)}, u32[]{:S(2)}) async-start(bf16[4,3,2,32,512]{4,3,2,1,0:T(8,128)(2,1)} %bitcast.26), calls=%async_computation.3 | async-start | bytes 1572864 | tf_op jit(solution)/shard_map/all_to_all | solution.py:165
  142.5 15.0 %all-to-all-start.6 = ((bf16[4,3,2,32,512]{4,3,2,1,0:T(8,128)(2,1)}), bf16[4,3,2,32,512]{4,3,2,1,0:T(8,128)(2,1)}, u32[]{:S(2)}, u32[]{:S(2)}) async-start(bf16[4,3,2,32,512]{4,3,2,1,0:T(8,128)(2,1)} %bitcast.127), calls=%async_computation.6 | async-start | bytes 1572864 | tf_op jit(solution)/shard_map/all_to_all | solution.py:177
  157.6 13.8 %all-to-all-start.4 = ((bf16[4,3,2,32,512]{4,3,2,1,0:T(8,128)(2,1)}), bf16[4,3,2,32,512]{4,3,2,1,0:T(8,128)(2,1)}, u32[]{:S(2)}, u32[]{:S(2)}) async-start(bf16[4,3,2,32,512]{4,3,2,1,0:T(8,128)(2,1)} %bitcast.126), calls=%async_computation.4 | async-start | bytes 1572864 | tf_op jit(solution)/shard_map/all_to_all | solution.py:177
  171.4 24.6 %all-to-all-start.7 = ((bf16[32,32,512]{2,1,0:T(8,128)(2,1)}), bf16[32,32,512]{2,1,0:T(8,128)(2,1)}, u32[]{:S(2)}, u32[]{:S(2)}) async-start(bf16[32,32,512]{2,1,0:T(8,128)(2,1)} %bitcast.120), calls=%async_computation.7 | async-start | bytes 2097152 | tf_op jit(solution)/shard_map/all_to_all | solution.py:180
  196.0 22.2 %all-to-all-start.5 = ((bf16[32,32,512]{2,1,0:T(8,128)(2,1)}), bf16[32,32,512]{2,1,0:T(8,128)(2,1)}, u32[]{:S(2)}, u32[]{:S(2)}) async-start(bf16[32,32,512]{2,1,0:T(8,128)(2,1)} %bitcast.119), calls=%async_computation.5 | async-start | bytes 2097152 | tf_op jit(solution)/shard_map/all_to_all | solution.py:180
  205.3 17.9 %collective-permute-start.20 = (bf16[16,7168]{1,0:T(8,128)(2,1)}, bf16[16,7168]{1,0:T(8,128)(2,1)}, u32[]{:S(2)}, u32[]{:S(2)}) collective-permute-start(bf16[16,7168]{1,0:T(8,128)(2,1)} %bitcast.67), channel_id=1, source_target_pairs={{0,32},{32,64},{64,96},{96,0},{1,33},{33,65},{65,97},{97,1},{2,34}... | collective-permute-start | bytes 688136 | tf_op jit(solution)/shard_map/ppermute | solution.py:19
  205.9 20.0 %collective-permute-start.18 = (bf16[16,7168]{1,0:T(8,128)(2,1)}, bf16[16,7168]{1,0:T(8,128)(2,1)}, u32[]{:S(2)}, u32[]{:S(2)}) collective-permute-start(bf16[16,7168]{1,0:T(8,128)(2,1)} %bitcast.67), channel_id=1, source_target_pairs={{0,96},{32,0},{64,32},{96,64},{1,97},{33,1},{65,33},{97,65},{2,98}... | collective-permute-start | bytes 688136 | tf_op jit(solution)/shard_map/ppermute | solution.py:23
  209.2 21.5 %collective-permute-start.23 = (bf16[16,7168]{1,0:T(8,128)(2,1)}, bf16[16,7168]{1,0:T(8,128)(2,1)}, u32[]{:S(2)}, u32[]{:S(2)}) collective-permute-start(bf16[16,7168]{1,0:T(8,128)(2,1)} %bitcast.69), channel_id=1, source_target_pairs={{0,32},{32,64},{64,96},{96,0},{1,33},{33,65},{65,97},{97,1},{2,34}... | collective-permute-start | bytes 688136 | tf_op jit(solution)/shard_map/ppermute | solution.py:19
  209.2 24.8 %collective-permute-start.19 = (bf16[16,7168]{1,0:T(8,128)(2,1)}, bf16[16,7168]{1,0:T(8,128)(2,1)}, u32[]{:S(2)}, u32[]{:S(2)}) collective-permute-start(bf16[16,7168]{1,0:T(8,128)(2,1)} %bitcast.69), channel_id=1, source_target_pairs={{0,96},{32,0},{64,32},{96,64},{1,97},{33,1},{65,33},{97,65},{2,98}... | collective-permute-start | bytes 688136 | tf_op jit(solution)/shard_map/ppermute | solution.py:23
  222.6 11.4 %collective-permute-start.14 = (bf16[16,7168]{1,0:T(8,128)(2,1)}, bf16[16,7168]{1,0:T(8,128)(2,1)}, u32[]{:S(2)}, u32[]{:S(2)}) collective-permute-start(bf16[16,7168]{1,0:T(8,128)(2,1)} %bitcast.61), channel_id=1, source_target_pairs={{0,32},{32,64},{64,96},{96,0},{1,33},{33,65},{65,97},{97,1},{2,34}... | collective-permute-start | bytes 688136 | tf_op jit(solution)/shard_map/ppermute | solution.py:19
  223.2 14.1 %collective-permute-start.13 = (bf16[16,7168]{1,0:T(8,128)(2,1)S(1)}, bf16[16,7168]{1,0:T(8,128)(2,1)}, u32[]{:S(2)}, u32[]{:S(2)}) collective-permute-start(bf16[16,7168]{1,0:T(8,128)(2,1)S(1)} %bitcast.135), channel_id=1, source_target_pairs={{0,96},{32,0},{64,32},{96,64},{1,97},{33,1},{65,33},{97,65},{2,98}... | collective-permute-start | bytes 688136 | tf_op jit(solution)/shard_map/ppermute | solution.py:23
  225.8 11.4 %collective-permute-start.21 = (bf16[16,7168]{1,0:T(8,128)(2,1)}, bf16[16,7168]{1,0:T(8,128)(2,1)S(1)}, u32[]{:S(2)}, u32[]{:S(2)}) collective-permute-start(bf16[16,7168]{1,0:T(8,128)(2,1)} %collective-permute-done.20.refs_5_), channel_id=1, source_target_pairs={{0,32},{32,64},{64,96},{96,0},{1,33},{33,65},{65,97},{97,1},{2,34}... | collective-permute-start | bytes 688136 | tf_op jit(solution)/shard_map/ppermute | solution.py:19
  230.7 17.0 %collective-permute-start.12 = (bf16[16,7168]{1,0:T(8,128)(2,1)}, bf16[16,7168]{1,0:T(8,128)(2,1)}, u32[]{:S(2)}, u32[]{:S(2)}) collective-permute-start(bf16[16,7168]{1,0:T(8,128)(2,1)} %bitcast.61), channel_id=1, source_target_pairs={{0,96},{32,0},{64,32},{96,64},{1,97},{33,1},{65,33},{97,65},{2,98}... | collective-permute-start | bytes 688136 | tf_op jit(solution)/shard_map/ppermute | solution.py:23
  234.0 13.7 %collective-permute-start.17 = (bf16[16,7168]{1,0:T(8,128)(2,1)S(1)}, bf16[16,7168]{1,0:T(8,128)(2,1)}, u32[]{:S(2)}, u32[]{:S(2)}) collective-permute-start(bf16[16,7168]{1,0:T(8,128)(2,1)S(1)} %bitcast.136), channel_id=1, source_target_pairs={{0,32},{32,64},{64,96},{96,0},{1,33},{33,65},{65,97},{97,1},{2,34}... | collective-permute-start | bytes 688136 | tf_op jit(solution)/shard_map/ppermute | solution.py:19
  234.0 11.3 %collective-permute-start.22 = (bf16[16,7168]{1,0:T(8,128)(2,1)}, bf16[16,7168]{1,0:T(8,128)(2,1)}, u32[]{:S(2)}, u32[]{:S(2)}) collective-permute-start(bf16[16,7168]{1,0:T(8,128)(2,1)} %collective-permute-done.19.refs_2_), channel_id=1, source_target_pairs={{0,96},{32,0},{64,32},{96,64},{1,97},{33,1},{65,33},{97,65},{2,98}... | collective-permute-start | bytes 688136 | tf_op jit(solution)/shard_map/ppermute | solution.py:23
  237.3 10.4 %collective-permute-start.15 = (bf16[16,7168]{1,0:T(8,128)(2,1)}, bf16[16,7168]{1,0:T(8,128)(2,1)}, u32[]{:S(2)}, u32[]{:S(2)}) collective-permute-start(bf16[16,7168]{1,0:T(8,128)(2,1)} %collective-permute-done.14.refs_5_), channel_id=1, source_target_pairs={{0,32},{32,64},{64,96},{96,0},{1,33},{33,65},{65,97},{97,1},{2,34}... | collective-permute-start | bytes 688136 | tf_op jit(solution)/shard_map/ppermute | solution.py:19
  237.3 11.2 %collective-permute-start.16 = (bf16[16,7168]{1,0:T(8,128)(2,1)}, bf16[16,7168]{1,0:T(8,128)(2,1)}, u32[]{:S(2)}, u32[]{:S(2)}) collective-permute-start(bf16[16,7168]{1,0:T(8,128)(2,1)} %collective-permute-done.13.refs_2_), channel_id=1, source_target_pairs={{0,96},{32,0},{64,32},{96,64},{1,97},{33,1},{65,33},{97,65},{2,98}... | collective-permute-start | bytes 688136 | tf_op jit(solution)/shard_map/ppermute | solution.py:23
  (9 other events, 230.4 us)

commit v3 on v1

v3 whole, which is shorter than its diff:
```python
import functools

import jax
import jax.numpy as jnp
from jax import lax
from jax.experimental import pallas as pl
from jax.experimental.pallas import tpu as pltpu
from jax.sharding import PartitionSpec as P

DECAY_RATE = 0.999
CHUNKS = 2
ANY = pl.BlockSpec(memory_space=pl.ANY)
SMEM = pl.BlockSpec(memory_space=pltpu.SMEM)


def shift(x, step):
    count = lax.axis_size("dp")
    return lax.ppermute(x, "dp", [(i, (i + step) % count) for i in range(count)])


def add(*terms):
    total = terms[0].astype(jnp.float32)
    for term in terms[1:]:
        total += term.astype(jnp.float32)
    return total.astype(terms[0].dtype)


def run_all(copies):
    for copy in copies:
        copy.start()
    for copy in copies:
        copy.wait()


def cost(moved, flops=0):
    return pl.CostEstimate(flops=flops, bytes_accessed=moved, transcendentals=0)


def pack_kernel(base, index_ref, me_ref, grad_ref, next_ref, prev_ref, out_ref, own, near, far, pieces, in_sems, out_sems):
    rows = own.shape[0]
    wide_count, _, block_cols = pieces.shape
    start = pl.multiple_of(base + me_ref[0] * rows, rows)
    run_all(
        [
            pltpu.make_async_copy(grad_ref.at[0, pl.ds(start, rows)], own, in_sems.at[0]),
            pltpu.make_async_copy(next_ref, near, in_sems.at[1]),
            pltpu.make_async_copy(prev_ref, far, in_sems.at[2]),
        ]
    )
    for w in range(wide_count):
        cols = slice(w * block_cols, (w + 1) * block_cols)
        pieces[w] = add(own[:, cols], near[:, cols], far[:, cols])
    run_all(
        [
            pltpu.make_async_copy(pieces.at[index_ref[c]], out_ref.at[c], out_sems.at[c])
            for c in range(out_ref.shape[0])
        ]
    )


def pack(base, index, me, grad_parts, from_next, from_prev, block_cols):
    rows, width = from_next.shape
    dtype = from_next.dtype
    dests = index.shape[0]
    return pl.pallas_call(
        functools.partial(pack_kernel, base),
        out_shape=jax.ShapeDtypeStruct((dests, rows, block_cols), dtype),
        in_specs=[SMEM, SMEM, ANY, ANY, ANY],
        out_specs=ANY,
        scratch_shapes=[pltpu.VMEM((rows, width), dtype)] * 3
        + [
            pltpu.VMEM((width // block_cols, rows, block_cols), dtype),
            pltpu.SemaphoreType.DMA((3,)),
            pltpu.SemaphoreType.DMA((dests,)),
        ],
        cost_estimate=cost(8 * rows * width + 2 * dests * rows * block_cols),
        name="pack",
    )(index, me, grad_parts, from_next, from_prev)


def pick_kernel(inputs, index_ref, *refs):
    sources, outs, stage, in_sems, out_sems = refs[:inputs], refs[inputs:-3], refs[-3], refs[-2], refs[-1]
    each = sources[0].shape[0]
    run_all(
        [
            pltpu.make_async_copy(source, stage.at[pl.ds(i * each, each)], in_sems.at[i])
            for i, source in enumerate(sources)
        ]
    )
    copies = []
    for out in outs:
        for i in range(out.shape[0]):
            at = len(copies)
            copies.append(pltpu.make_async_copy(stage.at[index_ref[at]], out.at[i], out_sems.at[at]))
    run_all(copies)


def pick(index, sources, out_counts):
    each, *entry = sources[0].shape
    dtype = sources[0].dtype
    total = each * len(sources)
    taken = sum(out_counts)
    size = 2 * entry[0] * entry[1] * entry[2]
    return pl.pallas_call(
        functools.partial(pick_kernel, len(sources)),
        out_shape=[jax.ShapeDtypeStruct((n, *entry), dtype) for n in out_counts],
        in_specs=[SMEM] + [ANY] * len(sources),
        out_specs=[ANY] * len(out_counts),
        scratch_shapes=[
            pltpu.VMEM((total, *entry), dtype),
            pltpu.SemaphoreType.DMA((len(sources),)),
            pltpu.SemaphoreType.DMA((taken,)),
        ],
        cost_estimate=cost((total + taken) * size),
        name="pick",
    )(index, *sources)


def precondition_kernel(
    used_ref, me_ref, own_ref, *refs
):
    rel = (own_ref,) + refs[:3]
    second_ref, left_ref, right_ref, grad_ref, first_out = refs[3:8]
    rel_out = refs[8:12]
    grad, left, right, update, in_sems, root_sems, grad_sems, out_sems = refs[12:]
    slots = left.shape[0]
    count = second_ref.shape[0]
    block = left.shape[1]
    me = me_ref[0]
    roots = [
        pltpu.make_async_copy(left_ref, left, root_sems.at[0]),
        pltpu.make_async_copy(right_ref, right, root_sems.at[1]),
    ]
    loads = [
        pltpu.make_async_copy(rel[d], grad.at[:, :, 0, (me + count - d) % count], in_sems.at[d]) for d in range(count)
    ] + [
        pltpu.make_async_copy(second_ref.at[q], grad.at[:, :, 1, q], in_sems.at[count + q]) for q in range(count)
    ]
    for copy in loads + roots:
        copy.start()
    for copy in loads + roots:
        copy.wait()
    outs = []
    for s in range(slots):
        whole = grad[s].reshape(block, block)
        whole = jnp.where(used_ref[s] > 0, whole, jnp.zeros_like(whole))
        grad[s] = whole.reshape(grad.shape[1:])
        keep = pltpu.make_async_copy(grad.at[s], grad_ref.at[s], grad_sems.at[s])
        keep.start()
        part = jnp.dot(left[s], whole, preferred_element_type=jnp.float32).astype(whole.dtype)
        result = jnp.dot(part, right[s], preferred_element_type=jnp.float32).astype(whole.dtype)
        update[s] = result.reshape(update.shape[1:])
        sends = [
            pltpu.make_async_copy(update.at[s, :, 0, q], first_out.at[q, s], out_sems.at[s, q]) for q in range(count)
        ] + [
            pltpu.make_async_copy(update.at[s, :, 1, (me + d) % count], rel_out[d].at[s], out_sems.at[s, count + d])
            for d in range(count)
        ]
        for copy in sends:
            copy.start()
        outs += sends + [keep]
    for copy in outs:
        copy.wait()


def precondition(used, me, rel, second, root_left, root_right):
    count = second.shape[0]
    slots, halves, rows, cols = rel[0].shape
    dtype = second.dtype
    block = root_left.shape[1]
    piece = jax.ShapeDtypeStruct(rel[0].shape, dtype)
    layout = (slots, halves, CHUNKS, count, rows, cols)
    outs = pl.pallas_call(
        precondition_kernel,
        out_shape=[jax.ShapeDtypeStruct(layout, dtype), jax.ShapeDtypeStruct(second.shape, dtype)] + [piece] * count,
        in_specs=[SMEM, SMEM] + [ANY] * (count + 3),
        out_specs=[ANY] * (count + 2),
        scratch_shapes=[
            pltpu.VMEM(layout, dtype),
            pltpu.VMEM(root_left.shape, dtype),
            pltpu.VMEM(root_right.shape, dtype),
            pltpu.VMEM(layout, dtype),
            pltpu.SemaphoreType.DMA((2 * count,)),
            pltpu.SemaphoreType.DMA((2,)),
            pltpu.SemaphoreType.DMA((slots,)),
            pltpu.SemaphoreType.DMA((slots, 2 * count)),
        ],
        compiler_params=pltpu.CompilerParams(vmem_limit_bytes=24 * 1024 * 1024),
        cost_estimate=cost(10 * slots * block * block, 4 * slots * block**3),
        name="precondition",
    )(used, me, *rel, second, root_left, root_right)
    return outs[0].reshape(slots, block, block), outs[1], outs[2:]


def unpack_kernel(index_ref, pieces_ref, out_ref, stage, in_sems, out_sem):
    cols = pieces_ref.shape[2]
    run_all(
        [
            pltpu.make_async_copy(pieces_ref.at[index_ref[w]], stage.at[:, pl.ds(w * cols, cols)], in_sems.at[w])
            for w in range(index_ref.shape[0])
        ]
    )
    run_all([pltpu.make_async_copy(stage, out_ref, out_sem)])


def unpack(index, pieces):
    _, rows, cols = pieces.shape
    shape = (rows, index.shape[0] * cols)
    return pl.pallas_call(
        unpack_kernel,
        out_shape=jax.ShapeDtypeStruct(shape, pieces.dtype),
        in_specs=[SMEM, ANY],
        out_specs=ANY,
        scratch_shapes=[
            pltpu.VMEM(shape, pieces.dtype),
            pltpu.SemaphoreType.DMA((index.shape[0],)),
            pltpu.SemaphoreType.DMA,
        ],
        cost_estimate=cost(4 * rows * shape[1]),
        name="unpack",
    )(index, pieces)


def place_kernel(base, me_ref, *refs):
    parts = refs[:5]
    out_ref, stage, in_sems, out_sems = refs[-4:]
    quarter = parts[0].shape[0]
    half = parts[3].shape[0]
    me = me_ref[0]
    places = ((0, 0), (1, 0), (3, 0), (2, 0), (2, half))
    loads, stores = [], []
    for i, (offset, down) in enumerate(places):
        rows = parts[i].shape[0]
        held = stage.at[pl.ds(offset * quarter + down, rows)]
        start = pl.multiple_of(base + (me + offset) % 4 * quarter + down, half)
        loads.append(pltpu.make_async_copy(parts[i], held, in_sems.at[i]))
        stores.append(pltpu.make_async_copy(held, out_ref.at[pl.ds(start, rows)], out_sems.at[i]))
    for load in loads:
        load.start()
    for load, store in zip(loads, stores):
        load.wait()
        store.start()
    for store in stores:
        store.wait()


def gather_over_replicas(me, own, updates, base, total_rows):
    quarter, width = own.shape
    half = quarter // 2
    from_prev = shift(own, 1)
    from_next = shift(own, -1)
    far_first = shift(from_prev[:half], 1)
    far_second = shift(from_next[half:], -1)
    operands = [me, own, from_next, from_prev, far_first, far_second]
    aliases = {}
    if updates is not None:
        aliases = {len(operands): 0}
        operands.append(updates)
    return pl.pallas_call(
        functools.partial(place_kernel, base),
        out_shape=jax.ShapeDtypeStruct((total_rows, width), own.dtype),
        in_specs=[SMEM] + [ANY] * (len(operands) - 1),
        out_specs=ANY,
        scratch_shapes=[
            pltpu.VMEM((4 * quarter, width), own.dtype),
            pltpu.SemaphoreType.DMA((5,)),
            pltpu.SemaphoreType.DMA((5,)),
        ],
        input_output_aliases=aliases,
        cost_estimate=cost(16 * quarter * width),
        name="place",
    )(*operands)


def expert_exchange(x):
    return lax.all_to_all(x, "expert", split_axis=0, concat_axis=0, tiled=True)


def replica_exchange(x):
    return lax.all_to_all(x, "dp", split_axis=0, concat_axis=0, tiled=True)


def shards(grad_parts, owner_slot, stat_left, stat_right, root_left, root_right):
    dp_count = lax.axis_size("dp")
    expert_count = lax.axis_size("expert")
    shard_rows = grad_parts.shape[1]
    row_width = grad_parts.shape[2]
    slot_count, block_rows, block_cols = stat_left.shape
    wide_count = row_width // block_cols
    halves = block_rows // shard_rows
    row_blocks = expert_count // halves
    block_count = owner_slot.shape[0]
    chunk_rows = shard_rows // CHUNKS
    quarter = chunk_rows // dp_count
    half = quarter // 2
    held_count = dp_count * slot_count

    my_expert = lax.axis_index("expert")
    my_dp = lax.axis_index("dp")
    me = my_dp.astype(jnp.int32).reshape(1)
    blocks = jnp.arange(block_count, dtype=jnp.int32)
    column = owner_slot // slot_count % expert_count

    my_column = lax.dynamic_slice(column, (my_expert // halves * wide_count,), (wide_count,))
    to_column = my_column[None, :] == jnp.arange(expert_count, dtype=jnp.int32)[:, None]
    pieces = jnp.arange(wide_count, dtype=jnp.int32)
    send_piece = jnp.sum(jnp.where(to_column, pieces[None, :], 0), axis=1)

    held = jnp.arange(held_count, dtype=jnp.int32)
    row_ids = jnp.arange(row_blocks, dtype=jnp.int32)

    def held_rows(replica):
        slot_ids = (replica * expert_count + my_expert) * slot_count + held % slot_count
        holds = owner_slot[None, :] == slot_ids[:, None]
        return jnp.sum(jnp.where(holds, blocks[None, :] // wide_count, 0), axis=1), jnp.any(holds, axis=1)

    def held_of_row(replica):
        rows, used = held_rows(replica)
        match = (rows[None, :] == row_ids[:, None]) & used[None, :]
        return jnp.sum(jnp.where(match, held[None, :], 0), axis=1)

    order = held // slot_count
    row_from, used = held_rows(order)
    row_from_rel, _ = held_rows((my_dp + order) % dp_count)
    back_from = held_of_row(order)
    back_from_rel = held_of_row((my_dp + dp_count - order) % dp_count)
    my_used = lax.dynamic_slice(used.astype(jnp.int32), (my_dp * slot_count,), (slot_count,))

    def part(chunk, offset, down, rows):
        start = chunk * chunk_rows + (my_dp + offset) % dp_count * quarter + down
        return lax.dynamic_slice(grad_parts, (0, start, 0), (1, rows, row_width))[0]

    def toward(chunk, from_next, from_prev):
        to_prev = add(part(chunk, 3, 0, quarter), jnp.pad(from_next, ((0, half), (0, 0))))
        to_next = add(part(chunk, 1, 0, quarter), jnp.pad(from_prev, ((half, 0), (0, 0))))
        return to_prev, to_next

    def relay(first, second):
        return shift(first, -1), shift(second, 1)

    def packed(chunk, to_prev, to_next):
        return pack(chunk * chunk_rows, send_piece, me, grad_parts, shift(to_prev, -1), shift(to_next, 1), block_cols)

    sends = toward(0, *relay(part(0, 2, 0, half), part(0, 2, half, half)))
    relays, sends = lax.optimization_barrier(((part(1, 2, 0, half), part(1, 2, half, half)), sends))
    first_packed = packed(0, *sends)
    sends = toward(1, *relay(*relays))
    sends, first_packed = lax.optimization_barrier((sends, first_packed))
    entry = (row_blocks, halves, quarter, block_cols)
    first_in = expert_exchange(first_packed).reshape(entry)
    second_packed = packed(1, *sends)
    rel = pick(row_from_rel, [first_in], (slot_count,) * dp_count)
    rel, second_packed = lax.optimization_barrier((rel, second_packed))
    rel = [rel[0]] + [shift(rel[d], d) for d in range(1, dp_count)]
    second_in = expert_exchange(second_packed).reshape(entry)
    (to_owner,) = pick(row_from, [second_in], (held_count,))
    second = replica_exchange(to_owner.reshape(dp_count, slot_count, *entry[1:]))

    grad, first_out, rel_out = precondition(my_used, me, rel, second, root_left, root_right)

    first_back = replica_exchange(first_out).reshape(held_count, *entry[1:])
    (to_rows,) = pick(back_from, [first_back], (row_blocks,))
    rel_out, to_rows = lax.optimization_barrier((rel_out, to_rows))
    rel_back = [rel_out[0]] + [shift(rel_out[d], d) for d in range(1, dp_count)]
    first_own = unpack(my_column, expert_exchange(to_rows.reshape(expert_count, quarter, block_cols)))
    (to_rows,) = pick(back_from_rel, rel_back, (row_blocks,))
    first_own, to_rows = lax.optimization_barrier((first_own, to_rows))
    second_own = unpack(my_column, expert_exchange(to_rows.reshape(expert_count, quarter, block_cols)))
    updates = gather_over_replicas(me, first_own, None, 0, shard_rows)
    updates = gather_over_replicas(me, second_own, updates, chunk_rows, shard_rows)

    left_gram = jnp.einsum("sij,skj->sik", grad, grad, preferred_element_type=jnp.float32)
    right_gram = jnp.einsum("sji,sjk->sik", grad, grad, preferred_element_type=jnp.float32)
    new_left = DECAY_RATE * stat_left + (1.0 - DECAY_RATE) * left_gram
    new_right = DECAY_RATE * stat_right + (1.0 - DECAY_RATE) * right_gram
    return new_left, new_right, updates


def solution(mesh):
    owned = P(("dp", "expert"), None, None)
    return jax.shard_map(
        shards,
        mesh=mesh,
        in_specs=(P("dp", "expert", None), P(), owned, owned, owned, owned),
        out_specs=(owned, owned, P("expert", None)),
        check_vma=False,
    )
```

time: 277 us -> 231 us (0.83)
  waiting for transfers between devices: 133 us -> 80.6 us
  Pallas kernels: 0 us -> 33 us
  starting transfers between devices: 31.2 us -> 60.6 us
  blocking collectives: 46 us -> 24.8 us
  local copies, waits for them, and re-layouts: 32.7 us -> 14.9 us
  between operations: 14 us -> 1.17 us
  matrix products: 12.2 us -> 7.68 us
    ppermute x0 -> x22, waiting for transfers between devices: none -> 54.9 us  [shift(): lax.ppermute(x, 'dp', [(i, (i + step) % count) for i in range(count)])]
    reduce_scatter x2 -> x0, waiting for transfers between devices: 50 us -> none  [shards(): part = lax.psum_scatter(rows, 'dp', scatter_dimension=0, tiled=True)]
    all_to_all x6 -> x5, waiting for transfers between devices: 65.6 us -> 25.7 us  [the longest x3 15 us: expert_exchange(): return lax.all_to_all(x, 'expert', split_axis=0, concat_axis=0, tiled=True)]
    ppermute x0 -> x22, starting transfers between devices: none -> 35.4 us  [shift(): lax.ppermute(x, 'dp', [(i, (i + step) % count) for i in range(count)])]
    pallas_call x0 -> x11, Pallas kernels: none -> 33 us  [the longest x4 11.6 us: pick(): pl.pallas_call(functools.partial(pick_kernel, len(sources)), out_shape=[j...]
    all_to_all x2 -> x1, blocking collectives: 46 us -> 24.8 us  [expert_exchange(): return lax.all_to_all(x, 'expert', split_axis=0, concat_axis=0, tiled=True)]
    gather x8 -> x0, local copies, waits for them, and re-layouts: 18 us -> none  [the longest x2 5.43 us: shards(): column_part[back_held].reshape(expert_count, part_rows, block_cols)]
    all_gather x2 -> x0, waiting for transfers between devices: 17 us -> none  [shards(): out.append(lax.all_gather(part, 'dp', axis=0, tiled=True))]
  transfers between devices with their start and end apart: 10 -> 27, of which waited for: 8 -> 14; matrix products, arithmetic and copies ran while one was open for 10% -> 6% of each run, Pallas kernels for 0% -> 5%
where the time goes in v3:
time: 231 us; the launch traced here: 229 us
  waiting for transfers between devices  80.6 us (35%)
  starting transfers between devices  60.6 us (26%)
  Pallas kernels  33 us (14%)
  blocking collectives  24.8 us (11%)
  local copies, waits for them, and re-layouts  14.9 us (6%)
  matrix products  7.68 us (3%)
  other arithmetic  6.66 us (3%)
    ppermute x22, waiting for transfers between devices, shift(): lax.ppermute(x, 'dp', [(i, (i + step) % count) for i in range(count)])  54.9 us
    ppermute x22, starting transfers between devices, shift(): lax.ppermute(x, 'dp', [(i, (i + step) % count) for i in range(count)])  35.4 us
    all_to_all x1, blocking collectives, expert_exchange(): return lax.all_to_all(x, 'expert', split_axis=0, concat_axis=0, tiled=True)  24.8 us
    all_to_all x3, starting transfers between devices, expert_exchange(): return lax.all_to_all(x, 'expert', split_axis=0, concat_axis=0, tiled=True)  18.1 us
    all_to_all x3, waiting for transfers between devices, expert_exchange(): return lax.all_to_all(x, 'expert', split_axis=0, concat_axis=0, tiled=True)  15 us
    unnamed x60, local copies, waits for them, and re-layouts  11.9 us
    pallas_call x4, Pallas kernels, pick(): pl.pallas_call(functools.partial(pick_kernel, len(sources)), out_shape=[j...  11.6 us
    all_to_all x2, waiting for transfers between devices, replica_exchange(): return lax.all_to_all(x, 'dp', split_axis=0, concat_axis=0, tiled=True)  10.7 us
  transfers between devices with their start and end apart: 27, of which 14 were waited for; matrix products, arithmetic and copies ran while one was open for 6% of the time, Pallas kernels for 5%

profile of v3, /device:TPU:0, one launch (start us, length us, event | category | flops | bytes accessed | tf_op | source)
XLA Modules:
  0.0 229.4 jit_solution(7495555833677587126)
XLA Ops:
  6.3 5.5 %collective-permute-done.1 = bf16[16,7168]{1,0:T(8,128)(2,1)S(1)} collective-permute-done((bf16[16,7168]{1,0:T(8,128)(2,1)S(1)}, bf16[16,7168]{1,0:T(8,128)(2,1)S(1)}, u32[]{:S(2)}, u32[]{:S(2)}) %collective-permute-start.1) | collective-permute-done | bytes 229408 | tf_op jit(solution)/shard_map/ppermute | solution.py:18
  13.1 3.1 %collective-permute-start.2 = (bf16[16,7168]{1,0:T(8,128)(2,1)S(1)}, bf16[16,7168]{1,0:T(8,128)(2,1)S(1)}, u32[]{:S(2)}, u32[]{:S(2)}) collective-permute-start(bf16[16,7168]{1,0:T(8,128)(2,1)S(1)} %get-tuple-element.32), channel_id=1, source_target_pairs={{0,96},{32,0},{64,32},{96,64},{1,97},{33,1},{65,33},{97,65},{2,98}... | collective-permute-start | bytes 688136 | tf_op jit(solution)/shard_map/ppermute | solution.py:18
  17.0 3.2 %collective-permute-start.4 = (bf16[32,7168]{1,0:T(8,128)(2,1)S(1)}, bf16[32,7168]{1,0:T(8,128)(2,1)S(1)}, u32[]{:S(2)}, u32[]{:S(2)}) collective-permute-start(bf16[32,7168]{1,0:T(8,128)(2,1)S(1)} %get-tuple-element.34), channel_id=1, source_target_pairs={{0,96},{32,0},{64,32},{96,64},{1,97},{33,1},{65,33},{97,65},{2,98}... | collective-permute-start | bytes 1376264 | tf_op jit(solution)/shard_map/ppermute | solution.py:18
  21.6 3.4 %collective-permute-done.3 = bf16[16,7168]{1,0:T(8,128)(2,1)S(1)} collective-permute-done((bf16[16,7168]{1,0:T(8,128)(2,1)S(1)}, bf16[16,7168]{1,0:T(8,128)(2,1)S(1)}, u32[]{:S(2)}, u32[]{:S(2)}) %collective-permute-start.3) | collective-permute-done | bytes 229408 | tf_op jit(solution)/shard_map/ppermute | solution.py:18
  26.3 3.7 %collective-permute-done.4.next_ref = bf16[32,7168]{1,0:T(8,128)(2,1)S(1)} collective-permute-done((bf16[32,7168]{1,0:T(8,128)(2,1)S(1)}, bf16[32,7168]{1,0:T(8,128)(2,1)S(1)}, u32[]{:S(2)}, u32[]{:S(2)}) %collective-permute-start.4) | collective-permute-done | bytes 458784 | tf_op jit(solution)/shard_map/ppermute | solution.py:18
  30.0 3.4 %collective-permute-done.5.prev_ref = bf16[32,7168]{1,0:T(8,128)(2,1)S(1)} collective-permute-done((bf16[32,7168]{1,0:T(8,128)(2,1)S(1)}, bf16[32,7168]{1,0:T(8,128)(2,1)S(1)}, u32[]{:S(2)}, u32[]{:S(2)}) %collective-permute-start.5) | collective-permute-done | bytes 458784 | tf_op jit(solution)/shard_map/ppermute | solution.py:18
  34.2 3.4 %pack.2 = bf16[32,32,512]{2,1,0:T(8,128)(2,1)} custom-call(s32[32]{0:T(128)} %select_reduce_fusion.3.index_ref, s32[1]{0:T(128)} %bitcast.me_ref, bf16[1,256,7168]{2,1,0:T(8,128)(2,1)} %grad_ref.3, bf16[32,7168]{1,0:T(8,128)(2,1)} %copy-done.16, bf16[32,7168]{1,0:T(8,128)(2,1)} %copy-done.18), custom_call_target="tpu_custom_call" | custom-call | bytes 2883584 | tf_op jit(solution)/shard_map/pack/pallas_call | solution.py:65
  37.6 7.3 %all-to-all-start = ((bf16[32,32,512]{2,1,0:T(8,128)(2,1)}), bf16[32,32,512]{2,1,0:T(8,128)(2,1)S(1)}, u32[]{:S(2)}, u32[]{:S(2)}) async-start(bf16[32,32,512]{2,1,0:T(8,128)(2,1)} %pack.2), calls=%async_computation | async-start | bytes 2097152 | tf_op jit(solution)/shard_map/all_to_all | solution.py:276
  47.8 9.9 %collective-permute-done.6.next_ref = bf16[32,7168]{1,0:T(8,128)(2,1)S(1)} collective-permute-done((bf16[32,7168]{1,0:T(8,128)(2,1)S(1)}, bf16[32,7168]{1,0:T(8,128)(2,1)S(1)}, u32[]{:S(2)}, u32[]{:S(2)}) %collective-permute-start.6) | collective-permute-done | bytes 458784 | tf_op jit(solution)/shard_map/ppermute | solution.py:18
  59.8 3.4 %pack.3 = bf16[32,32,512]{2,1,0:T(8,128)(2,1)} custom-call(s32[32]{0:T(128)} %select_reduce_fusion.3.index_ref, s32[1]{0:T(128)} %bitcast.me_ref, bf16[1,256,7168]{2,1,0:T(8,128)(2,1)} %grad_ref.3, bf16[32,7168]{1,0:T(8,128)(2,1)} %copy-done.15, bf16[32,7168]{1,0:T(8,128)(2,1)} %copy-done.17), custom_call_target="tpu_custom_call" | custom-call | bytes 2883584 | tf_op jit(solution)/shard_map/pack/pallas_call | solution.py:65
  64.2 2.8 %pick.4 = (bf16[3,2,32,512]{3,2,1,0:T(8,128)(2,1)}, bf16[3,2,32,512]{3,2,1,0:T(8,128)(2,1)}, bf16[3,2,32,512]{3,2,1,0:T(8,128)(2,1)}, bf16[3,2,32,512]{3,2,1,0:T(8,128)(2,1)}) custom-call(s32[12]{0:T(128)} %get-tuple-element.63.index_ref, bf16[16,2,32,512]{3,2,1,0:T(8,128)(2,1)} %bitcast.34), custom_call_target="tpu_custom_call" | custom-call | bytes 1835008 | tf_op jit(solution)/shard_map/pick/pallas_call | solution.py:104
  67.1 24.8 %all_to_all.30 = bf16[32,32,512]{2,1,0:T(8,128)(2,1)} all-to-all(bf16[32,32,512]{2,1,0:T(8,128)(2,1)} %pack.3), channel_id=1, replica_groups=mesh['dp'=4,'expert'=32] {'expert'}, dimensions={0} | all-to-all | bytes 2097152 | tf_op jit(solution)/shard_map/all_to_all | solution.py:276
  91.9 2.9 %pick.5 = bf16[12,2,32,512]{3,2,1,0:T(8,128)(2,1)} custom-call(s32[12]{0:T(128)} %get-tuple-element.62.index_ref, bf16[16,2,32,512]{3,2,1,0:T(8,128)(2,1)} %bitcast.37), custom_call_target="tpu_custom_call" | custom-call | bytes 1835008 | tf_op jit(solution)/shard_map/pick/pallas_call | solution.py:104
  94.8 3.5 %all-to-all-start.2 = ((bf16[4,3,2,32,512]{4,3,2,1,0:T(8,128)(2,1)}), bf16[4,3,2,32,512]{4,3,2,1,0:T(8,128)(2,1)S(1)}, u32[]{:S(2)}, u32[]{:S(2)}) async-start(bf16[4,3,2,32,512]{4,3,2,1,0:T(8,128)(2,1)} %bitcast.38), calls=%async_computation.2 | async-start | bytes 1572864 | tf_op jit(solution)/shard_map/all_to_all | solution.py:280
  105.2 10.3 %collective-permute-done.8.refs_0_ = bf16[3,2,32,512]{3,2,1,0:T(8,128)(2,1)S(1)} collective-permute-done((bf16[3,2,32,512]{3,2,1,0:T(8,128)(2,1)S(1)}, bf16[3,2,32,512]{3,2,1,0:T(8,128)(2,1)S(1)}, u32[]{:S(2)}, u32[]{:S(2)}) %collective-permute-start.8) | collective-permute-done | bytes 196640 | tf_op jit(solution)/shard_map/ppermute | solution.py:18
  115.5 4.1 %collective-permute-done.9.refs_1_ = bf16[3,2,32,512]{3,2,1,0:T(8,128)(2,1)S(1)} collective-permute-done((bf16[3,2,32,512]{3,2,1,0:T(8,128)(2,1)S(1)}, bf16[3,2,32,512]{3,2,1,0:T(8,128)(2,1)S(1)}, u32[]{:S(2)}, u32[]{:S(2)}) %collective-permute-start.9) | collective-permute-done | bytes 196640 | tf_op jit(solution)/shard_map/ppermute | solution.py:18
  124.0 4.9 %precondition.1 = (bf16[3,2,2,4,32,512]{5,4,3,2,1,0:T(8,128)(2,1)S(1)}, bf16[4,3,2,32,512]{4,3,2,1,0:T(8,128)(2,1)}, bf16[3,2,32,512]{3,2,1,0:T(8,128)(2,1)S(1)}...) custom-call(s32[3]{0:T(128)S(1)} %dynamic_slice.30.used_ref, ...), custom_call_target="tpu_custom_call" | custom-call | flops 1610612736 | bytes 7864320 | tf_op jit(solution)/shard_map/precondition/pallas_call | solution.py:173
  129.6 3.6 %all-to-all-start.3 = ((bf16[4,3,2,32,512]{4,3,2,1,0:T(8,128)(2,1)}), bf16[4,3,2,32,512]{4,3,2,1,0:T(8,128)(2,1)S(1)}, u32[]{:S(2)}, u32[]{:S(2)}) async-start(bf16[4,3,2,32,512]{4,3,2,1,0:T(8,128)(2,1)} %get-tuple-element.53), calls=%async_computation.3 | async-start | bytes 1572864 | tf_op jit(solution)/shard_map/all_to_all | solution.py:280
  134.6 10.7 %all-to-all-done.3 = bf16[4,3,2,32,512]{4,3,2,1,0:T(8,128)(2,1)S(1)} async-done(((bf16[4,3,2,32,512]{4,3,2,1,0:T(8,128)(2,1)}), bf16[4,3,2,32,512]{4,3,2,1,0:T(8,128)(2,1)S(1)}, u32[]{:S(2)}, u32[]{:S(2)}) %all-to-all-start.3) | async-done | bytes 786464 | tf_op jit(solution)/shard_map/all_to_all | solution.py:280
  146.1 2.9 %pick.6 = bf16[16,2,32,512]{3,2,1,0:T(8,128)(2,1)} custom-call(s32[16]{0:T(128)} %select_reduce_fusion.2.index_ref, bf16[12,2,32,512]{3,2,1,0:T(8,128)(2,1)} %bitcast.39), custom_call_target="tpu_custom_call" | custom-call | bytes 1835008 | tf_op jit(solution)/shard_map/pick/pallas_call | solution.py:104
  149.0 4.5 %all-to-all-start.4 = ((bf16[32,32,512]{2,1,0:T(8,128)(2,1)}), bf16[32,32,512]{2,1,0:T(8,128)(2,1)S(1)}, u32[]{:S(2)}, u32[]{:S(2)}) async-start(bf16[32,32,512]{2,1,0:T(8,128)(2,1)} %bitcast.35), calls=%async_computation.4 | async-start | bytes 2097152 | tf_op jit(solution)/shard_map/all_to_all | solution.py:276
  157.5 8.5 %collective-permute-done.11.refs_1_ = bf16[3,2,32,512]{3,2,1,0:T(8,128)(2,1)S(1)} collective-permute-done((bf16[3,2,32,512]{3,2,1,0:T(8,128)(2,1)S(1)}, bf16[3,2,32,512]{3,2,1,0:T(8,128)(2,1)S(1)}, u32[]{:S(2)}, u32[]{:S(2)}) %collective-permute-start.11) | collective-permute-done | bytes 196640 | tf_op jit(solution)/shard_map/ppermute | solution.py:18
  166.8 3.0 %pick.7 = bf16[16,2,32,512]{3,2,1,0:T(8,128)(2,1)} custom-call(s32[16]{0:T(128)} %select_reduce_fusion.1.index_ref, bf16[3,2,32,512]{3,2,1,0:T(8,128)(2,1)} %copy-done, bf16[3,2,32,512]{3,2,1,0:T(8,128)(2,1)} %copy-done.20, bf16[3,2,32,512]{3,2,1,0:T(8,128)(2,1)} %copy-done.21, bf16[3,2,32,512]{3,2,1,0:T(8,128)(2,1)} %collective-permute-done.13.refs_3_), custom_call_target="tpu_custom_call" | custom-call | bytes 1835008 | tf_op jit(solution)/shard_map/pick/pallas_call | solution.py:104
  174.3 6.3 %all-to-all-start.5 = ((bf16[32,32,512]{2,1,0:T(8,128)(2,1)}), bf16[32,32,512]{2,1,0:T(8,128)(2,1)S(1)}, u32[]{:S(2)}, u32[]{:S(2)}) async-start(bf16[32,32,512]{2,1,0:T(8,128)(2,1)} %bitcast.36), calls=%async_computation.5 | async-start | bytes 2097152 | tf_op jit(solution)/shard_map/all_to_all | solution.py:276
  181.0 2.9 %collective-permute-start.18 = (bf16[32,7168]{1,0:T(8,128)(2,1)}, bf16[32,7168]{1,0:T(8,128)(2,1)S(1)}, u32[]{:S(2)}, u32[]{:S(2)}) collective-permute-start(bf16[32,7168]{1,0:T(8,128)(2,1)} %unpack.2.refs_0_), channel_id=1, source_target_pairs={{0,96},{32,0},{64,32},{96,64},{1,97},{33,1},{65,33},{97,65},{2,98}... | collective-permute-start | bytes 1376264 | tf_op jit(solution)/shard_map/ppermute | solution.py:18
  183.9 14.0 %all-to-all-done.5.pieces_ref = bf16[32,32,512]{2,1,0:T(8,128)(2,1)S(1)} async-done(((bf16[32,32,512]{2,1,0:T(8,128)(2,1)}), bf16[32,32,512]{2,1,0:T(8,128)(2,1)S(1)}, u32[]{:S(2)}, u32[]{:S(2)}) %all-to-all-start.5) | async-done | bytes 1048608 | tf_op jit(solution)/shard_map/all_to_all | solution.py:276
  201.8 2.9 %collective-permute-start.14 = (bf16[32,7168]{1,0:T(8,128)(2,1)}, bf16[32,7168]{1,0:T(8,128)(2,1)S(1)}, u32[]{:S(2)}, u32[]{:S(2)}) collective-permute-start(bf16[32,7168]{1,0:T(8,128)(2,1)} %unpack.3.refs_0_), channel_id=1, source_target_pairs={{0,96},{32,0},{64,32},{96,64},{1,97},{33,1},{65,33},{97,65},{2,98}... | collective-permute-start | bytes 1376264 | tf_op jit(solution)/shard_map/ppermute | solution.py:18
  204.8 4.9 %multiply_add_fusion = f32[3,512,512]{2,1,0:T(8,128)} fusion(f32[3,512,512]{2,1,0:T(8,128)} %param.9, bf16[3,512,512]{2,1,0:T(8,128)(2,1)S(1)} %bitcast.32), kind=kOutput, calls=%fused_computation | convolution fusion | flops 807665664 | bytes 7864320 | tf_op jit(solution)/shard_map/sji,sjk->sik/dot_general | solution.py:373
  209.8 3.3 %collective-permute-start.21 = (bf16[16,7168]{1,0:T(8,128)(2,1)S(1)}, bf16[16,7168]{1,0:T(8,128)(2,1)}, u32[]{:S(2)}, u32[]{:S(2)}) collective-permute-start(bf16[16,7168]{1,0:T(8,128)(2,1)S(1)} %slice.19), channel_id=1, source_target_pairs={{0,96},{32,0},{64,32},{96,64},{1,97},{33,1},{65,33},{97,65},{2,98}... | collective-permute-start | bytes 688136 | tf_op jit(solution)/shard_map/ppermute | solution.py:18
  213.1 3.2 %collective-permute-done.15.refs_2_ = bf16[32,7168]{1,0:T(8,128)(2,1)S(1)} collective-permute-done((bf16[32,7168]{1,0:T(8,128)(2,1)}, bf16[32,7168]{1,0:T(8,128)(2,1)S(1)}, u32[]{:S(2)}, u32[]{:S(2)}) %collective-permute-start.15) | collective-permute-done | bytes 458784 | tf_op jit(solution)/shard_map/ppermute | solution.py:18
  217.8 3.2 %collective-permute-start.17 = (bf16[16,7168]{1,0:T(8,128)(2,1)}, bf16[16,7168]{1,0:T(8,128)(2,1)}, u32[]{:S(2)}, u32[]{:S(2)}) collective-permute-start(bf16[16,7168]{1,0:T(8,128)(2,1)} %slice.17), channel_id=1, source_target_pairs={{0,96},{32,0},{64,32},{96,64},{1,97},{33,1},{65,33},{97,65},{2,98}... | collective-permute-start | bytes 688136 | tf_op jit(solution)/shard_map/ppermute | solution.py:18
  221.1 2.8 %multiply_add_fusion.1 = f32[3,512,512]{2,1,0:T(8,128)} fusion(f32[3,512,512]{2,1,0:T(8,128)S(1)} %copy-done.10, bf16[3,512,512]{2,1,0:T(8,128)(2,1)S(1)} %bitcast.33), kind=kOutput, calls=%fused_computation.1 | convolution fusion | flops 807665664 | bytes 7864320 | tf_op jit(solution)/shard_map/sij,skj->sik/dot_general | solution.py:372
  (114 shorter events, 51.8 us)
Async XLA Ops:
  2.0 9.8 %collective-permute-start.1 = (bf16[16,7168]{1,0:T(8,128)(2,1)S(1)}, bf16[16,7168]{1,0:T(8,128)(2,1)S(1)}, u32[]{:S(2)}, u32[]{:S(2)}) collective-permute-start(bf16[16,7168]{1,0:T(8,128)(2,1)S(1)} %get-tuple-element.70), channel_id=1, source_target_pairs={{0,32},{32,64},{64,96},{96,0},{1,33},{33,65},{65,97},{97,1},{2,34}... | collective-permute-start | bytes 688136 | tf_op jit(solution)/shard_map/ppermute | solution.py:18
  4.1 7.7 %collective-permute-start = (bf16[16,7168]{1,0:T(8,128)(2,1)S(1)}, bf16[16,7168]{1,0:T(8,128)(2,1)S(1)}, u32[]{:S(2)}, u32[]{:S(2)}) collective-permute-start(bf16[16,7168]{1,0:T(8,128)(2,1)S(1)} %get-tuple-element.71), channel_id=1, source_target_pairs={{0,96},{32,0},{64,32},{96,64},{1,97},{33,1},{65,33},{97,65},{2,98}... | collective-permute-start | bytes 688136 | tf_op jit(solution)/shard_map/ppermute | solution.py:18
  13.1 8.5 %collective-permute-start.2 = (bf16[16,7168]{1,0:T(8,128)(2,1)S(1)}, bf16[16,7168]{1,0:T(8,128)(2,1)S(1)}, u32[]{:S(2)}, u32[]{:S(2)}) collective-permute-start(bf16[16,7168]{1,0:T(8,128)(2,1)S(1)} %get-tuple-element.32), channel_id=1, source_target_pairs={{0,96},{32,0},{64,32},{96,64},{1,97},{33,1},{65,33},{97,65},{2,98}... | collective-permute-start | bytes 688136 | tf_op jit(solution)/shard_map/ppermute | solution.py:18
  16.2 8.9 %collective-permute-start.3 = (bf16[16,7168]{1,0:T(8,128)(2,1)S(1)}, bf16[16,7168]{1,0:T(8,128)(2,1)S(1)}, u32[]{:S(2)}, u32[]{:S(2)}) collective-permute-start(bf16[16,7168]{1,0:T(8,128)(2,1)S(1)} %get-tuple-element.33), channel_id=1, source_target_pairs={{0,32},{32,64},{64,96},{96,0},{1,33},{33,65},{65,97},{97,1},{2,34}... | collective-permute-start | bytes 688136 | tf_op jit(solution)/shard_map/ppermute | solution.py:18
  17.0 13.1 %collective-permute-start.4 = (bf16[32,7168]{1,0:T(8,128)(2,1)S(1)}, bf16[32,7168]{1,0:T(8,128)(2,1)S(1)}, u32[]{:S(2)}, u32[]{:S(2)}) collective-permute-start(bf16[32,7168]{1,0:T(8,128)(2,1)S(1)} %get-tuple-element.34), channel_id=1, source_target_pairs={{0,96},{32,0},{64,32},{96,64},{1,97},{33,1},{65,33},{97,65},{2,98}... | collective-permute-start | bytes 1376264 | tf_op jit(solution)/shard_map/ppermute | solution.py:18
  20.2 13.2 %collective-permute-start.5 = (bf16[32,7168]{1,0:T(8,128)(2,1)S(1)}, bf16[32,7168]{1,0:T(8,128)(2,1)S(1)}, u32[]{:S(2)}, u32[]{:S(2)}) collective-permute-start(bf16[32,7168]{1,0:T(8,128)(2,1)S(1)} %get-tuple-element.35), channel_id=1, source_target_pairs={{0,32},{32,64},{64,96},{96,0},{1,33},{33,65},{65,97},{97,1},{2,34}... | collective-permute-start | bytes 1376264 | tf_op jit(solution)/shard_map/ppermute | solution.py:18
  37.6 25.6 %all-to-all-start = ((bf16[32,32,512]{2,1,0:T(8,128)(2,1)}), bf16[32,32,512]{2,1,0:T(8,128)(2,1)S(1)}, u32[]{:S(2)}, u32[]{:S(2)}) async-start(bf16[32,32,512]{2,1,0:T(8,128)(2,1)} %pack.2), calls=%async_computation | async-start | bytes 2097152 | tf_op jit(solution)/shard_map/all_to_all | solution.py:276
  44.9 12.8 %collective-permute-start.6 = (bf16[32,7168]{1,0:T(8,128)(2,1)S(1)}, bf16[32,7168]{1,0:T(8,128)(2,1)S(1)}, u32[]{:S(2)}, u32[]{:S(2)}) collective-permute-start(bf16[32,7168]{1,0:T(8,128)(2,1)S(1)} %get-tuple-element.41), channel_id=1, source_target_pairs={{0,96},{32,0},{64,32},{96,64},{1,97},{33,1},{65,33},{97,65},{2,98}... | collective-permute-start | bytes 1376264 | tf_op jit(solution)/shard_map/ppermute | solution.py:18
  45.4 13.6 %collective-permute-start.7 = (bf16[32,7168]{1,0:T(8,128)(2,1)S(1)}, bf16[32,7168]{1,0:T(8,128)(2,1)S(1)}, u32[]{:S(2)}, u32[]{:S(2)}) collective-permute-start(bf16[32,7168]{1,0:T(8,128)(2,1)S(1)} %get-tuple-element.42), channel_id=1, source_target_pairs={{0,32},{32,64},{64,96},{96,0},{1,33},{33,65},{65,97},{97,1},{2,34}... | collective-permute-start | bytes 1376264 | tf_op jit(solution)/shard_map/ppermute | solution.py:18
  67.0 31.3 %copy-start.29 = (bf16[3,2,32,512]{3,2,1,0:T(8,128)(2,1)S(1)}, bf16[3,2,32,512]{3,2,1,0:T(8,128)(2,1)}, u32[]{:S(2)}) copy-start(bf16[3,2,32,512]{3,2,1,0:T(8,128)(2,1)} %get-tuple-element.44) | copy-start | bytes 589828
  67.0 33.2 %copy-start.28 = (bf16[3,2,32,512]{3,2,1,0:T(8,128)(2,1)S(1)}, bf16[3,2,32,512]{3,2,1,0:T(8,128)(2,1)}, u32[]{:S(2)}) copy-start(bf16[3,2,32,512]{3,2,1,0:T(8,128)(2,1)} %get-tuple-element.45) | copy-start | bytes 589828
  67.1 35.9 %copy-start.27 = (bf16[3,2,32,512]{3,2,1,0:T(8,128)(2,1)S(1)}, bf16[3,2,32,512]{3,2,1,0:T(8,128)(2,1)}, u32[]{:S(2)}) copy-start(bf16[3,2,32,512]{3,2,1,0:T(8,128)(2,1)} %get-tuple-element.46) | copy-start | bytes 589828
  67.1 53.2 %copy-start.3 = (bf16[3,2,32,512]{3,2,1,0:T(8,128)(2,1)S(1)}, bf16[3,2,32,512]{3,2,1,0:T(8,128)(2,1)}, u32[]{:S(2)}) copy-start(bf16[3,2,32,512]{3,2,1,0:T(8,128)(2,1)} %get-tuple-element.43.own_ref) | copy-start | bytes 589828
  94.8 25.5 %all-to-all-start.2 = ((bf16[4,3,2,32,512]{4,3,2,1,0:T(8,128)(2,1)}), bf16[4,3,2,32,512]{4,3,2,1,0:T(8,128)(2,1)S(1)}, u32[]{:S(2)}, u32[]{:S(2)}) async-start(bf16[4,3,2,32,512]{4,3,2,1,0:T(8,128)(2,1)} %bitcast.38), calls=%async_computation.2 | async-start | bytes 1572864 | tf_op jit(solution)/shard_map/all_to_all | solution.py:280
  98.3 17.2 %collective-permute-start.8 = (bf16[3,2,32,512]{3,2,1,0:T(8,128)(2,1)S(1)}, bf16[3,2,32,512]{3,2,1,0:T(8,128)(2,1)S(1)}, u32[]{:S(2)}, u32[]{:S(2)}) collective-permute-start(bf16[3,2,32,512]{3,2,1,0:T(8,128)(2,1)S(1)} %copy-done.29), channel_id=1, source_target_pairs={{0,32},{32,64},{64,96},{96,0},{1,33},{33,65},{65,97},{97,1},{2,34}... | collective-permute-start | bytes 589832 | tf_op jit(solution)/shard_map/ppermute | solution.py:18
  100.3 19.3 %collective-permute-start.9 = (bf16[3,2,32,512]{3,2,1,0:T(8,128)(2,1)S(1)}, bf16[3,2,32,512]{3,2,1,0:T(8,128)(2,1)S(1)}, u32[]{:S(2)}, u32[]{:S(2)}) collective-permute-start(bf16[3,2,32,512]{3,2,1,0:T(8,128)(2,1)S(1)} %copy-done.28), channel_id=1, source_target_pairs={{0,64},{32,96},{64,0},{96,32},{1,65},{33,97},{65,1},{97,33},{2,66}... | collective-permute-start | bytes 589832 | tf_op jit(solution)/shard_map/ppermute | solution.py:18
  103.0 16.6 %collective-permute-start.10 = (bf16[3,2,32,512]{3,2,1,0:T(8,128)(2,1)S(1)}, bf16[3,2,32,512]{3,2,1,0:T(8,128)(2,1)S(1)}, u32[]{:S(2)}, u32[]{:S(2)}) collective-permute-start(bf16[3,2,32,512]{3,2,1,0:T(8,128)(2,1)S(1)} %copy-done.27), channel_id=1, source_target_pairs={{0,96},{32,0},{64,32},{96,64},{1,97},{33,1},{65,33},{97,65},{2,98}... | collective-permute-start | bytes 589832 | tf_op jit(solution)/shard_map/ppermute | solution.py:18
  105.1 28.1 %copy-start.24 = (s32[12]{0:T(128)S(1)}, s32[12]{0:T(128)}, u32[]{:S(2)}) copy-start(s32[12]{0:T(128)} %get-tuple-element.62.index_ref) | copy-start | bytes 148
  129.6 15.6 %all-to-all-start.3 = ((bf16[4,3,2,32,512]{4,3,2,1,0:T(8,128)(2,1)}), bf16[4,3,2,32,512]{4,3,2,1,0:T(8,128)(2,1)S(1)}, u32[]{:S(2)}, u32[]{:S(2)}) async-start(bf16[4,3,2,32,512]{4,3,2,1,0:T(8,128)(2,1)} %get-tuple-element.53), calls=%async_computation.3 | async-start | bytes 1572864 | tf_op jit(solution)/shard_map/all_to_all | solution.py:280
  149.0 21.8 %all-to-all-start.4 = ((bf16[32,32,512]{2,1,0:T(8,128)(2,1)}), bf16[32,32,512]{2,1,0:T(8,128)(2,1)S(1)}, u32[]{:S(2)}, u32[]{:S(2)}) async-start(bf16[32,32,512]{2,1,0:T(8,128)(2,1)} %bitcast.35), calls=%async_computation.4 | async-start | bytes 2097152 | tf_op jit(solution)/shard_map/all_to_all | solution.py:276
  153.5 12.6 %collective-permute-start.11 = (bf16[3,2,32,512]{3,2,1,0:T(8,128)(2,1)S(1)}, bf16[3,2,32,512]{3,2,1,0:T(8,128)(2,1)S(1)}, u32[]{:S(2)}, u32[]{:S(2)}) collective-permute-start(bf16[3,2,32,512]{3,2,1,0:T(8,128)(2,1)S(1)} %get-tuple-element.56), channel_id=1, source_target_pairs={{0,32},{32,64},{64,96},{96,0},{1,33},{33,65},{65,97},{97,1},{2,34}... | collective-permute-start | bytes 589832 | tf_op jit(solution)/shard_map/ppermute | solution.py:18
  154.1 11.9 %collective-permute-start.12 = (bf16[3,2,32,512]{3,2,1,0:T(8,128)(2,1)S(1)}, bf16[3,2,32,512]{3,2,1,0:T(8,128)(2,1)S(1)}, u32[]{:S(2)}, u32[]{:S(2)}) collective-permute-start(bf16[3,2,32,512]{3,2,1,0:T(8,128)(2,1)S(1)} %get-tuple-element.57), channel_id=1, source_target_pairs={{0,64},{32,96},{64,0},{96,32},{1,65},{33,97},{65,1},{97,33},{2,66}... | collective-permute-start | bytes 589832 | tf_op jit(solution)/shard_map/ppermute | solution.py:18
  156.2 10.6 %collective-permute-start.13 = (bf16[3,2,32,512]{3,2,1,0:T(8,128)(2,1)S(1)}, bf16[3,2,32,512]{3,2,1,0:T(8,128)(2,1)}, u32[]{:S(2)}, u32[]{:S(2)}) collective-permute-start(bf16[3,2,32,512]{3,2,1,0:T(8,128)(2,1)S(1)} %get-tuple-element.58), channel_id=1, source_target_pairs={{0,96},{32,0},{64,32},{96,64},{1,97},{33,1},{65,33},{97,65},{2,98}... | collective-permute-start | bytes 589832 | tf_op jit(solution)/shard_map/ppermute | solution.py:18
  174.3 23.6 %all-to-all-start.5 = ((bf16[32,32,512]{2,1,0:T(8,128)(2,1)}), bf16[32,32,512]{2,1,0:T(8,128)(2,1)S(1)}, u32[]{:S(2)}, u32[]{:S(2)}) async-start(bf16[32,32,512]{2,1,0:T(8,128)(2,1)} %bitcast.36), calls=%async_computation.5 | async-start | bytes 2097152 | tf_op jit(solution)/shard_map/all_to_all | solution.py:276
  180.6 29.0 %collective-permute-start.19 = (bf16[32,7168]{1,0:T(8,128)(2,1)}, bf16[32,7168]{1,0:T(8,128)(2,1)S(1)}, u32[]{:S(2)}, u32[]{:S(2)}) collective-permute-start(bf16[32,7168]{1,0:T(8,128)(2,1)} %unpack.2.refs_0_), channel_id=1, source_target_pairs={{0,32},{32,64},{64,96},{96,0},{1,33},{33,65},{65,97},{97,1},{2,34}... | collective-permute-start | bytes 1376264 | tf_op jit(solution)/shard_map/ppermute | solution.py:18
  181.0 28.8 %collective-permute-start.18 = (bf16[32,7168]{1,0:T(8,128)(2,1)}, bf16[32,7168]{1,0:T(8,128)(2,1)S(1)}, u32[]{:S(2)}, u32[]{:S(2)}) collective-permute-start(bf16[32,7168]{1,0:T(8,128)(2,1)} %unpack.2.refs_0_), channel_id=1, source_target_pairs={{0,96},{32,0},{64,32},{96,64},{1,97},{33,1},{65,33},{97,65},{2,98}... | collective-permute-start | bytes 1376264 | tf_op jit(solution)/shard_map/ppermute | solution.py:18
  201.5 14.9 %collective-permute-start.15 = (bf16[32,7168]{1,0:T(8,128)(2,1)}, bf16[32,7168]{1,0:T(8,128)(2,1)S(1)}, u32[]{:S(2)}, u32[]{:S(2)}) collective-permute-start(bf16[32,7168]{1,0:T(8,128)(2,1)} %unpack.3.refs_0_), channel_id=1, source_target_pairs={{0,32},{32,64},{64,96},{96,0},{1,33},{33,65},{65,97},{97,1},{2,34}... | collective-permute-start | bytes 1376264 | tf_op jit(solution)/shard_map/ppermute | solution.py:18
  201.8 15.2 %collective-permute-start.14 = (bf16[32,7168]{1,0:T(8,128)(2,1)}, bf16[32,7168]{1,0:T(8,128)(2,1)S(1)}, u32[]{:S(2)}, u32[]{:S(2)}) collective-permute-start(bf16[32,7168]{1,0:T(8,128)(2,1)} %unpack.3.refs_0_), channel_id=1, source_target_pairs={{0,96},{32,0},{64,32},{96,64},{1,97},{33,1},{65,33},{97,65},{2,98}... | collective-permute-start | bytes 1376264 | tf_op jit(solution)/shard_map/ppermute | solution.py:18
  209.7 14.2 %collective-permute-start.20 = (bf16[16,7168]{1,0:T(8,128)(2,1)S(1)}, bf16[16,7168]{1,0:T(8,128)(2,1)S(1)}, u32[]{:S(2)}, u32[]{:S(2)}) collective-permute-start(bf16[16,7168]{1,0:T(8,128)(2,1)S(1)} %slice.18), channel_id=1, source_target_pairs={{0,32},{32,64},{64,96},{96,0},{1,33},{33,65},{65,97},{97,1},{2,34}... | collective-permute-start | bytes 688136 | tf_op jit(solution)/shard_map/ppermute | solution.py:18
  209.8 14.8 %collective-permute-start.21 = (bf16[16,7168]{1,0:T(8,128)(2,1)S(1)}, bf16[16,7168]{1,0:T(8,128)(2,1)}, u32[]{:S(2)}, u32[]{:S(2)}) collective-permute-start(bf16[16,7168]{1,0:T(8,128)(2,1)S(1)} %slice.19), channel_id=1, source_target_pairs={{0,96},{32,0},{64,32},{96,64},{1,97},{33,1},{65,33},{97,65},{2,98}... | collective-permute-start | bytes 688136 | tf_op jit(solution)/shard_map/ppermute | solution.py:18
  217.1 9.8 %collective-permute-start.16 = (bf16[16,7168]{1,0:T(8,128)(2,1)}, bf16[16,7168]{1,0:T(8,128)(2,1)}, u32[]{:S(2)}, u32[]{:S(2)}) collective-permute-start(bf16[16,7168]{1,0:T(8,128)(2,1)} %slice.16), channel_id=1, source_target_pairs={{0,32},{32,64},{64,96},{96,0},{1,33},{33,65},{65,97},{97,1},{2,34}... | collective-permute-start | bytes 688136 | tf_op jit(solution)/shard_map/ppermute | solution.py:18
  217.8 9.1 %collective-permute-start.17 = (bf16[16,7168]{1,0:T(8,128)(2,1)}, bf16[16,7168]{1,0:T(8,128)(2,1)}, u32[]{:S(2)}, u32[]{:S(2)}) collective-permute-start(bf16[16,7168]{1,0:T(8,128)(2,1)} %slice.17), channel_id=1, source_target_pairs={{0,96},{32,0},{64,32},{96,64},{1,97},{33,1},{65,33},{97,65},{2,98}... | collective-permute-start | bytes 688136 | tf_op jit(solution)/shard_map/ppermute | solution.py:18
  (25 other events, 155.0 us)

commit v4 on v3

--- a/solution.py
+++ b/solution.py
@@ -34,6 +34,10 @@
 
 def cost(moved, flops=0):
     return pl.CostEstimate(flops=flops, bytes_accessed=moved, transcendentals=0)
+
+
+def vmem(mebibytes):
+    return pltpu.CompilerParams(vmem_limit_bytes=mebibytes * 1024 * 1024)
 
 
 def pack_kernel(base, index_ref, me_ref, grad_ref, next_ref, prev_ref, out_ref, own, near, far, pieces, in_sems, out_sems):
@@ -74,6 +78,7 @@
             pltpu.SemaphoreType.DMA((dests,)),
         ],
         cost_estimate=cost(8 * rows * width + 2 * dests * rows * block_cols),
+        compiler_params=vmem(4),
         name="pack",
     )(index, me, grad_parts, from_next, from_prev)
 
@@ -112,84 +117,71 @@
             pltpu.SemaphoreType.DMA((taken,)),
         ],
         cost_estimate=cost((total + taken) * size),
+        compiler_params=vmem(4),
         name="pick",
     )(index, *sources)
 
 
-def precondition_kernel(
-    used_ref, me_ref, own_ref, *refs
-):
-    rel = (own_ref,) + refs[:3]
-    second_ref, left_ref, right_ref, grad_ref, first_out = refs[3:8]
-    rel_out = refs[8:12]
-    grad, left, right, update, in_sems, root_sems, grad_sems, out_sems = refs[12:]
-    slots = left.shape[0]
-    count = second_ref.shape[0]
+def precondition_kernel(chunk_pieces, used_ref, me_ref, *refs):
+    pieces, (left_ref, right_ref, grad_ref) = refs[:chunk_pieces], refs[chunk_pieces : chunk_pieces + 3]
+    outs = refs[chunk_pieces + 3 : 2 * chunk_pieces + 3]
+    grad, left, right, update, in_sems, root_sems, grad_sems, out_sems = refs[2 * chunk_pieces + 3 :]
+    slots, _, _, count = grad.shape[:4]
     block = left.shape[1]
     me = me_ref[0]
-    roots = [
+    loads = [
+        pltpu.make_async_copy(piece, grad.at[:, :, i // count, (me + count - i % count) % count], in_sems.at[i])
+        for i, piece in enumerate(pieces)
+    ] + [
         pltpu.make_async_copy(left_ref, left, root_sems.at[0]),
         pltpu.make_async_copy(right_ref, right, root_sems.at[1]),
     ]
-    loads = [
-        pltpu.make_async_copy(rel[d], grad.at[:, :, 0, (me + count - d) % count], in_sems.at[d]) for d in range(count)
-    ] + [
-        pltpu.make_async_copy(second_ref.at[q], grad.at[:, :, 1, q], in_sems.at[count + q]) for q in range(count)
-    ]
-    for copy in loads + roots:
-        copy.start()
-    for copy in loads + roots:
-        copy.wait()
-    outs = []
+    run_all(loads)
+    stores = []
     for s in range(slots):
         whole = grad[s].reshape(block, block)
         whole = jnp.where(used_ref[s] > 0, whole, jnp.zeros_like(whole))
         grad[s] = whole.reshape(grad.shape[1:])
-        keep = pltpu.make_async_copy(grad.at[s], grad_ref.at[s], grad_sems.at[s])
-        keep.start()
         part = jnp.dot(left[s], whole, preferred_element_type=jnp.float32).astype(whole.dtype)
         result = jnp.dot(part, right[s], preferred_element_type=jnp.float32).astype(whole.dtype)
         update[s] = result.reshape(update.shape[1:])
-        sends = [
-            pltpu.make_async_copy(update.at[s, :, 0, q], first_out.at[q, s], out_sems.at[s, q]) for q in range(count)
-        ] + [
-            pltpu.make_async_copy(update.at[s, :, 1, (me + d) % count], rel_out[d].at[s], out_sems.at[s, count + d])
-            for d in range(count)
+        sends = [pltpu.make_async_copy(grad.at[s], grad_ref.at[s], grad_sems.at[s])] + [
+            pltpu.make_async_copy(update.at[s, :, i // count, (me + i % count) % count], out.at[s], out_sems.at[s, i])
+            for i, out in enumerate(outs)
         ]
         for copy in sends:
             copy.start()
-        outs += sends + [keep]
-    for copy in outs:
+        stores += sends
+    for copy in stores:
         copy.wait()
 
 
-def precondition(used, me, rel, second, root_left, root_right):
-    count = second.shape[0]
-    slots, halves, rows, cols = rel[0].shape
-    dtype = second.dtype
+def precondition(used, me, pieces, root_left, root_right):
+    slots, halves, rows, cols = pieces[0].shape
+    dtype = pieces[0].dtype
     block = root_left.shape[1]
-    piece = jax.ShapeDtypeStruct(rel[0].shape, dtype)
-    layout = (slots, halves, CHUNKS, count, rows, cols)
-    outs = pl.pallas_call(
-        precondition_kernel,
-        out_shape=[jax.ShapeDtypeStruct(layout, dtype), jax.ShapeDtypeStruct(second.shape, dtype)] + [piece] * count,
-        in_specs=[SMEM, SMEM] + [ANY] * (count + 3),
-        out_specs=[ANY] * (count + 2),
+    total = len(pieces)
+    layout = (slots, halves, CHUNKS, total // CHUNKS, rows, cols)
+    grad, *outs = pl.pallas_call(
+        functools.partial(precondition_kernel, total),
+        out_shape=[jax.ShapeDtypeStruct(layout, dtype)] + [jax.ShapeDtypeStruct(pieces[0].shape, dtype)] * total,
+        in_specs=[SMEM, SMEM] + [ANY] * (total + 2),
+        out_specs=[ANY] * (total + 1),
         scratch_shapes=[
             pltpu.VMEM(layout, dtype),
             pltpu.VMEM(root_left.shape, dtype),
             pltpu.VMEM(root_right.shape, dtype),
             pltpu.VMEM(layout, dtype),
-            pltpu.SemaphoreType.DMA((2 * count,)),
+            pltpu.SemaphoreType.DMA((total,)),
             pltpu.SemaphoreType.DMA((2,)),
             pltpu.SemaphoreType.DMA((slots,)),
-            pltpu.SemaphoreType.DMA((slots, 2 * count)),
-        ],
-        compiler_params=pltpu.CompilerParams(vmem_limit_bytes=24 * 1024 * 1024),
+            pltpu.SemaphoreType.DMA((slots, total)),
+        ],
+        compiler_params=vmem(16),
         cost_estimate=cost(10 * slots * block * block, 4 * slots * block**3),
         name="precondition",
-    )(used, me, *rel, second, root_left, root_right)
-    return outs[0].reshape(slots, block, block), outs[1], outs[2:]
+    )(used, me, *pieces, root_left, root_right)
+    return grad.reshape(slots, block, block), outs[: total // CHUNKS], outs[total // CHUNKS :]
 
 
 def unpack_kernel(index_ref, pieces_ref, out_ref, stage, in_sems, out_sem):
@@ -217,6 +209,7 @@
             pltpu.SemaphoreType.DMA,
         ],
         cost_estimate=cost(4 * rows * shape[1]),
+        compiler_params=vmem(4),
         name="unpack",
     )(index, pieces)
 
@@ -244,30 +237,35 @@
         store.wait()
 
 
-def gather_over_replicas(me, own, updates, base, total_rows):
-    quarter, width = own.shape
-    half = quarter // 2
-    from_prev = shift(own, 1)
-    from_next = shift(own, -1)
-    far_first = shift(from_prev[:half], 1)
-    far_second = shift(from_next[half:], -1)
-    operands = [me, own, from_next, from_prev, far_first, far_second]
+def spread(own):
+    return shift(own, -1), shift(own, 1)
+
+
+def spread_far(from_next, from_prev):
+    half = from_prev.shape[0] // 2
+    return shift(from_prev[:half], 1), shift(from_next[half:], -1)
+
+
+def place(me, parts, updates, base, total_rows):
+    quarter, width = parts[0].shape
+    operands = [me, *parts]
     aliases = {}
     if updates is not None:
         aliases = {len(operands): 0}
         operands.append(updates)
     return pl.pallas_call(
         functools.partial(place_kernel, base),
-        out_shape=jax.ShapeDtypeStruct((total_rows, width), own.dtype),
+        out_shape=jax.ShapeDtypeStruct((total_rows, width), parts[0].dtype),
         in_specs=[SMEM] + [ANY] * (len(operands) - 1),
         out_specs=ANY,
         scratch_shapes=[
-            pltpu.VMEM((4 * quarter, width), own.dtype),
+            pltpu.VMEM((4 * quarter, width), parts[0].dtype),
             pltpu.SemaphoreType.DMA((5,)),
             pltpu.SemaphoreType.DMA((5,)),
         ],
         input_output_aliases=aliases,
         cost_estimate=cost(16 * quarter * width),
+        compiler_params=vmem(4),
         name="place",
     )(*operands)
 
@@ -276,8 +274,8 @@
     return lax.all_to_all(x, "expert", split_axis=0, concat_axis=0, tiled=True)
 
 
-def replica_exchange(x):
-    return lax.all_to_all(x, "dp", split_axis=0, concat_axis=0, tiled=True)
+def replica_exchange(parts):
+    return [parts[0]] + [shift(parts[d], d) for d in range(1, len(parts))]
 
 
 def shards(grad_parts, owner_slot, stat_left, stat_right, root_left, root_right):
@@ -319,12 +317,10 @@
         match = (rows[None, :] == row_ids[:, None]) & used[None, :]
         return jnp.sum(jnp.where(match, held[None, :], 0), axis=1)
 
-    order = held // slot_count
-    row_from, used = held_rows(order)
-    row_from_rel, _ = held_rows((my_dp + order) % dp_count)
-    back_from = held_of_row(order)
-    back_from_rel = held_of_row((my_dp + dp_count - order) % dp_count)
-    my_used = lax.dynamic_slice(used.astype(jnp.int32), (my_dp * slot_count,), (slot_count,))
+    ahead = held // slot_count
+    row_from, used = held_rows((my_dp + ahead) % dp_count)
+    back_from = held_of_row((my_dp + dp_count - ahead) % dp_count)
+    my_used = used[:slot_count].astype(jnp.int32)
 
     def part(chunk, offset, down, rows):
         start = chunk * chunk_rows + (my_dp + offset) % dp_count * quarter + down
@@ -335,44 +331,52 @@
         to_next = add(part(chunk, 1, 0, quarter), jnp.pad(from_prev, ((half, 0), (0, 0))))
         return to_prev, to_next
 
-    def relay(first, second):
-        return shift(first, -1), shift(second, 1)
-
     def packed(chunk, to_prev, to_next):
         return pack(chunk * chunk_rows, send_piece, me, grad_parts, shift(to_prev, -1), shift(to_next, 1), block_cols)
 
-    sends = toward(0, *relay(part(0, 2, 0, half), part(0, 2, half, half)))
-    relays, sends = lax.optimization_barrier(((part(1, 2, 0, half), part(1, 2, half, half)), sends))
-    first_packed = packed(0, *sends)
-    sends = toward(1, *relay(*relays))
+    entry = (row_blocks, halves, quarter, block_cols)
+    slots_of = (slot_count,) * dp_count
+
+    def to_owners(incoming):
+        return replica_exchange(pick(row_from, [incoming.reshape(entry)], slots_of))
+
+    def to_rows(column_parts):
+        (rows,) = pick(back_from, column_parts, (row_blocks,))
+        return rows.reshape(expert_count, quarter, block_cols)
+
+    from_next = shift(jnp.concatenate([part(chunk, 2, 0, half) for chunk in range(CHUNKS)]), -1)
+    from_prev = shift(jnp.concatenate([part(chunk, 2, half, half) for chunk in range(CHUNKS)]), 1)
+    first_packed = packed(0, *toward(0, from_next[:half], from_prev[:half]))
+    sends = toward(1, from_next[half:], from_prev[half:])
     sends, first_packed = lax.optimization_barrier((sends, first_packed))
-    entry = (row_blocks, halves, quarter, block_cols)
-    first_in = expert_exchange(first_packed).reshape(entry)
-    second_packed = packed(1, *sends)
-    rel = pick(row_from_rel, [first_in], (slot_count,) * dp_count)
-    rel, second_packed = lax.optimization_barrier((rel, second_packed))
-    rel = [rel[0]] + [shift(rel[d], d) for d in range(1, dp_count)]
-    second_in = expert_exchange(second_packed).reshape(entry)
-    (to_owner,) = pick(row_from, [second_in], (held_count,))
-    second = replica_exchange(to_owner.reshape(dp_count, slot_count, *entry[1:]))
-
-    grad, first_out, rel_out = precondition(my_used, me, rel, second, root_left, root_right)
-
-    first_back = replica_exchange(first_out).reshape(held_count, *entry[1:])
-    (to_rows,) = pick(back_from, [first_back], (row_blocks,))
-    rel_out, to_rows = lax.optimization_barrier((rel_out, to_rows))
-    rel_back = [rel_out[0]] + [shift(rel_out[d], d) for d in range(1, dp_count)]
-    first_own = unpack(my_column, expert_exchange(to_rows.reshape(expert_count, quarter, block_cols)))
-    (to_rows,) = pick(back_from_rel, rel_back, (row_blocks,))
-    first_own, to_rows = lax.optimization_barrier((first_own, to_rows))
-    second_own = unpack(my_column, expert_exchange(to_rows.reshape(expert_count, quarter, block_cols)))
-    updates = gather_over_replicas(me, first_own, None, 0, shard_rows)
-    updates = gather_over_replicas(me, second_own, updates, chunk_rows, shard_rows)
-
+    first_in = expert_exchange(first_packed)
+    second_in = expert_exchange(packed(1, *sends))
+    first_owned = to_owners(first_in)
+    first_owned, second_in = lax.optimization_barrier((first_owned, second_in))
+    second_owned = to_owners(second_in)
+
+    grad, first_out, second_out = precondition(my_used, me, first_owned + second_owned, root_left, root_right)
+
+    first_back = replica_exchange(first_out)
     left_gram = jnp.einsum("sij,skj->sik", grad, grad, preferred_element_type=jnp.float32)
     right_gram = jnp.einsum("sji,sjk->sik", grad, grad, preferred_element_type=jnp.float32)
     new_left = DECAY_RATE * stat_left + (1.0 - DECAY_RATE) * left_gram
     new_right = DECAY_RATE * stat_right + (1.0 - DECAY_RATE) * right_gram
+    first_back, new_left, new_right = lax.optimization_barrier((first_back, new_left, new_right))
+    first_rows = to_rows(first_back)
+    second_out, first_rows = lax.optimization_barrier((second_out, first_rows))
+    first_in, second_back = lax.optimization_barrier((expert_exchange(first_rows), replica_exchange(second_out)))
+    first_own = unpack(my_column, first_in)
+    second_in = expert_exchange(to_rows(second_back))
+
+    near = spread(first_own)
+    far = spread_far(*near)
+    far, second_in = lax.optimization_barrier((far, second_in))
+    second_own = unpack(my_column, second_in)
+    updates = place(me, (first_own, *near, *far), None, 0, shard_rows)
+    near = spread(second_own)
+    near, updates = lax.optimization_barrier((near, updates))
+    updates = place(me, (second_own, *near, *spread_far(*near)), updates, chunk_rows, shard_rows)
     return new_left, new_right, updates
 
 

time: 231 us -> 208 us (0.900)
  blocking collectives: 24.8 us -> 0 us
  waiting for transfers between devices: 80.6 us -> 102 us
  local copies, waits for them, and re-layouts: 14.9 us -> 8.45 us
  Pallas kernels: 33 us -> 27 us
  other arithmetic: 6.66 us -> 2.45 us
    ppermute x22 -> x26, waiting for transfers between devices: 54.9 us -> 95.4 us  [shift(): lax.ppermute(x, 'dp', [(i, (i + step) % count) for i in range(count)])]
    all_to_all x1 -> x0, blocking collectives: 24.8 us -> none  [expert_exchange(): return lax.all_to_all(x, 'expert', split_axis=0, concat_axis=0, tiled=True)]
    all_to_all x2 -> x0, waiting for transfers between devices: 10.7 us -> none  [replica_exchange(): return lax.all_to_all(x, 'dp', split_axis=0, concat_axis=0, tiled=True)]
    all_to_all x3 -> x4, waiting for transfers between devices: 15 us -> 6.29 us  [expert_exchange(): return lax.all_to_all(x, 'expert', split_axis=0, concat_axis=0, tiled=True)]
    all_to_all x2 -> x0, starting transfers between devices: 7.13 us -> none  [replica_exchange(): return lax.all_to_all(x, 'dp', split_axis=0, concat_axis=0, tiled=True)]
    all_to_all x3 -> x4, starting transfers between devices: 18.1 us -> 23.3 us  [expert_exchange(): return lax.all_to_all(x, 'expert', split_axis=0, concat_axis=0, tiled=True)]
    unnamed x60 -> x16, local copies, waits for them, and re-layouts: 11.9 us -> 6.91 us
    pallas_call x2, Pallas kernels: 5.05 us -> 2.25 us  [unpack(): pl.pallas_call(unpack_kernel, out_shape=jax.ShapeDtypeStruct(shape, piece...]
  transfers between devices with their start and end apart: 27 -> 30, of which waited for: 14 -> 20; matrix products, arithmetic and copies ran while one was open for 6% -> 3% of each run, Pallas kernels for 5% -> 4%
where the time goes in v4:
time: 208 us; the launch traced here: 207 us
  waiting for transfers between devices  102 us (49%)
  starting transfers between devices  60.4 us (29%)
  Pallas kernels  27 us (13%)
  local copies, waits for them, and re-layouts  8.45 us (4%)
  matrix products  5.67 us (3%)
  other arithmetic  2.45 us (1%)
    ppermute x26, waiting for transfers between devices, shift(): lax.ppermute(x, 'dp', [(i, (i + step) % count) for i in range(count)])  95.4 us
    ppermute x26, starting transfers between devices, shift(): lax.ppermute(x, 'dp', [(i, (i + step) % count) for i in range(count)])  37.1 us
    all_to_all x4, starting transfers between devices, expert_exchange(): return lax.all_to_all(x, 'expert', split_axis=0, concat_axis=0, tiled=True)  23.3 us
    pallas_call x4, Pallas kernels, pick(): pl.pallas_call(functools.partial(pick_kernel, len(sources)), out_shape=[j...  8.91 us
    unnamed x16, local copies, waits for them, and re-layouts  6.91 us
    all_to_all x4, waiting for transfers between devices, expert_exchange(): return lax.all_to_all(x, 'expert', split_axis=0, concat_axis=0, tiled=True)  6.29 us
    pallas_call x2, Pallas kernels, pack(): pl.pallas_call(functools.partial(pack_kernel, base), out_shape=jax.ShapeD...  5.55 us
    pallas_call x2, Pallas kernels, place(): pl.pallas_call(functools.partial(place_kernel, base), out_shape=jax.Shape...  5.4 us
  transfers between devices with their start and end apart: 30, of which 20 were waited for; matrix products, arithmetic and copies ran while one was open for 3% of the time, Pallas kernels for 4%

profile of v4, /device:TPU:0, one launch (start us, length us, event | category | flops | bytes accessed | tf_op | source)
XLA Modules:
  0.0 206.8 jit_solution(2463034983118166513)
XLA Ops:
  2.1 4.2 %collective-permute-start = (bf16[32,7168]{1,0:T(8,128)(2,1)S(1)}, bf16[32,7168]{1,0:T(8,128)(2,1)S(1)}, u32[]{:S(2)}, u32[]{:S(2)}) collective-permute-start(bf16[32,7168]{1,0:T(8,128)(2,1)S(1)} %pad_maximum_fusion), channel_id=1, source_target_pairs={{0,96},{32,0},{64,32},{96,64},{1,97},{33,1},{65,33},{97,65},{2,98}... | collective-permute-start | bytes 1376264 | tf_op jit(solution)/shard_map/ppermute | solution.py:18
  6.4 9.6 %collective-permute-done = bf16[32,7168]{1,0:T(8,128)(2,1)S(1)} collective-permute-done((bf16[32,7168]{1,0:T(8,128)(2,1)S(1)}, bf16[32,7168]{1,0:T(8,128)(2,1)S(1)}, u32[]{:S(2)}, u32[]{:S(2)}) %collective-permute-start) | collective-permute-done | bytes 458784 | tf_op jit(solution)/shard_map/ppermute | solution.py:18
  16.1 3.5 %collective-permute-done.1 = bf16[32,7168]{1,0:T(8,128)(2,1)S(1)} collective-permute-done((bf16[32,7168]{1,0:T(8,128)(2,1)S(1)}, bf16[32,7168]{1,0:T(8,128)(2,1)S(1)}, u32[]{:S(2)}, u32[]{:S(2)}) %collective-permute-start.1) | collective-permute-done | bytes 458784 | tf_op jit(solution)/shard_map/ppermute | solution.py:18
  21.5 3.2 %collective-permute-start.2 = (bf16[32,7168]{1,0:T(8,128)(2,1)S(1)}, bf16[32,7168]{1,0:T(8,128)(2,1)S(1)}, u32[]{:S(2)}, u32[]{:S(2)}) collective-permute-start(bf16[32,7168]{1,0:T(8,128)(2,1)S(1)} %get-tuple-element.102), channel_id=1, source_target_pairs={{0,96},{32,0},{64,32},{96,64},{1,97},{33,1},{65,33},{97,65},{2,98}... | collective-permute-start | bytes 1376264 | tf_op jit(solution)/shard_map/ppermute | solution.py:18
  24.9 8.9 %collective-permute-done.3.prev_ref = bf16[32,7168]{1,0:T(8,128)(2,1)S(1)} collective-permute-done((bf16[32,7168]{1,0:T(8,128)(2,1)S(1)}, bf16[32,7168]{1,0:T(8,128)(2,1)S(1)}, u32[]{:S(2)}, u32[]{:S(2)}) %collective-permute-start.3) | collective-permute-done | bytes 458784 | tf_op jit(solution)/shard_map/ppermute | solution.py:18
  38.5 7.3 %all-to-all-start = ((bf16[32,32,512]{2,1,0:T(8,128)(2,1)}), bf16[32,32,512]{2,1,0:T(8,128)(2,1)S(1)}, u32[]{:S(2)}, u32[]{:S(2)}) async-start(bf16[32,32,512]{2,1,0:T(8,128)(2,1)} %pack.2), calls=%async_computation | async-start | bytes 2097152 | tf_op jit(solution)/shard_map/all_to_all | solution.py:274
  45.9 3.0 %collective-permute-start.7 = (bf16[32,7168]{1,0:T(8,128)(2,1)S(1)}, bf16[32,7168]{1,0:T(8,128)(2,1)S(1)}, u32[]{:S(2)}, u32[]{:S(2)}) collective-permute-start(bf16[32,7168]{1,0:T(8,128)(2,1)S(1)} %get-tuple-element.55), channel_id=1, source_target_pairs={{0,96},{32,0},{64,32},{96,64},{1,97},{33,1},{65,33},{97,65},{2,98}... | collective-permute-start | bytes 1376264 | tf_op jit(solution)/shard_map/ppermute | solution.py:18
  48.9 10.2 %collective-permute-done.7.next_ref = bf16[32,7168]{1,0:T(8,128)(2,1)S(1)} collective-permute-done((bf16[32,7168]{1,0:T(8,128)(2,1)S(1)}, bf16[32,7168]{1,0:T(8,128)(2,1)S(1)}, u32[]{:S(2)}, u32[]{:S(2)}) %collective-permute-start.7) | collective-permute-done | bytes 458784 | tf_op jit(solution)/shard_map/ppermute | solution.py:18
  59.1 3.4 %collective-permute-done.8.prev_ref = bf16[32,7168]{1,0:T(8,128)(2,1)S(1)} collective-permute-done((bf16[32,7168]{1,0:T(8,128)(2,1)S(1)}, bf16[32,7168]{1,0:T(8,128)(2,1)S(1)}, u32[]{:S(2)}, u32[]{:S(2)}) %collective-permute-start.8) | collective-permute-done | bytes 458784 | tf_op jit(solution)/shard_map/ppermute | solution.py:18
  64.6 2.8 %pack.3 = bf16[32,32,512]{2,1,0:T(8,128)(2,1)} custom-call(s32[32]{0:T(128)S(1)} %select_reduce_fusion.1.index_ref, s32[1]{0:T(128)} %bitcast.me_ref, bf16[1,256,7168]{2,1,0:T(8,128)(2,1)S(1)} %copy-done.1, bf16[32,7168]{1,0:T(8,128)(2,1)S(1)} %collective-permute-done.7.next_ref, bf16[32,7168]{1,0:T(8,128)(2,1)S(1)} %collective-permute-done.8.prev_ref), custom_call_target="tpu_custom_call" | custom-call | bytes 2883584 | tf_op jit(solution)/shard_map/pack/pallas_call | solution.py:69
  67.4 7.3 %all-to-all-start.1 = ((bf16[32,32,512]{2,1,0:T(8,128)(2,1)}), bf16[32,32,512]{2,1,0:T(8,128)(2,1)S(1)}, u32[]{:S(2)}, u32[]{:S(2)}) async-start(bf16[32,32,512]{2,1,0:T(8,128)(2,1)} %pack.3), calls=%async_computation.1 | async-start | bytes 2097152 | tf_op jit(solution)/shard_map/all_to_all | solution.py:274
  80.3 9.0 %collective-permute-done.4.refs_1_ = bf16[3,2,32,512]{3,2,1,0:T(8,128)(2,1)S(1)} collective-permute-done((bf16[3,2,32,512]{3,2,1,0:T(8,128)(2,1)S(1)}, bf16[3,2,32,512]{3,2,1,0:T(8,128)(2,1)S(1)}, u32[]{:S(2)}, u32[]{:S(2)}) %collective-permute-start.4) | collective-permute-done | bytes 196640 | tf_op jit(solution)/shard_map/ppermute | solution.py:18
  97.1 9.1 %collective-permute-done.9.refs_5_ = bf16[3,2,32,512]{3,2,1,0:T(8,128)(2,1)S(1)} collective-permute-done((bf16[3,2,32,512]{3,2,1,0:T(8,128)(2,1)S(1)}, bf16[3,2,32,512]{3,2,1,0:T(8,128)(2,1)S(1)}, u32[]{:S(2)}, u32[]{:S(2)}) %collective-permute-start.9) | collective-permute-done | bytes 196640 | tf_op jit(solution)/shard_map/ppermute | solution.py:18
  109.6 4.9 %precondition.1 = (bf16[3,2,2,4,32,512]{5,4,3,2,1,0:T(8,128)(2,1)S(1)}, bf16[3,2,32,512]{3,2,1,0:T(8,128)(2,1)S(1)}, bf16[3,2,32,512]{3,2,1,0:T(8,128)(2,1)S(1)}...) custom-call(s32[3]{0:T(128)S(1)} %slice_convert_fusion.used_ref, ...), custom_call_target="tpu_custom_call" | custom-call | flops 1610612736 | bytes 7864320 | tf_op jit(solution)/shard_map/precondition/pallas_call | solution.py:165
  114.8 3.6 %collective-permute-start.13 = (bf16[3,2,32,512]{3,2,1,0:T(8,128)(2,1)S(1)}, bf16[3,2,32,512]{3,2,1,0:T(8,128)(2,1)S(1)}, u32[]{:S(2)}, u32[]{:S(2)}) collective-permute-start(bf16[3,2,32,512]{3,2,1,0:T(8,128)(2,1)S(1)} %get-tuple-element.68), channel_id=1, source_target_pairs={{0,64},{32,96},{64,0},{96,32},{1,65},{33,97},{65,1},{97,33},{2,66}... | collective-permute-start | bytes 589832 | tf_op jit(solution)/shard_map/ppermute | solution.py:18
  118.4 2.9 %multiply_add_fusion = f32[3,512,512]{2,1,0:T(8,128)} fusion(f32[3,512,512]{2,1,0:T(8,128)S(1)} %copy-done.4, bf16[3,512,512]{2,1,0:T(8,128)(2,1)S(1)} %bitcast.30), kind=kOutput, calls=%fused_computation | convolution fusion | flops 807665664 | bytes 7864320 | tf_op jit(solution)/shard_map/sji,sjk->sik/dot_general | solution.py:362
  121.3 2.8 %multiply_add_fusion.1 = f32[3,512,512]{2,1,0:T(8,128)} fusion(f32[3,512,512]{2,1,0:T(8,128)S(1)} %copy-done.5, bf16[3,512,512]{2,1,0:T(8,128)(2,1)S(1)} %bitcast.31), kind=kOutput, calls=%fused_computation.1 | convolution fusion | flops 807665664 | bytes 7864320 | tf_op jit(solution)/shard_map/sij,skj->sik/dot_general | solution.py:361
  124.1 3.0 %collective-permute-done.13.refs_2_ = bf16[3,2,32,512]{3,2,1,0:T(8,128)(2,1)S(1)} collective-permute-done((bf16[3,2,32,512]{3,2,1,0:T(8,128)(2,1)S(1)}, bf16[3,2,32,512]{3,2,1,0:T(8,128)(2,1)S(1)}, u32[]{:S(2)}, u32[]{:S(2)}) %collective-permute-start.13) | collective-permute-done | bytes 196640 | tf_op jit(solution)/shard_map/ppermute | solution.py:18
  129.8 4.8 %all-to-all-start.2 = ((bf16[32,32,512]{2,1,0:T(8,128)(2,1)}), bf16[32,32,512]{2,1,0:T(8,128)(2,1)S(1)}, u32[]{:S(2)}, u32[]{:S(2)}) async-start(bf16[32,32,512]{2,1,0:T(8,128)(2,1)} %bitcast.12), calls=%async_computation.2 | async-start | bytes 2097152 | tf_op jit(solution)/shard_map/all_to_all | solution.py:274
  134.8 3.4 %collective-permute-start.16 = (bf16[3,2,32,512]{3,2,1,0:T(8,128)(2,1)S(1)}, bf16[3,2,32,512]{3,2,1,0:T(8,128)(2,1)S(1)}, u32[]{:S(2)}, u32[]{:S(2)}) collective-permute-start(bf16[3,2,32,512]{3,2,1,0:T(8,128)(2,1)S(1)} %get-tuple-element.84), channel_id=1, source_target_pairs={{0,64},{32,96},{64,0},{96,32},{1,65},{33,97},{65,1},{97,33},{2,66}... | collective-permute-start | bytes 589832 | tf_op jit(solution)/shard_map/ppermute | solution.py:18
  138.2 4.9 %collective-permute-done.15.refs_1_ = bf16[3,2,32,512]{3,2,1,0:T(8,128)(2,1)S(1)} collective-permute-done((bf16[3,2,32,512]{3,2,1,0:T(8,128)(2,1)S(1)}, bf16[3,2,32,512]{3,2,1,0:T(8,128)(2,1)S(1)}, u32[]{:S(2)}, u32[]{:S(2)}) %collective-permute-start.15) | collective-permute-done | bytes 196640 | tf_op jit(solution)/shard_map/ppermute | solution.py:18
  143.2 4.3 %collective-permute-done.16.refs_2_ = bf16[3,2,32,512]{3,2,1,0:T(8,128)(2,1)S(1)} collective-permute-done((bf16[3,2,32,512]{3,2,1,0:T(8,128)(2,1)S(1)}, bf16[3,2,32,512]{3,2,1,0:T(8,128)(2,1)S(1)}, u32[]{:S(2)}, u32[]{:S(2)}) %collective-permute-start.16) | collective-permute-done | bytes 196640 | tf_op jit(solution)/shard_map/ppermute | solution.py:18
  147.7 4.1 %all-to-all-done.2.pieces_ref = bf16[32,32,512]{2,1,0:T(8,128)(2,1)S(1)} async-done(((bf16[32,32,512]{2,1,0:T(8,128)(2,1)}), bf16[32,32,512]{2,1,0:T(8,128)(2,1)S(1)}, u32[]{:S(2)}, u32[]{:S(2)}) %all-to-all-start.2) | async-done | bytes 1048608 | tf_op jit(solution)/shard_map/all_to_all | solution.py:274
  154.6 3.9 %all-to-all-start.3 = ((bf16[32,32,512]{2,1,0:T(8,128)(2,1)}), bf16[32,32,512]{2,1,0:T(8,128)(2,1)S(1)}, u32[]{:S(2)}, u32[]{:S(2)}) async-start(bf16[32,32,512]{2,1,0:T(8,128)(2,1)} %bitcast.13), calls=%async_computation.3 | async-start | bytes 2097152 | tf_op jit(solution)/shard_map/all_to_all | solution.py:274
  161.9 10.4 %collective-permute-done.20.refs_1_ = bf16[32,7168]{1,0:T(8,128)(2,1)S(1)} collective-permute-done((bf16[32,7168]{1,0:T(8,128)(2,1)S(1)}, bf16[32,7168]{1,0:T(8,128)(2,1)S(1)}, u32[]{:S(2)}, u32[]{:S(2)}) %collective-permute-start.20) | collective-permute-done | bytes 458784 | tf_op jit(solution)/shard_map/ppermute | solution.py:18
  172.3 3.4 %collective-permute-start.21 = (bf16[16,7168]{1,0:T(8,128)(2,1)S(1)}, bf16[16,7168]{1,0:T(8,128)(2,1)S(1)}, u32[]{:S(2)}, u32[]{:S(2)}) collective-permute-start(bf16[16,7168]{1,0:T(8,128)(2,1)S(1)} %slice.38), channel_id=1, source_target_pairs={{0,96},{32,0},{64,32},{96,64},{1,97},{33,1},{65,33},{97,65},{2,98}... | collective-permute-start | bytes 688136 | tf_op jit(solution)/shard_map/ppermute | solution.py:18
  175.9 4.3 %collective-permute-done.21.refs_4_ = bf16[16,7168]{1,0:T(8,128)(2,1)S(1)} collective-permute-done((bf16[16,7168]{1,0:T(8,128)(2,1)S(1)}, bf16[16,7168]{1,0:T(8,128)(2,1)S(1)}, u32[]{:S(2)}, u32[]{:S(2)}) %collective-permute-start.21) | collective-permute-done | bytes 229408 | tf_op jit(solution)/shard_map/ppermute | solution.py:18
  180.1 3.5 %collective-permute-done.19.refs_3_ = bf16[16,7168]{1,0:T(8,128)(2,1)S(1)} collective-permute-done((bf16[16,7168]{1,0:T(8,128)(2,1)S(1)}, bf16[16,7168]{1,0:T(8,128)(2,1)S(1)}, u32[]{:S(2)}, u32[]{:S(2)}) %collective-permute-start.19) | collective-permute-done | bytes 229408 | tf_op jit(solution)/shard_map/ppermute | solution.py:18
  184.8 3.2 %collective-permute-start.22 = (bf16[32,7168]{1,0:T(8,128)(2,1)S(1)}, bf16[32,7168]{1,0:T(8,128)(2,1)S(1)}, u32[]{:S(2)}, u32[]{:S(2)}) collective-permute-start(bf16[32,7168]{1,0:T(8,128)(2,1)S(1)} %unpack.3.refs_0_), channel_id=1, source_target_pairs={{0,96},{32,0},{64,32},{96,64},{1,97},{33,1},{65,33},{97,65},{2,98}... | collective-permute-start | bytes 1376264 | tf_op jit(solution)/shard_map/ppermute | solution.py:18
  190.8 5.8 %collective-permute-done.23.refs_2_ = bf16[32,7168]{1,0:T(8,128)(2,1)S(1)} collective-permute-done((bf16[32,7168]{1,0:T(8,128)(2,1)S(1)}, bf16[32,7168]{1,0:T(8,128)(2,1)S(1)}, u32[]{:S(2)}, u32[]{:S(2)}) %collective-permute-start.23) | collective-permute-done | bytes 458784 | tf_op jit(solution)/shard_map/ppermute | solution.py:18
  196.7 3.2 %collective-permute-start.25 = (bf16[16,7168]{1,0:T(8,128)(2,1)S(1)}, bf16[16,7168]{1,0:T(8,128)(2,1)S(1)}, u32[]{:S(2)}, u32[]{:S(2)}) collective-permute-start(bf16[16,7168]{1,0:T(8,128)(2,1)S(1)} %slice.33), channel_id=1, source_target_pairs={{0,96},{32,0},{64,32},{96,64},{1,97},{33,1},{65,33},{97,65},{2,98}... | collective-permute-start | bytes 688136 | tf_op jit(solution)/shard_map/ppermute | solution.py:18
  199.9 4.0 %collective-permute-done.24.refs_3_ = bf16[16,7168]{1,0:T(8,128)(2,1)S(1)} collective-permute-done((bf16[16,7168]{1,0:T(8,128)(2,1)S(1)}, bf16[16,7168]{1,0:T(8,128)(2,1)S(1)}, u32[]{:S(2)}, u32[]{:S(2)}) %collective-permute-start.24) | collective-permute-done | bytes 229408 | tf_op jit(solution)/shard_map/ppermute | solution.py:18
  (75 shorter events, 43.7 us)
Async XLA Ops:
  0.6 19.0 %copy-start.7 = (pred[32]{0:T(512)(128)(4,1)S(1)}, pred[32]{0:T(512)(128)(4,1)}, u32[]{:S(2)}) copy-start(pred[32]{0:T(512)(128)(4,1)} %constant.141.clone.1) | copy-start | bytes 100
  2.1 14.0 %collective-permute-start = (bf16[32,7168]{1,0:T(8,128)(2,1)S(1)}, bf16[32,7168]{1,0:T(8,128)(2,1)S(1)}, u32[]{:S(2)}, u32[]{:S(2)}) collective-permute-start(bf16[32,7168]{1,0:T(8,128)(2,1)S(1)} %pad_maximum_fusion), channel_id=1, source_target_pairs={{0,96},{32,0},{64,32},{96,64},{1,97},{33,1},{65,33},{97,65},{2,98}... | collective-permute-start | bytes 1376264 | tf_op jit(solution)/shard_map/ppermute | solution.py:18
  6.3 13.3 %collective-permute-start.1 = (bf16[32,7168]{1,0:T(8,128)(2,1)S(1)}, bf16[32,7168]{1,0:T(8,128)(2,1)S(1)}, u32[]{:S(2)}, u32[]{:S(2)}) collective-permute-start(bf16[32,7168]{1,0:T(8,128)(2,1)S(1)} %pad_maximum_fusion.1), channel_id=1, source_target_pairs={{0,32},{32,64},{64,96},{96,0},{1,33},{33,65},{65,97},{97,1},{2,34}... | collective-permute-start | bytes 1376264 | tf_op jit(solution)/shard_map/ppermute | solution.py:18
  6.4 18.3 %copy-start.6 = (s32[224]{0:T(256)S(1)}, s32[224]{0:T(256)}, u32[]{:S(2)}) copy-start(s32[224]{0:T(256)} %param.7) | copy-start | bytes 2692
  21.4 12.3 %collective-permute-start.3 = (bf16[32,7168]{1,0:T(8,128)(2,1)S(1)}, bf16[32,7168]{1,0:T(8,128)(2,1)S(1)}, u32[]{:S(2)}, u32[]{:S(2)}) collective-permute-start(bf16[32,7168]{1,0:T(8,128)(2,1)S(1)} %get-tuple-element.101), channel_id=1, source_target_pairs={{0,32},{32,64},{64,96},{96,0},{1,33},{33,65},{65,97},{97,1},{2,34}... | collective-permute-start | bytes 1376264 | tf_op jit(solution)/shard_map/ppermute | solution.py:18
  21.5 12.3 %collective-permute-start.2 = (bf16[32,7168]{1,0:T(8,128)(2,1)S(1)}, bf16[32,7168]{1,0:T(8,128)(2,1)S(1)}, u32[]{:S(2)}, u32[]{:S(2)}) collective-permute-start(bf16[32,7168]{1,0:T(8,128)(2,1)S(1)} %get-tuple-element.102), channel_id=1, source_target_pairs={{0,96},{32,0},{64,32},{96,64},{1,97},{33,1},{65,33},{97,65},{2,98}... | collective-permute-start | bytes 1376264 | tf_op jit(solution)/shard_map/ppermute | solution.py:18
  38.5 28.8 %all-to-all-start = ((bf16[32,32,512]{2,1,0:T(8,128)(2,1)}), bf16[32,32,512]{2,1,0:T(8,128)(2,1)S(1)}, u32[]{:S(2)}, u32[]{:S(2)}) async-start(bf16[32,32,512]{2,1,0:T(8,128)(2,1)} %pack.2), calls=%async_computation | async-start | bytes 2097152 | tf_op jit(solution)/shard_map/all_to_all | solution.py:274
  45.9 13.2 %collective-permute-start.7 = (bf16[32,7168]{1,0:T(8,128)(2,1)S(1)}, bf16[32,7168]{1,0:T(8,128)(2,1)S(1)}, u32[]{:S(2)}, u32[]{:S(2)}) collective-permute-start(bf16[32,7168]{1,0:T(8,128)(2,1)S(1)} %get-tuple-element.55), channel_id=1, source_target_pairs={{0,96},{32,0},{64,32},{96,64},{1,97},{33,1},{65,33},{97,65},{2,98}... | collective-permute-start | bytes 1376264 | tf_op jit(solution)/shard_map/ppermute | solution.py:18
  48.9 13.6 %collective-permute-start.8 = (bf16[32,7168]{1,0:T(8,128)(2,1)S(1)}, bf16[32,7168]{1,0:T(8,128)(2,1)S(1)}, u32[]{:S(2)}, u32[]{:S(2)}) collective-permute-start(bf16[32,7168]{1,0:T(8,128)(2,1)S(1)} %get-tuple-element.56), channel_id=1, source_target_pairs={{0,32},{32,64},{64,96},{96,0},{1,33},{33,65},{65,97},{97,1},{2,34}... | collective-permute-start | bytes 1376264 | tf_op jit(solution)/shard_map/ppermute | solution.py:18
  67.4 24.6 %all-to-all-start.1 = ((bf16[32,32,512]{2,1,0:T(8,128)(2,1)}), bf16[32,32,512]{2,1,0:T(8,128)(2,1)S(1)}, u32[]{:S(2)}, u32[]{:S(2)}) async-start(bf16[32,32,512]{2,1,0:T(8,128)(2,1)} %pack.3), calls=%async_computation.1 | async-start | bytes 2097152 | tf_op jit(solution)/shard_map/all_to_all | solution.py:274
  76.6 12.6 %collective-permute-start.4 = (bf16[3,2,32,512]{3,2,1,0:T(8,128)(2,1)S(1)}, bf16[3,2,32,512]{3,2,1,0:T(8,128)(2,1)S(1)}, u32[]{:S(2)}, u32[]{:S(2)}) collective-permute-start(bf16[3,2,32,512]{3,2,1,0:T(8,128)(2,1)S(1)} %get-tuple-element.52), channel_id=1, source_target_pairs={{0,32},{32,64},{64,96},{96,0},{1,33},{33,65},{65,97},{97,1},{2,34}... | collective-permute-start | bytes 589832 | tf_op jit(solution)/shard_map/ppermute | solution.py:18
  76.7 12.5 %collective-permute-start.5 = (bf16[3,2,32,512]{3,2,1,0:T(8,128)(2,1)S(1)}, bf16[3,2,32,512]{3,2,1,0:T(8,128)(2,1)S(1)}, u32[]{:S(2)}, u32[]{:S(2)}) collective-permute-start(bf16[3,2,32,512]{3,2,1,0:T(8,128)(2,1)S(1)} %get-tuple-element.53), channel_id=1, source_target_pairs={{0,64},{32,96},{64,0},{96,32},{1,65},{33,97},{65,1},{97,33},{2,66}... | collective-permute-start | bytes 589832 | tf_op jit(solution)/shard_map/ppermute | solution.py:18
  78.5 11.4 %collective-permute-start.6 = (bf16[3,2,32,512]{3,2,1,0:T(8,128)(2,1)S(1)}, bf16[3,2,32,512]{3,2,1,0:T(8,128)(2,1)S(1)}, u32[]{:S(2)}, u32[]{:S(2)}) collective-permute-start(bf16[3,2,32,512]{3,2,1,0:T(8,128)(2,1)S(1)} %get-tuple-element.54), channel_id=1, source_target_pairs={{0,96},{32,0},{64,32},{96,64},{1,97},{33,1},{65,33},{97,65},{2,98}... | collective-permute-start | bytes 589832 | tf_op jit(solution)/shard_map/ppermute | solution.py:18
  93.8 12.4 %collective-permute-start.9 = (bf16[3,2,32,512]{3,2,1,0:T(8,128)(2,1)S(1)}, bf16[3,2,32,512]{3,2,1,0:T(8,128)(2,1)S(1)}, u32[]{:S(2)}, u32[]{:S(2)}) collective-permute-start(bf16[3,2,32,512]{3,2,1,0:T(8,128)(2,1)S(1)} %get-tuple-element.63), channel_id=1, source_target_pairs={{0,32},{32,64},{64,96},{96,0},{1,33},{33,65},{65,97},{97,1},{2,34}... | collective-permute-start | bytes 589832 | tf_op jit(solution)/shard_map/ppermute | solution.py:18
  93.8 12.3 %collective-permute-start.10 = (bf16[3,2,32,512]{3,2,1,0:T(8,128)(2,1)S(1)}, bf16[3,2,32,512]{3,2,1,0:T(8,128)(2,1)S(1)}, u32[]{:S(2)}, u32[]{:S(2)}) collective-permute-start(bf16[3,2,32,512]{3,2,1,0:T(8,128)(2,1)S(1)} %get-tuple-element.64), channel_id=1, source_target_pairs={{0,64},{32,96},{64,0},{96,32},{1,65},{33,97},{65,1},{97,33},{2,66}... | collective-permute-start | bytes 589832 | tf_op jit(solution)/shard_map/ppermute | solution.py:18
  95.6 11.2 %collective-permute-start.11 = (bf16[3,2,32,512]{3,2,1,0:T(8,128)(2,1)S(1)}, bf16[3,2,32,512]{3,2,1,0:T(8,128)(2,1)S(1)}, u32[]{:S(2)}, u32[]{:S(2)}) collective-permute-start(bf16[3,2,32,512]{3,2,1,0:T(8,128)(2,1)S(1)} %get-tuple-element.65), channel_id=1, source_target_pairs={{0,96},{32,0},{64,32},{96,64},{1,97},{33,1},{65,33},{97,65},{2,98}... | collective-permute-start | bytes 589832 | tf_op jit(solution)/shard_map/ppermute | solution.py:18
  114.5 9.6 %collective-permute-start.12 = (bf16[3,2,32,512]{3,2,1,0:T(8,128)(2,1)S(1)}, bf16[3,2,32,512]{3,2,1,0:T(8,128)(2,1)S(1)}, u32[]{:S(2)}, u32[]{:S(2)}) collective-permute-start(bf16[3,2,32,512]{3,2,1,0:T(8,128)(2,1)S(1)} %get-tuple-element.67), channel_id=1, source_target_pairs={{0,32},{32,64},{64,96},{96,0},{1,33},{33,65},{65,97},{97,1},{2,34}... | collective-permute-start | bytes 589832 | tf_op jit(solution)/shard_map/ppermute | solution.py:18
  114.8 12.3 %collective-permute-start.13 = (bf16[3,2,32,512]{3,2,1,0:T(8,128)(2,1)S(1)}, bf16[3,2,32,512]{3,2,1,0:T(8,128)(2,1)S(1)}, u32[]{:S(2)}, u32[]{:S(2)}) collective-permute-start(bf16[3,2,32,512]{3,2,1,0:T(8,128)(2,1)S(1)} %get-tuple-element.68), channel_id=1, source_target_pairs={{0,64},{32,96},{64,0},{96,32},{1,65},{33,97},{65,1},{97,33},{2,66}... | collective-permute-start | bytes 589832 | tf_op jit(solution)/shard_map/ppermute | solution.py:18
  118.4 8.7 %collective-permute-start.14 = (bf16[3,2,32,512]{3,2,1,0:T(8,128)(2,1)S(1)}, bf16[3,2,32,512]{3,2,1,0:T(8,128)(2,1)S(1)}, u32[]{:S(2)}, u32[]{:S(2)}) collective-permute-start(bf16[3,2,32,512]{3,2,1,0:T(8,128)(2,1)S(1)} %get-tuple-element.69), channel_id=1, source_target_pairs={{0,96},{32,0},{64,32},{96,64},{1,97},{33,1},{65,33},{97,65},{2,98}... | collective-permute-start | bytes 589832 | tf_op jit(solution)/shard_map/ppermute | solution.py:18
  129.8 22.1 %all-to-all-start.2 = ((bf16[32,32,512]{2,1,0:T(8,128)(2,1)}), bf16[32,32,512]{2,1,0:T(8,128)(2,1)S(1)}, u32[]{:S(2)}, u32[]{:S(2)}) async-start(bf16[32,32,512]{2,1,0:T(8,128)(2,1)} %bitcast.12), calls=%async_computation.2 | async-start | bytes 2097152 | tf_op jit(solution)/shard_map/all_to_all | solution.py:274
  134.5 8.6 %collective-permute-start.15 = (bf16[3,2,32,512]{3,2,1,0:T(8,128)(2,1)S(1)}, bf16[3,2,32,512]{3,2,1,0:T(8,128)(2,1)S(1)}, u32[]{:S(2)}, u32[]{:S(2)}) collective-permute-start(bf16[3,2,32,512]{3,2,1,0:T(8,128)(2,1)S(1)} %get-tuple-element.83), channel_id=1, source_target_pairs={{0,32},{32,64},{64,96},{96,0},{1,33},{33,65},{65,97},{97,1},{2,34}... | collective-permute-start | bytes 589832 | tf_op jit(solution)/shard_map/ppermute | solution.py:18
  134.8 12.7 %collective-permute-start.16 = (bf16[3,2,32,512]{3,2,1,0:T(8,128)(2,1)S(1)}, bf16[3,2,32,512]{3,2,1,0:T(8,128)(2,1)S(1)}, u32[]{:S(2)}, u32[]{:S(2)}) collective-permute-start(bf16[3,2,32,512]{3,2,1,0:T(8,128)(2,1)S(1)} %get-tuple-element.84), channel_id=1, source_target_pairs={{0,64},{32,96},{64,0},{96,32},{1,65},{33,97},{65,1},{97,33},{2,66}... | collective-permute-start | bytes 589832 | tf_op jit(solution)/shard_map/ppermute | solution.py:18
  138.2 9.5 %collective-permute-start.17 = (bf16[3,2,32,512]{3,2,1,0:T(8,128)(2,1)S(1)}, bf16[3,2,32,512]{3,2,1,0:T(8,128)(2,1)S(1)}, u32[]{:S(2)}, u32[]{:S(2)}) collective-permute-start(bf16[3,2,32,512]{3,2,1,0:T(8,128)(2,1)S(1)} %get-tuple-element.85), channel_id=1, source_target_pairs={{0,96},{32,0},{64,32},{96,64},{1,97},{33,1},{65,33},{97,65},{2,98}... | collective-permute-start | bytes 589832 | tf_op jit(solution)/shard_map/ppermute | solution.py:18
  154.6 29.1 %all-to-all-start.3 = ((bf16[32,32,512]{2,1,0:T(8,128)(2,1)}), bf16[32,32,512]{2,1,0:T(8,128)(2,1)S(1)}, u32[]{:S(2)}, u32[]{:S(2)}) async-start(bf16[32,32,512]{2,1,0:T(8,128)(2,1)} %bitcast.13), calls=%async_computation.3 | async-start | bytes 2097152 | tf_op jit(solution)/shard_map/all_to_all | solution.py:274
  159.7 12.7 %collective-permute-start.20 = (bf16[32,7168]{1,0:T(8,128)(2,1)S(1)}, bf16[32,7168]{1,0:T(8,128)(2,1)S(1)}, u32[]{:S(2)}, u32[]{:S(2)}) collective-permute-start(bf16[32,7168]{1,0:T(8,128)(2,1)S(1)} %unpack.2.refs_0_), channel_id=1, source_target_pairs={{0,96},{32,0},{64,32},{96,64},{1,97},{33,1},{65,33},{97,65},{2,98}... | collective-permute-start | bytes 1376264 | tf_op jit(solution)/shard_map/ppermute | solution.py:18
  161.9 13.9 %collective-permute-start.18 = (bf16[32,7168]{1,0:T(8,128)(2,1)S(1)}, bf16[32,7168]{1,0:T(8,128)(2,1)S(1)}, u32[]{:S(2)}, u32[]{:S(2)}) collective-permute-start(bf16[32,7168]{1,0:T(8,128)(2,1)S(1)} %unpack.2.refs_0_), channel_id=1, source_target_pairs={{0,32},{32,64},{64,96},{96,0},{1,33},{33,65},{65,97},{97,1},{2,34}... | collective-permute-start | bytes 1376264 | tf_op jit(solution)/shard_map/ppermute | solution.py:18
  172.3 7.8 %collective-permute-start.21 = (bf16[16,7168]{1,0:T(8,128)(2,1)S(1)}, bf16[16,7168]{1,0:T(8,128)(2,1)S(1)}, u32[]{:S(2)}, u32[]{:S(2)}) collective-permute-start(bf16[16,7168]{1,0:T(8,128)(2,1)S(1)} %slice.38), channel_id=1, source_target_pairs={{0,96},{32,0},{64,32},{96,64},{1,97},{33,1},{65,33},{97,65},{2,98}... | collective-permute-start | bytes 688136 | tf_op jit(solution)/shard_map/ppermute | solution.py:18
  175.8 7.8 %collective-permute-start.19 = (bf16[16,7168]{1,0:T(8,128)(2,1)S(1)}, bf16[16,7168]{1,0:T(8,128)(2,1)S(1)}, u32[]{:S(2)}, u32[]{:S(2)}) collective-permute-start(bf16[16,7168]{1,0:T(8,128)(2,1)S(1)} %slice.37), channel_id=1, source_target_pairs={{0,32},{32,64},{64,96},{96,0},{1,33},{33,65},{65,97},{97,1},{2,34}... | collective-permute-start | bytes 688136 | tf_op jit(solution)/shard_map/ppermute | solution.py:18
  184.8 11.8 %collective-permute-start.23 = (bf16[32,7168]{1,0:T(8,128)(2,1)S(1)}, bf16[32,7168]{1,0:T(8,128)(2,1)S(1)}, u32[]{:S(2)}, u32[]{:S(2)}) collective-permute-start(bf16[32,7168]{1,0:T(8,128)(2,1)S(1)} %unpack.3.refs_0_), channel_id=1, source_target_pairs={{0,32},{32,64},{64,96},{96,0},{1,33},{33,65},{65,97},{97,1},{2,34}... | collective-permute-start | bytes 1376264 | tf_op jit(solution)/shard_map/ppermute | solution.py:18
  184.8 11.8 %collective-permute-start.22 = (bf16[32,7168]{1,0:T(8,128)(2,1)S(1)}, bf16[32,7168]{1,0:T(8,128)(2,1)S(1)}, u32[]{:S(2)}, u32[]{:S(2)}) collective-permute-start(bf16[32,7168]{1,0:T(8,128)(2,1)S(1)} %unpack.3.refs_0_), channel_id=1, source_target_pairs={{0,96},{32,0},{64,32},{96,64},{1,97},{33,1},{65,33},{97,65},{2,98}... | collective-permute-start | bytes 1376264 | tf_op jit(solution)/shard_map/ppermute | solution.py:18
  196.6 7.3 %collective-permute-start.24 = (bf16[16,7168]{1,0:T(8,128)(2,1)S(1)}, bf16[16,7168]{1,0:T(8,128)(2,1)S(1)}, u32[]{:S(2)}, u32[]{:S(2)}) collective-permute-start(bf16[16,7168]{1,0:T(8,128)(2,1)S(1)} %slice.32), channel_id=1, source_target_pairs={{0,32},{32,64},{64,96},{96,0},{1,33},{33,65},{65,97},{97,1},{2,34}... | collective-permute-start | bytes 688136 | tf_op jit(solution)/shard_map/ppermute | solution.py:18
  196.7 7.2 %collective-permute-start.25 = (bf16[16,7168]{1,0:T(8,128)(2,1)S(1)}, bf16[16,7168]{1,0:T(8,128)(2,1)S(1)}, u32[]{:S(2)}, u32[]{:S(2)}) collective-permute-start(bf16[16,7168]{1,0:T(8,128)(2,1)S(1)} %slice.33), channel_id=1, source_target_pairs={{0,96},{32,0},{64,32},{96,64},{1,97},{33,1},{65,33},{97,65},{2,98}... | collective-permute-start | bytes 688136 | tf_op jit(solution)/shard_map/ppermute | solution.py:18
  (6 other events, 18.6 us)

commit v5 on v4

--- a/solution.py
+++ b/solution.py
@@ -11,6 +11,7 @@
 CHUNKS = 2
 ANY = pl.BlockSpec(memory_space=pl.ANY)
 SMEM = pl.BlockSpec(memory_space=pltpu.SMEM)
+HBM = pl.BlockSpec(memory_space=pltpu.HBM)
 
 
 def shift(x, step):
@@ -40,13 +41,11 @@
     return pltpu.CompilerParams(vmem_limit_bytes=mebibytes * 1024 * 1024)
 
 
-def pack_kernel(base, index_ref, me_ref, grad_ref, next_ref, prev_ref, out_ref, own, near, far, pieces, in_sems, out_sems):
-    rows = own.shape[0]
+def pack_kernel(index_ref, own_ref, next_ref, prev_ref, out_ref, own, near, far, pieces, in_sems, out_sems):
     wide_count, _, block_cols = pieces.shape
-    start = pl.multiple_of(base + me_ref[0] * rows, rows)
     run_all(
         [
-            pltpu.make_async_copy(grad_ref.at[0, pl.ds(start, rows)], own, in_sems.at[0]),
+            pltpu.make_async_copy(own_ref, own, in_sems.at[0]),
             pltpu.make_async_copy(next_ref, near, in_sems.at[1]),
             pltpu.make_async_copy(prev_ref, far, in_sems.at[2]),
         ]
@@ -62,64 +61,87 @@
     )
 
 
-def pack(base, index, me, grad_parts, from_next, from_prev, block_cols):
-    rows, width = from_next.shape
-    dtype = from_next.dtype
+def pack(index, own, from_next, from_prev, block_cols):
+    rows, width = own.shape
     dests = index.shape[0]
     return pl.pallas_call(
-        functools.partial(pack_kernel, base),
-        out_shape=jax.ShapeDtypeStruct((dests, rows, block_cols), dtype),
-        in_specs=[SMEM, SMEM, ANY, ANY, ANY],
+        pack_kernel,
+        out_shape=jax.ShapeDtypeStruct((dests, rows, block_cols), own.dtype),
+        in_specs=[SMEM, ANY, ANY, ANY],
         out_specs=ANY,
-        scratch_shapes=[pltpu.VMEM((rows, width), dtype)] * 3
+        scratch_shapes=[pltpu.VMEM((rows, width), own.dtype)] * 3
         + [
-            pltpu.VMEM((width // block_cols, rows, block_cols), dtype),
+            pltpu.VMEM((width // block_cols, rows, block_cols), own.dtype),
             pltpu.SemaphoreType.DMA((3,)),
             pltpu.SemaphoreType.DMA((dests,)),
         ],
         cost_estimate=cost(8 * rows * width + 2 * dests * rows * block_cols),
         compiler_params=vmem(4),
         name="pack",
-    )(index, me, grad_parts, from_next, from_prev)
-
-
-def pick_kernel(inputs, index_ref, *refs):
-    sources, outs, stage, in_sems, out_sems = refs[:inputs], refs[inputs:-3], refs[-3], refs[-2], refs[-1]
-    each = sources[0].shape[0]
-    run_all(
+    )(index, own, from_next, from_prev)
+
+
+def run_used(used_ref, copies):
+    for start in (True, False):
+        for i, copy in enumerate(copies):
+
+            @pl.when(used_ref[i] > 0)
+            def _():
+                copy.start() if start else copy.wait()
+
+
+def to_slots_kernel(row_ref, used_ref, rows_ref, *refs):
+    outs, sems = refs[:-1], refs[-1]
+    slots = outs[0].shape[0]
+    run_used(
+        used_ref,
         [
-            pltpu.make_async_copy(source, stage.at[pl.ds(i * each, each)], in_sems.at[i])
-            for i, source in enumerate(sources)
-        ]
-    )
-    copies = []
-    for out in outs:
-        for i in range(out.shape[0]):
-            at = len(copies)
-            copies.append(pltpu.make_async_copy(stage.at[index_ref[at]], out.at[i], out_sems.at[at]))
-    run_all(copies)
-
-
-def pick(index, sources, out_counts):
-    each, *entry = sources[0].shape
-    dtype = sources[0].dtype
-    total = each * len(sources)
-    taken = sum(out_counts)
-    size = 2 * entry[0] * entry[1] * entry[2]
+            pltpu.make_async_copy(rows_ref.at[row_ref[i]], outs[i // slots].at[i % slots], sems.at[i])
+            for i in range(len(outs) * slots)
+        ],
+    )
+
+
+def to_slots(row, used, rows, replicas):
+    entry = rows.shape[1:]
+    held = row.shape[0]
     return pl.pallas_call(
-        functools.partial(pick_kernel, len(sources)),
-        out_shape=[jax.ShapeDtypeStruct((n, *entry), dtype) for n in out_counts],
-        in_specs=[SMEM] + [ANY] * len(sources),
-        out_specs=[ANY] * len(out_counts),
-        scratch_shapes=[
-            pltpu.VMEM((total, *entry), dtype),
-            pltpu.SemaphoreType.DMA((len(sources),)),
-            pltpu.SemaphoreType.DMA((taken,)),
-        ],
-        cost_estimate=cost((total + taken) * size),
+        to_slots_kernel,
+        out_shape=[jax.ShapeDtypeStruct((held // replicas, *entry), rows.dtype)] * replicas,
+        in_specs=[SMEM, SMEM, ANY],
+        out_specs=[ANY] * replicas,
+        scratch_shapes=[pltpu.SemaphoreType.DMA((held,))],
+        cost_estimate=cost(4 * held * entry[0] * entry[1] * entry[2]),
         compiler_params=vmem(4),
-        name="pick",
-    )(index, *sources)
+        name="to_slots",
+    )(row, used, rows)
+
+
+def from_slots_kernel(row_ref, used_ref, *refs):
+    parts, rows_ref, sems = refs[:-2], refs[-2], refs[-1]
+    slots = parts[0].shape[0]
+    run_used(
+        used_ref,
+        [
+            pltpu.make_async_copy(parts[i // slots].at[i % slots], rows_ref.at[row_ref[i]], sems.at[i])
+            for i in range(len(parts) * slots)
+        ],
+    )
+
+
+def from_slots(row, used, parts, row_blocks):
+    slots, *entry = parts[0].shape
+    held = row.shape[0]
+    return pl.pallas_call(
+        from_slots_kernel,
+        out_shape=jax.ShapeDtypeStruct((row_blocks, *entry), parts[0].dtype),
+        in_specs=[SMEM, SMEM] + [ANY] * len(parts),
+        out_specs=ANY,
+        scratch_shapes=[pltpu.SemaphoreType.DMA((held,))],
+        cost_estimate=cost(4 * held * entry[0] * entry[1] * entry[2]),
+        compiler_params=vmem(4),
+        name="from_slots",
+    )(row, used, *parts)
 
 
 def precondition_kernel(chunk_pieces, used_ref, me_ref, *refs):
@@ -132,17 +154,26 @@
     loads = [
         pltpu.make_async_copy(piece, grad.at[:, :, i // count, (me + count - i % count) % count], in_sems.at[i])
         for i, piece in enumerate(pieces)
-    ] + [
-        pltpu.make_async_copy(left_ref, left, root_sems.at[0]),
-        pltpu.make_async_copy(right_ref, right, root_sems.at[1]),
     ]
+    roots = [
+        (
+            pltpu.make_async_copy(left_ref.at[s], left.at[s], root_sems.at[0, s]),
+            pltpu.make_async_copy(right_ref.at[s], right.at[s], root_sems.at[1, s]),
+        )
+        for s in range(slots)
+    ]
+    for pair in roots:
+        for copy in pair:
+            copy.start()
     run_all(loads)
     stores = []
     for s in range(slots):
         whole = grad[s].reshape(block, block)
         whole = jnp.where(used_ref[s] > 0, whole, jnp.zeros_like(whole))
         grad[s] = whole.reshape(grad.shape[1:])
+        roots[s][0].wait()
         part = jnp.dot(left[s], whole, preferred_element_type=jnp.float32).astype(whole.dtype)
+        roots[s][1].wait()
         result = jnp.dot(part, right[s], preferred_element_type=jnp.float32).astype(whole.dtype)
         update[s] = result.reshape(update.shape[1:])
         sends = [pltpu.make_async_copy(grad.at[s], grad_ref.at[s], grad_sems.at[s])] + [
@@ -165,7 +196,7 @@
     grad, *outs = pl.pallas_call(
         functools.partial(precondition_kernel, total),
         out_shape=[jax.ShapeDtypeStruct(layout, dtype)] + [jax.ShapeDtypeStruct(pieces[0].shape, dtype)] * total,
-        in_specs=[SMEM, SMEM] + [ANY] * (total + 2),
+        in_specs=[SMEM, SMEM] + [ANY] * total + [HBM] * 2,
         out_specs=[ANY] * (total + 1),
         scratch_shapes=[
             pltpu.VMEM(layout, dtype),
@@ -173,7 +204,7 @@
             pltpu.VMEM(root_right.shape, dtype),
             pltpu.VMEM(layout, dtype),
             pltpu.SemaphoreType.DMA((total,)),
-            pltpu.SemaphoreType.DMA((2,)),
+            pltpu.SemaphoreType.DMA((2, slots)),
             pltpu.SemaphoreType.DMA((slots,)),
             pltpu.SemaphoreType.DMA((slots, total)),
         ],
@@ -214,18 +245,17 @@
     )(index, pieces)
 
 
-def place_kernel(base, me_ref, *refs):
-    parts = refs[:5]
+def place_kernel(base, quarter, places, me_ref, *refs):
+    parts = refs[: len(places)]
     out_ref, stage, in_sems, out_sems = refs[-4:]
-    quarter = parts[0].shape[0]
-    half = parts[3].shape[0]
     me = me_ref[0]
-    places = ((0, 0), (1, 0), (3, 0), (2, 0), (2, half))
     loads, stores = [], []
+    filled = 0
     for i, (offset, down) in enumerate(places):
         rows = parts[i].shape[0]
-        held = stage.at[pl.ds(offset * quarter + down, rows)]
-        start = pl.multiple_of(base + (me + offset) % 4 * quarter + down, half)
+        held = stage.at[pl.ds(filled, rows)]
+        filled += rows
+        start = pl.multiple_of(base + (me + offset) % 4 * quarter + down, quarter // 2)
         loads.append(pltpu.make_async_copy(parts[i], held, in_sems.at[i]))
         stores.append(pltpu.make_async_copy(held, out_ref.at[pl.ds(start, rows)], out_sems.at[i]))
     for load in loads:
@@ -246,25 +276,28 @@
     return shift(from_prev[:half], 1), shift(from_next[half:], -1)
 
 
-def place(me, parts, updates, base, total_rows):
-    quarter, width = parts[0].shape
+def place(me, near, far, updates, base, quarter, total_rows):
+    places = ((0, 0), (1, 0), (3, 0)) * (len(near) > 0) + ((2, 0), (2, quarter // 2)) * (len(far) > 0)
+    parts = [*near, *far]
+    rows = sum(part.shape[0] for part in parts)
+    width = parts[0].shape[1]
     operands = [me, *parts]
     aliases = {}
     if updates is not None:
         aliases = {len(operands): 0}
         operands.append(updates)
     return pl.pallas_call(
-        functools.partial(place_kernel, base),
+        functools.partial(place_kernel, base, quarter, places),
         out_shape=jax.ShapeDtypeStruct((total_rows, width), parts[0].dtype),
-        in_specs=[SMEM] + [ANY] * (len(operands) - 1),
-        out_specs=ANY,
+        in_specs=[SMEM] + [ANY] * len(parts) + [HBM] * len(aliases),
+        out_specs=HBM,
         scratch_shapes=[
-            pltpu.VMEM((4 * quarter, width), parts[0].dtype),
-            pltpu.SemaphoreType.DMA((5,)),
-            pltpu.SemaphoreType.DMA((5,)),
+            pltpu.VMEM((rows, width), parts[0].dtype),
+            pltpu.SemaphoreType.DMA((len(parts),)),
+            pltpu.SemaphoreType.DMA((len(parts),)),
         ],
         input_output_aliases=aliases,
-        cost_estimate=cost(16 * quarter * width),
+        cost_estimate=cost(4 * rows * width),
         compiler_params=vmem(4),
         name="place",
     )(*operands)
@@ -305,22 +338,16 @@
     send_piece = jnp.sum(jnp.where(to_column, pieces[None, :], 0), axis=1)
 
     held = jnp.arange(held_count, dtype=jnp.int32)
-    row_ids = jnp.arange(row_blocks, dtype=jnp.int32)
 
     def held_rows(replica):
         slot_ids = (replica * expert_count + my_expert) * slot_count + held % slot_count
         holds = owner_slot[None, :] == slot_ids[:, None]
-        return jnp.sum(jnp.where(holds, blocks[None, :] // wide_count, 0), axis=1), jnp.any(holds, axis=1)
-
-    def held_of_row(replica):
-        rows, used = held_rows(replica)
-        match = (rows[None, :] == row_ids[:, None]) & used[None, :]
-        return jnp.sum(jnp.where(match, held[None, :], 0), axis=1)
+        return jnp.sum(jnp.where(holds, blocks[None, :] // wide_count, 0), axis=1), jnp.sum(holds.astype(jnp.int32), axis=1)
 
     ahead = held // slot_count
-    row_from, used = held_rows((my_dp + ahead) % dp_count)
-    back_from = held_of_row((my_dp + dp_count - ahead) % dp_count)
-    my_used = used[:slot_count].astype(jnp.int32)
+    rows_ahead = held_rows((my_dp + ahead) % dp_count)
+    rows_behind = held_rows((my_dp + dp_count - ahead) % dp_count)
+    my_used = rows_ahead[1][:slot_count]
 
     def part(chunk, offset, down, rows):
         start = chunk * chunk_rows + (my_dp + offset) % dp_count * quarter + down
@@ -332,17 +359,15 @@
         return to_prev, to_next
 
     def packed(chunk, to_prev, to_next):
-        return pack(chunk * chunk_rows, send_piece, me, grad_parts, shift(to_prev, -1), shift(to_next, 1), block_cols)
+        return pack(send_piece, part(chunk, 0, 0, quarter), shift(to_prev, -1), shift(to_next, 1), block_cols)
 
     entry = (row_blocks, halves, quarter, block_cols)
-    slots_of = (slot_count,) * dp_count
 
     def to_owners(incoming):
-        return replica_exchange(pick(row_from, [incoming.reshape(entry)], slots_of))
+        return replica_exchange(to_slots(*rows_ahead, incoming.reshape(entry), dp_count))
 
     def to_rows(column_parts):
-        (rows,) = pick(back_from, column_parts, (row_blocks,))
-        return rows.reshape(expert_count, quarter, block_cols)
+        return from_slots(*rows_behind, column_parts, row_blocks).reshape(expert_count, quarter, block_cols)
 
     from_next = shift(jnp.concatenate([part(chunk, 2, 0, half) for chunk in range(CHUNKS)]), -1)
     from_prev = shift(jnp.concatenate([part(chunk, 2, half, half) for chunk in range(CHUNKS)]), 1)
@@ -365,18 +390,23 @@
     first_back, new_left, new_right = lax.optimization_barrier((first_back, new_left, new_right))
     first_rows = to_rows(first_back)
     second_out, first_rows = lax.optimization_barrier((second_out, first_rows))
-    first_in, second_back = lax.optimization_barrier((expert_exchange(first_rows), replica_exchange(second_out)))
-    first_own = unpack(my_column, first_in)
-    second_in = expert_exchange(to_rows(second_back))
+    first_in, second_rows = lax.optimization_barrier(
+        (expert_exchange(first_rows), to_rows(replica_exchange(second_out)))
+    )
+    first_own, second_rows = lax.optimization_barrier((unpack(my_column, first_in), second_rows))
+    second_in = expert_exchange(second_rows)
 
     near = spread(first_own)
     far = spread_far(*near)
     far, second_in = lax.optimization_barrier((far, second_in))
     second_own = unpack(my_column, second_in)
-    updates = place(me, (first_own, *near, *far), None, 0, shard_rows)
+    updates = place(me, (first_own, *near), far, None, 0, quarter, shard_rows)
     near = spread(second_own)
     near, updates = lax.optimization_barrier((near, updates))
-    updates = place(me, (second_own, *near, *spread_far(*near)), updates, chunk_rows, shard_rows)
+    far = spread_far(*near)
+    updates = place(me, (second_own, *near), (), updates, chunk_rows, quarter, shard_rows)
+    far, updates = lax.optimization_barrier((far, updates))
+    updates = place(me, (), far, updates, chunk_rows, quarter, shard_rows)
     return new_left, new_right, updates
 
 

time: 208 us -> 204 us (0.981)
  local copies, waits for them, and re-layouts: 8.45 us -> 5.59 us
  Pallas kernels: 27 us -> 24.9 us
    unnamed x16 -> x12, local copies, waits for them, and re-layouts: 6.91 us -> 2.84 us
    pallas_call x8 -> x9, Pallas kernels: 19.9 us -> 17.1 us  [the longest x3 5.99 us: place(): pl.pallas_call(functools.partial(place_kernel, base, quarter, places), ou...]
  transfers between devices with their start and end apart: 30 -> 30, of which waited for: 20 -> 21; matrix products, arithmetic and copies ran while one was open for 3% -> 4% of each run, Pallas kernels for 4% -> 5%
where the time goes in v5:
time: 204 us; the launch traced here: 203 us
  waiting for transfers between devices  101 us (50%)
  starting transfers between devices  61.2 us (30%)
  Pallas kernels  24.9 us (12%)
  matrix products  5.67 us (3%)
  local copies, waits for them, and re-layouts  5.59 us (3%)
  other arithmetic  3.11 us (2%)
    ppermute x26, waiting for transfers between devices, shift(): lax.ppermute(x, 'dp', [(i, (i + step) % count) for i in range(count)])  96 us
    ppermute x26, starting transfers between devices, shift(): lax.ppermute(x, 'dp', [(i, (i + step) % count) for i in range(count)])  37.5 us
    all_to_all x4, starting transfers between devices, expert_exchange(): return lax.all_to_all(x, 'expert', split_axis=0, concat_axis=0, tiled=True)  23.6 us
    pallas_call x3, Pallas kernels, place(): pl.pallas_call(functools.partial(place_kernel, base, quarter, places), ou...  5.99 us
    pallas_call x1, Pallas kernels, precondition(): pl.pallas_call(functools.partial(precondition_kernel, total), out_shape=[...  5.55 us
    pallas_call x2, Pallas kernels, pack(): pl.pallas_call(pack_kernel, out_shape=jax.ShapeDtypeStruct((dests, rows,...  5.55 us
    all_to_all x4, waiting for transfers between devices, expert_exchange(): return lax.all_to_all(x, 'expert', split_axis=0, concat_axis=0, tiled=True)  5.23 us
  transfers between devices with their start and end apart: 30, of which 21 were waited for; matrix products, arithmetic and copies ran while one was open for 4% of the time, Pallas kernels for 5%

profile of v5, /device:TPU:0, one launch (start us, length us, event | category | flops | bytes accessed | tf_op | source)
XLA Modules:
  0.0 202.9 jit_solution(74300104990017421)
XLA Ops:
  2.1 4.2 %collective-permute-start = (bf16[32,7168]{1,0:T(8,128)(2,1)S(1)}, bf16[32,7168]{1,0:T(8,128)(2,1)S(1)}, u32[]{:S(2)}, u32[]{:S(2)}) collective-permute-start(bf16[32,7168]{1,0:T(8,128)(2,1)S(1)} %pad_maximum_fusion), channel_id=1, source_target_pairs={{0,96},{32,0},{64,32},{96,64},{1,97},{33,1},{65,33},{97,65},{2,98}... | collective-permute-start | bytes 1376264 | tf_op jit(solution)/shard_map/ppermute | solution.py:19
  6.4 9.6 %collective-permute-done = bf16[32,7168]{1,0:T(8,128)(2,1)S(1)} collective-permute-done((bf16[32,7168]{1,0:T(8,128)(2,1)S(1)}, bf16[32,7168]{1,0:T(8,128)(2,1)S(1)}, u32[]{:S(2)}, u32[]{:S(2)}) %collective-permute-start) | collective-permute-done | bytes 458784 | tf_op jit(solution)/shard_map/ppermute | solution.py:19
  16.1 3.5 %collective-permute-done.1 = bf16[32,7168]{1,0:T(8,128)(2,1)S(1)} collective-permute-done((bf16[32,7168]{1,0:T(8,128)(2,1)S(1)}, bf16[32,7168]{1,0:T(8,128)(2,1)S(1)}, u32[]{:S(2)}, u32[]{:S(2)}) %collective-permute-start.1) | collective-permute-done | bytes 458784 | tf_op jit(solution)/shard_map/ppermute | solution.py:19
  22.3 3.2 %collective-permute-start.2 = (bf16[32,7168]{1,0:T(8,128)(2,1)S(1)}, bf16[32,7168]{1,0:T(8,128)(2,1)S(1)}, u32[]{:S(2)}, u32[]{:S(2)}) collective-permute-start(bf16[32,7168]{1,0:T(8,128)(2,1)S(1)} %get-tuple-element.108), channel_id=1, source_target_pairs={{0,96},{32,0},{64,32},{96,64},{1,97},{33,1},{65,33},{97,65},{2,98}... | collective-permute-start | bytes 1376264 | tf_op jit(solution)/shard_map/ppermute | solution.py:19
  27.0 7.6 %collective-permute-done.3.prev_ref = bf16[32,7168]{1,0:T(8,128)(2,1)S(1)} collective-permute-done((bf16[32,7168]{1,0:T(8,128)(2,1)S(1)}, bf16[32,7168]{1,0:T(8,128)(2,1)S(1)}, u32[]{:S(2)}, u32[]{:S(2)}) %collective-permute-start.3) | collective-permute-done | bytes 458784 | tf_op jit(solution)/shard_map/ppermute | solution.py:19
  34.6 2.8 %pack.2 = bf16[32,32,512]{2,1,0:T(8,128)(2,1)} custom-call(s32[32]{0:T(128)S(1)} %select_reduce_fusion.index_ref, bf16[32,7168]{1,0:T(8,128)(2,1)S(1)} %get-tuple-element.106.own_ref, bf16[32,7168]{1,0:T(8,128)(2,1)S(1)} %collective-permute-done.2.next_ref, bf16[32,7168]{1,0:T(8,128)(2,1)S(1)} %collective-permute-done.3.prev_ref), custom_call_target="tpu_custom_call" | custom-call | bytes 2883584 | tf_op jit(solution)/shard_map/pack/pallas_call | solution.py:67
  37.4 7.3 %all-to-all-start = ((bf16[32,32,512]{2,1,0:T(8,128)(2,1)}), bf16[32,32,512]{2,1,0:T(8,128)(2,1)S(1)}, u32[]{:S(2)}, u32[]{:S(2)}) async-start(bf16[32,32,512]{2,1,0:T(8,128)(2,1)} %pack.2), calls=%async_computation | async-start | bytes 2097152 | tf_op jit(solution)/shard_map/all_to_all | solution.py:307
  44.7 3.0 %collective-permute-start.7 = (bf16[32,7168]{1,0:T(8,128)(2,1)}, bf16[32,7168]{1,0:T(8,128)(2,1)S(1)}, u32[]{:S(2)}, u32[]{:S(2)}) collective-permute-start(bf16[32,7168]{1,0:T(8,128)(2,1)} %get-tuple-element.57), channel_id=1, source_target_pairs={{0,96},{32,0},{64,32},{96,64},{1,97},{33,1},{65,33},{97,65},{2,98}... | collective-permute-start | bytes 1376264 | tf_op jit(solution)/shard_map/ppermute | solution.py:19
  47.7 10.5 %collective-permute-done.7.next_ref = bf16[32,7168]{1,0:T(8,128)(2,1)S(1)} collective-permute-done((bf16[32,7168]{1,0:T(8,128)(2,1)}, bf16[32,7168]{1,0:T(8,128)(2,1)S(1)}, u32[]{:S(2)}, u32[]{:S(2)}) %collective-permute-start.7) | collective-permute-done | bytes 458784 | tf_op jit(solution)/shard_map/ppermute | solution.py:19
  58.3 3.3 %collective-permute-done.8.prev_ref = bf16[32,7168]{1,0:T(8,128)(2,1)S(1)} collective-permute-done((bf16[32,7168]{1,0:T(8,128)(2,1)}, bf16[32,7168]{1,0:T(8,128)(2,1)S(1)}, u32[]{:S(2)}, u32[]{:S(2)}) %collective-permute-start.8) | collective-permute-done | bytes 458784 | tf_op jit(solution)/shard_map/ppermute | solution.py:19
  61.6 2.8 %pack.3 = bf16[32,32,512]{2,1,0:T(8,128)(2,1)} custom-call(s32[32]{0:T(128)S(1)} %select_reduce_fusion.index_ref, bf16[32,7168]{1,0:T(8,128)(2,1)S(1)} %get-tuple-element.105.own_ref, bf16[32,7168]{1,0:T(8,128)(2,1)S(1)} %collective-permute-done.7.next_ref, bf16[32,7168]{1,0:T(8,128)(2,1)S(1)} %collective-permute-done.8.prev_ref), custom_call_target="tpu_custom_call" | custom-call | bytes 2883584 | tf_op jit(solution)/shard_map/pack/pallas_call | solution.py:67
  64.4 7.3 %all-to-all-start.1 = ((bf16[32,32,512]{2,1,0:T(8,128)(2,1)}), bf16[32,32,512]{2,1,0:T(8,128)(2,1)S(1)}, u32[]{:S(2)}, u32[]{:S(2)}) async-start(bf16[32,32,512]{2,1,0:T(8,128)(2,1)} %pack.3), calls=%async_computation.1 | async-start | bytes 2097152 | tf_op jit(solution)/shard_map/all_to_all | solution.py:307
  76.6 9.3 %collective-permute-done.4.refs_1_ = bf16[3,2,32,512]{3,2,1,0:T(8,128)(2,1)S(1)} collective-permute-done((bf16[3,2,32,512]{3,2,1,0:T(8,128)(2,1)S(1)}, bf16[3,2,32,512]{3,2,1,0:T(8,128)(2,1)S(1)}, u32[]{:S(2)}, u32[]{:S(2)}) %collective-permute-start.4) | collective-permute-done | bytes 196640 | tf_op jit(solution)/shard_map/ppermute | solution.py:19
  93.7 9.1 %collective-permute-done.9.refs_5_ = bf16[3,2,32,512]{3,2,1,0:T(8,128)(2,1)S(1)} collective-permute-done((bf16[3,2,32,512]{3,2,1,0:T(8,128)(2,1)S(1)}, bf16[3,2,32,512]{3,2,1,0:T(8,128)(2,1)S(1)}, u32[]{:S(2)}, u32[]{:S(2)}) %collective-permute-start.9) | collective-permute-done | bytes 196640 | tf_op jit(solution)/shard_map/ppermute | solution.py:19
  106.2 5.6 %precondition.1 = (bf16[3,2,2,4,32,512]{5,4,3,2,1,0:T(8,128)(2,1)S(1)}, bf16[3,2,32,512]{3,2,1,0:T(8,128)(2,1)S(1)}, bf16[3,2,32,512]{3,2,1,0:T(8,128)(2,1)S(1)}...) custom-call(s32[3]{0:T(128)S(1)} %bitcast.39, ...), custom_call_target="tpu_custom_call" | custom-call | flops 1610612736 | bytes 7864320 | tf_op jit(solution)/shard_map/precondition/pallas_call | solution.py:196
  112.1 3.6 %collective-permute-start.13 = (bf16[3,2,32,512]{3,2,1,0:T(8,128)(2,1)S(1)}, bf16[3,2,32,512]{3,2,1,0:T(8,128)(2,1)S(1)}, u32[]{:S(2)}, u32[]{:S(2)}) collective-permute-start(bf16[3,2,32,512]{3,2,1,0:T(8,128)(2,1)S(1)} %get-tuple-element.70), channel_id=1, source_target_pairs={{0,64},{32,96},{64,0},{96,32},{1,65},{33,97},{65,1},{97,33},{2,66}... | collective-permute-start | bytes 589832 | tf_op jit(solution)/shard_map/ppermute | solution.py:19
  115.7 2.9 %multiply_add_fusion = f32[3,512,512]{2,1,0:T(8,128)} fusion(f32[3,512,512]{2,1,0:T(8,128)S(1)} %copy-done.2, bf16[3,512,512]{2,1,0:T(8,128)(2,1)S(1)} %bitcast.35), kind=kOutput, calls=%fused_computation | convolution fusion | flops 807665664 | bytes 7864320 | tf_op jit(solution)/shard_map/sji,sjk->sik/dot_general | solution.py:387
  118.5 2.8 %multiply_add_fusion.1 = f32[3,512,512]{2,1,0:T(8,128)} fusion(f32[3,512,512]{2,1,0:T(8,128)S(1)} %copy-done.3, bf16[3,512,512]{2,1,0:T(8,128)(2,1)S(1)} %bitcast.36), kind=kOutput, calls=%fused_computation.1 | convolution fusion | flops 807665664 | bytes 7864320 | tf_op jit(solution)/shard_map/sij,skj->sik/dot_general | solution.py:386
  121.3 3.0 %collective-permute-done.13.refs_2_ = bf16[3,2,32,512]{3,2,1,0:T(8,128)(2,1)S(1)} collective-permute-done((bf16[3,2,32,512]{3,2,1,0:T(8,128)(2,1)S(1)}, bf16[3,2,32,512]{3,2,1,0:T(8,128)(2,1)S(1)}, u32[]{:S(2)}, u32[]{:S(2)}) %collective-permute-start.13) | collective-permute-done | bytes 196640 | tf_op jit(solution)/shard_map/ppermute | solution.py:19
  125.8 4.5 %all-to-all-start.2 = ((bf16[32,32,512]{2,1,0:T(8,128)(2,1)}), bf16[32,32,512]{2,1,0:T(8,128)(2,1)S(1)}, u32[]{:S(2)}, u32[]{:S(2)}) async-start(bf16[32,32,512]{2,1,0:T(8,128)(2,1)} %bitcast.14), calls=%async_computation.2 | async-start | bytes 2097152 | tf_op jit(solution)/shard_map/all_to_all | solution.py:307
  130.5 3.4 %collective-permute-start.16 = (bf16[3,2,32,512]{3,2,1,0:T(8,128)(2,1)S(1)}, bf16[3,2,32,512]{3,2,1,0:T(8,128)(2,1)S(1)}, u32[]{:S(2)}, u32[]{:S(2)}) collective-permute-start(bf16[3,2,32,512]{3,2,1,0:T(8,128)(2,1)S(1)} %get-tuple-element.86), channel_id=1, source_target_pairs={{0,64},{32,96},{64,0},{96,32},{1,65},{33,97},{65,1},{97,33},{2,66}... | collective-permute-start | bytes 589832 | tf_op jit(solution)/shard_map/ppermute | solution.py:19
  134.0 4.9 %collective-permute-done.15.refs_1_ = bf16[3,2,32,512]{3,2,1,0:T(8,128)(2,1)S(1)} collective-permute-done((bf16[3,2,32,512]{3,2,1,0:T(8,128)(2,1)S(1)}, bf16[3,2,32,512]{3,2,1,0:T(8,128)(2,1)S(1)}, u32[]{:S(2)}, u32[]{:S(2)}) %collective-permute-start.15) | collective-permute-done | bytes 196640 | tf_op jit(solution)/shard_map/ppermute | solution.py:19
  138.9 4.3 %collective-permute-done.16.refs_2_ = bf16[3,2,32,512]{3,2,1,0:T(8,128)(2,1)S(1)} collective-permute-done((bf16[3,2,32,512]{3,2,1,0:T(8,128)(2,1)S(1)}, bf16[3,2,32,512]{3,2,1,0:T(8,128)(2,1)S(1)}, u32[]{:S(2)}, u32[]{:S(2)}) %collective-permute-start.16) | collective-permute-done | bytes 196640 | tf_op jit(solution)/shard_map/ppermute | solution.py:19
  148.7 4.6 %all-to-all-start.3 = ((bf16[32,32,512]{2,1,0:T(8,128)(2,1)}), bf16[32,32,512]{2,1,0:T(8,128)(2,1)S(1)}, u32[]{:S(2)}, u32[]{:S(2)}) async-start(bf16[32,32,512]{2,1,0:T(8,128)(2,1)} %bitcast.15), calls=%async_computation.3 | async-start | bytes 2097152 | tf_op jit(solution)/shard_map/all_to_all | solution.py:307
  156.0 10.2 %collective-permute-done.20.refs_1_ = bf16[32,7168]{1,0:T(8,128)(2,1)S(1)} collective-permute-done((bf16[32,7168]{1,0:T(8,128)(2,1)S(1)}, bf16[32,7168]{1,0:T(8,128)(2,1)S(1)}, u32[]{:S(2)}, u32[]{:S(2)}) %collective-permute-start.20) | collective-permute-done | bytes 458784 | tf_op jit(solution)/shard_map/ppermute | solution.py:19
  166.2 3.8 %collective-permute-start.21 = (bf16[16,7168]{1,0:T(8,128)(2,1)S(1)}, bf16[16,7168]{1,0:T(8,128)(2,1)S(1)}, u32[]{:S(2)}, u32[]{:S(2)}) collective-permute-start(bf16[16,7168]{1,0:T(8,128)(2,1)S(1)} %slice.38), channel_id=1, source_target_pairs={{0,96},{32,0},{64,32},{96,64},{1,97},{33,1},{65,33},{97,65},{2,98}... | collective-permute-start | bytes 688136 | tf_op jit(solution)/shard_map/ppermute | solution.py:19
  170.1 4.4 %collective-permute-done.21.refs_4_ = bf16[16,7168]{1,0:T(8,128)(2,1)S(1)} collective-permute-done((bf16[16,7168]{1,0:T(8,128)(2,1)S(1)}, bf16[16,7168]{1,0:T(8,128)(2,1)S(1)}, u32[]{:S(2)}, u32[]{:S(2)}) %collective-permute-start.21) | collective-permute-done | bytes 229408 | tf_op jit(solution)/shard_map/ppermute | solution.py:19
  174.5 3.5 %collective-permute-done.19.refs_3_ = bf16[16,7168]{1,0:T(8,128)(2,1)S(1)} collective-permute-done((bf16[16,7168]{1,0:T(8,128)(2,1)S(1)}, bf16[16,7168]{1,0:T(8,128)(2,1)S(1)}, u32[]{:S(2)}, u32[]{:S(2)}) %collective-permute-start.19) | collective-permute-done | bytes 229408 | tf_op jit(solution)/shard_map/ppermute | solution.py:19
  179.2 3.2 %collective-permute-start.22 = (bf16[32,7168]{1,0:T(8,128)(2,1)S(1)}, bf16[32,7168]{1,0:T(8,128)(2,1)S(1)}, u32[]{:S(2)}, u32[]{:S(2)}) collective-permute-start(bf16[32,7168]{1,0:T(8,128)(2,1)S(1)} %unpack.3.refs_0_), channel_id=1, source_target_pairs={{0,96},{32,0},{64,32},{96,64},{1,97},{33,1},{65,33},{97,65},{2,98}... | collective-permute-start | bytes 1376264 | tf_op jit(solution)/shard_map/ppermute | solution.py:19
  185.1 6.0 %collective-permute-done.23.refs_2_ = bf16[32,7168]{1,0:T(8,128)(2,1)S(1)} collective-permute-done((bf16[32,7168]{1,0:T(8,128)(2,1)S(1)}, bf16[32,7168]{1,0:T(8,128)(2,1)S(1)}, u32[]{:S(2)}, u32[]{:S(2)}) %collective-permute-start.23) | collective-permute-done | bytes 458784 | tf_op jit(solution)/shard_map/ppermute | solution.py:19
  191.1 3.0 %collective-permute-start.25 = (bf16[16,7168]{1,0:T(8,128)(2,1)S(1)}, bf16[16,7168]{1,0:T(8,128)(2,1)S(1)}, u32[]{:S(2)}, u32[]{:S(2)}) collective-permute-start(bf16[16,7168]{1,0:T(8,128)(2,1)S(1)} %slice.33), channel_id=1, source_target_pairs={{0,96},{32,0},{64,32},{96,64},{1,97},{33,1},{65,33},{97,65},{2,98}... | collective-permute-start | bytes 688136 | tf_op jit(solution)/shard_map/ppermute | solution.py:19
  197.7 3.7 %collective-permute-done.24.refs_0_ = bf16[16,7168]{1,0:T(8,128)(2,1)S(1)} collective-permute-done((bf16[16,7168]{1,0:T(8,128)(2,1)S(1)}, bf16[16,7168]{1,0:T(8,128)(2,1)S(1)}, u32[]{:S(2)}, u32[]{:S(2)}) %collective-permute-start.24) | collective-permute-done | bytes 229408 | tf_op jit(solution)/shard_map/ppermute | solution.py:19
  (70 shorter events, 40.9 us)
Async XLA Ops:
  0.6 19.0 %copy-start.5 = (pred[32]{0:T(512)(128)(4,1)S(1)}, pred[32]{0:T(512)(128)(4,1)}, u32[]{:S(2)}) copy-start(pred[32]{0:T(512)(128)(4,1)} %constant.146.clone.1) | copy-start | bytes 100
  2.1 14.0 %collective-permute-start = (bf16[32,7168]{1,0:T(8,128)(2,1)S(1)}, bf16[32,7168]{1,0:T(8,128)(2,1)S(1)}, u32[]{:S(2)}, u32[]{:S(2)}) collective-permute-start(bf16[32,7168]{1,0:T(8,128)(2,1)S(1)} %pad_maximum_fusion), channel_id=1, source_target_pairs={{0,96},{32,0},{64,32},{96,64},{1,97},{33,1},{65,33},{97,65},{2,98}... | collective-permute-start | bytes 1376264 | tf_op jit(solution)/shard_map/ppermute | solution.py:19
  6.3 13.3 %collective-permute-start.1 = (bf16[32,7168]{1,0:T(8,128)(2,1)S(1)}, bf16[32,7168]{1,0:T(8,128)(2,1)S(1)}, u32[]{:S(2)}, u32[]{:S(2)}) collective-permute-start(bf16[32,7168]{1,0:T(8,128)(2,1)S(1)} %pad_maximum_fusion.1), channel_id=1, source_target_pairs={{0,32},{32,64},{64,96},{96,0},{1,33},{33,65},{65,97},{97,1},{2,34}... | collective-permute-start | bytes 1376264 | tf_op jit(solution)/shard_map/ppermute | solution.py:19
  22.3 12.3 %collective-permute-start.3 = (bf16[32,7168]{1,0:T(8,128)(2,1)S(1)}, bf16[32,7168]{1,0:T(8,128)(2,1)S(1)}, u32[]{:S(2)}, u32[]{:S(2)}) collective-permute-start(bf16[32,7168]{1,0:T(8,128)(2,1)S(1)} %get-tuple-element.107), channel_id=1, source_target_pairs={{0,32},{32,64},{64,96},{96,0},{1,33},{33,65},{65,97},{97,1},{2,34}... | collective-permute-start | bytes 1376264 | tf_op jit(solution)/shard_map/ppermute | solution.py:19
  22.3 12.3 %collective-permute-start.2 = (bf16[32,7168]{1,0:T(8,128)(2,1)S(1)}, bf16[32,7168]{1,0:T(8,128)(2,1)S(1)}, u32[]{:S(2)}, u32[]{:S(2)}) collective-permute-start(bf16[32,7168]{1,0:T(8,128)(2,1)S(1)} %get-tuple-element.108), channel_id=1, source_target_pairs={{0,96},{32,0},{64,32},{96,64},{1,97},{33,1},{65,33},{97,65},{2,98}... | collective-permute-start | bytes 1376264 | tf_op jit(solution)/shard_map/ppermute | solution.py:19
  37.4 27.0 %all-to-all-start = ((bf16[32,32,512]{2,1,0:T(8,128)(2,1)}), bf16[32,32,512]{2,1,0:T(8,128)(2,1)S(1)}, u32[]{:S(2)}, u32[]{:S(2)}) async-start(bf16[32,32,512]{2,1,0:T(8,128)(2,1)} %pack.2), calls=%async_computation | async-start | bytes 2097152 | tf_op jit(solution)/shard_map/all_to_all | solution.py:307
  44.7 13.6 %collective-permute-start.7 = (bf16[32,7168]{1,0:T(8,128)(2,1)}, bf16[32,7168]{1,0:T(8,128)(2,1)S(1)}, u32[]{:S(2)}, u32[]{:S(2)}) collective-permute-start(bf16[32,7168]{1,0:T(8,128)(2,1)} %get-tuple-element.57), channel_id=1, source_target_pairs={{0,96},{32,0},{64,32},{96,64},{1,97},{33,1},{65,33},{97,65},{2,98}... | collective-permute-start | bytes 1376264 | tf_op jit(solution)/shard_map/ppermute | solution.py:19
  47.7 13.8 %collective-permute-start.8 = (bf16[32,7168]{1,0:T(8,128)(2,1)}, bf16[32,7168]{1,0:T(8,128)(2,1)S(1)}, u32[]{:S(2)}, u32[]{:S(2)}) collective-permute-start(bf16[32,7168]{1,0:T(8,128)(2,1)} %get-tuple-element.58), channel_id=1, source_target_pairs={{0,32},{32,64},{64,96},{96,0},{1,33},{33,65},{65,97},{97,1},{2,34}... | collective-permute-start | bytes 1376264 | tf_op jit(solution)/shard_map/ppermute | solution.py:19
  64.4 24.6 %all-to-all-start.1 = ((bf16[32,32,512]{2,1,0:T(8,128)(2,1)}), bf16[32,32,512]{2,1,0:T(8,128)(2,1)S(1)}, u32[]{:S(2)}, u32[]{:S(2)}) async-start(bf16[32,32,512]{2,1,0:T(8,128)(2,1)} %pack.3), calls=%async_computation.1 | async-start | bytes 2097152 | tf_op jit(solution)/shard_map/all_to_all | solution.py:307
  73.3 12.6 %collective-permute-start.4 = (bf16[3,2,32,512]{3,2,1,0:T(8,128)(2,1)S(1)}, bf16[3,2,32,512]{3,2,1,0:T(8,128)(2,1)S(1)}, u32[]{:S(2)}, u32[]{:S(2)}) collective-permute-start(bf16[3,2,32,512]{3,2,1,0:T(8,128)(2,1)S(1)} %get-tuple-element.54), channel_id=1, source_target_pairs={{0,32},{32,64},{64,96},{96,0},{1,33},{33,65},{65,97},{97,1},{2,34}... | collective-permute-start | bytes 589832 | tf_op jit(solution)/shard_map/ppermute | solution.py:19
  73.4 12.5 %collective-permute-start.5 = (bf16[3,2,32,512]{3,2,1,0:T(8,128)(2,1)S(1)}, bf16[3,2,32,512]{3,2,1,0:T(8,128)(2,1)S(1)}, u32[]{:S(2)}, u32[]{:S(2)}) collective-permute-start(bf16[3,2,32,512]{3,2,1,0:T(8,128)(2,1)S(1)} %get-tuple-element.55), channel_id=1, source_target_pairs={{0,64},{32,96},{64,0},{96,32},{1,65},{33,97},{65,1},{97,33},{2,66}... | collective-permute-start | bytes 589832 | tf_op jit(solution)/shard_map/ppermute | solution.py:19
  75.1 11.4 %collective-permute-start.6 = (bf16[3,2,32,512]{3,2,1,0:T(8,128)(2,1)S(1)}, bf16[3,2,32,512]{3,2,1,0:T(8,128)(2,1)S(1)}, u32[]{:S(2)}, u32[]{:S(2)}) collective-permute-start(bf16[3,2,32,512]{3,2,1,0:T(8,128)(2,1)S(1)} %get-tuple-element.56), channel_id=1, source_target_pairs={{0,96},{32,0},{64,32},{96,64},{1,97},{33,1},{65,33},{97,65},{2,98}... | collective-permute-start | bytes 589832 | tf_op jit(solution)/shard_map/ppermute | solution.py:19
  90.4 12.4 %collective-permute-start.9 = (bf16[3,2,32,512]{3,2,1,0:T(8,128)(2,1)S(1)}, bf16[3,2,32,512]{3,2,1,0:T(8,128)(2,1)S(1)}, u32[]{:S(2)}, u32[]{:S(2)}) collective-permute-start(bf16[3,2,32,512]{3,2,1,0:T(8,128)(2,1)S(1)} %get-tuple-element.65), channel_id=1, source_target_pairs={{0,32},{32,64},{64,96},{96,0},{1,33},{33,65},{65,97},{97,1},{2,34}... | collective-permute-start | bytes 589832 | tf_op jit(solution)/shard_map/ppermute | solution.py:19
  90.4 12.3 %collective-permute-start.10 = (bf16[3,2,32,512]{3,2,1,0:T(8,128)(2,1)S(1)}, bf16[3,2,32,512]{3,2,1,0:T(8,128)(2,1)S(1)}, u32[]{:S(2)}, u32[]{:S(2)}) collective-permute-start(bf16[3,2,32,512]{3,2,1,0:T(8,128)(2,1)S(1)} %get-tuple-element.66), channel_id=1, source_target_pairs={{0,64},{32,96},{64,0},{96,32},{1,65},{33,97},{65,1},{97,33},{2,66}... | collective-permute-start | bytes 589832 | tf_op jit(solution)/shard_map/ppermute | solution.py:19
  92.2 11.2 %collective-permute-start.11 = (bf16[3,2,32,512]{3,2,1,0:T(8,128)(2,1)S(1)}, bf16[3,2,32,512]{3,2,1,0:T(8,128)(2,1)S(1)}, u32[]{:S(2)}, u32[]{:S(2)}) collective-permute-start(bf16[3,2,32,512]{3,2,1,0:T(8,128)(2,1)S(1)} %get-tuple-element.67), channel_id=1, source_target_pairs={{0,96},{32,0},{64,32},{96,64},{1,97},{33,1},{65,33},{97,65},{2,98}... | collective-permute-start | bytes 589832 | tf_op jit(solution)/shard_map/ppermute | solution.py:19
  106.2 9.4 %copy-start.2 = (f32[3,512,512]{2,1,0:T(8,128)S(1)}, f32[3,512,512]{2,1,0:T(8,128)}, u32[]{:S(2)}) copy-start(f32[3,512,512]{2,1,0:T(8,128)} %param.9) | copy-start | bytes 9437188
  111.8 9.6 %collective-permute-start.12 = (bf16[3,2,32,512]{3,2,1,0:T(8,128)(2,1)S(1)}, bf16[3,2,32,512]{3,2,1,0:T(8,128)(2,1)S(1)}, u32[]{:S(2)}, u32[]{:S(2)}) collective-permute-start(bf16[3,2,32,512]{3,2,1,0:T(8,128)(2,1)S(1)} %get-tuple-element.69), channel_id=1, source_target_pairs={{0,32},{32,64},{64,96},{96,0},{1,33},{33,65},{65,97},{97,1},{2,34}... | collective-permute-start | bytes 589832 | tf_op jit(solution)/shard_map/ppermute | solution.py:19
  112.1 12.3 %collective-permute-start.13 = (bf16[3,2,32,512]{3,2,1,0:T(8,128)(2,1)S(1)}, bf16[3,2,32,512]{3,2,1,0:T(8,128)(2,1)S(1)}, u32[]{:S(2)}, u32[]{:S(2)}) collective-permute-start(bf16[3,2,32,512]{3,2,1,0:T(8,128)(2,1)S(1)} %get-tuple-element.70), channel_id=1, source_target_pairs={{0,64},{32,96},{64,0},{96,32},{1,65},{33,97},{65,1},{97,33},{2,66}... | collective-permute-start | bytes 589832 | tf_op jit(solution)/shard_map/ppermute | solution.py:19
  115.6 8.7 %collective-permute-start.14 = (bf16[3,2,32,512]{3,2,1,0:T(8,128)(2,1)S(1)}, bf16[3,2,32,512]{3,2,1,0:T(8,128)(2,1)S(1)}, u32[]{:S(2)}, u32[]{:S(2)}) collective-permute-start(bf16[3,2,32,512]{3,2,1,0:T(8,128)(2,1)S(1)} %get-tuple-element.71), channel_id=1, source_target_pairs={{0,96},{32,0},{64,32},{96,64},{1,97},{33,1},{65,33},{97,65},{2,98}... | collective-permute-start | bytes 589832 | tf_op jit(solution)/shard_map/ppermute | solution.py:19
  125.8 21.8 %all-to-all-start.2 = ((bf16[32,32,512]{2,1,0:T(8,128)(2,1)}), bf16[32,32,512]{2,1,0:T(8,128)(2,1)S(1)}, u32[]{:S(2)}, u32[]{:S(2)}) async-start(bf16[32,32,512]{2,1,0:T(8,128)(2,1)} %bitcast.14), calls=%async_computation.2 | async-start | bytes 2097152 | tf_op jit(solution)/shard_map/all_to_all | solution.py:307
  130.3 8.6 %collective-permute-start.15 = (bf16[3,2,32,512]{3,2,1,0:T(8,128)(2,1)S(1)}, bf16[3,2,32,512]{3,2,1,0:T(8,128)(2,1)S(1)}, u32[]{:S(2)}, u32[]{:S(2)}) collective-permute-start(bf16[3,2,32,512]{3,2,1,0:T(8,128)(2,1)S(1)} %get-tuple-element.85), channel_id=1, source_target_pairs={{0,32},{32,64},{64,96},{96,0},{1,33},{33,65},{65,97},{97,1},{2,34}... | collective-permute-start | bytes 589832 | tf_op jit(solution)/shard_map/ppermute | solution.py:19
  130.5 12.7 %collective-permute-start.16 = (bf16[3,2,32,512]{3,2,1,0:T(8,128)(2,1)S(1)}, bf16[3,2,32,512]{3,2,1,0:T(8,128)(2,1)S(1)}, u32[]{:S(2)}, u32[]{:S(2)}) collective-permute-start(bf16[3,2,32,512]{3,2,1,0:T(8,128)(2,1)S(1)} %get-tuple-element.86), channel_id=1, source_target_pairs={{0,64},{32,96},{64,0},{96,32},{1,65},{33,97},{65,1},{97,33},{2,66}... | collective-permute-start | bytes 589832 | tf_op jit(solution)/shard_map/ppermute | solution.py:19
  133.9 9.5 %collective-permute-start.17 = (bf16[3,2,32,512]{3,2,1,0:T(8,128)(2,1)S(1)}, bf16[3,2,32,512]{3,2,1,0:T(8,128)(2,1)S(1)}, u32[]{:S(2)}, u32[]{:S(2)}) collective-permute-start(bf16[3,2,32,512]{3,2,1,0:T(8,128)(2,1)S(1)} %get-tuple-element.87), channel_id=1, source_target_pairs={{0,96},{32,0},{64,32},{96,64},{1,97},{33,1},{65,33},{97,65},{2,98}... | collective-permute-start | bytes 589832 | tf_op jit(solution)/shard_map/ppermute | solution.py:19
  148.7 29.3 %all-to-all-start.3 = ((bf16[32,32,512]{2,1,0:T(8,128)(2,1)}), bf16[32,32,512]{2,1,0:T(8,128)(2,1)S(1)}, u32[]{:S(2)}, u32[]{:S(2)}) async-start(bf16[32,32,512]{2,1,0:T(8,128)(2,1)} %bitcast.15), calls=%async_computation.3 | async-start | bytes 2097152 | tf_op jit(solution)/shard_map/all_to_all | solution.py:307
  153.3 12.9 %collective-permute-start.20 = (bf16[32,7168]{1,0:T(8,128)(2,1)S(1)}, bf16[32,7168]{1,0:T(8,128)(2,1)S(1)}, u32[]{:S(2)}, u32[]{:S(2)}) collective-permute-start(bf16[32,7168]{1,0:T(8,128)(2,1)S(1)} %unpack.2.refs_0_), channel_id=1, source_target_pairs={{0,96},{32,0},{64,32},{96,64},{1,97},{33,1},{65,33},{97,65},{2,98}... | collective-permute-start | bytes 1376264 | tf_op jit(solution)/shard_map/ppermute | solution.py:19
  156.0 14.0 %collective-permute-start.18 = (bf16[32,7168]{1,0:T(8,128)(2,1)S(1)}, bf16[32,7168]{1,0:T(8,128)(2,1)S(1)}, u32[]{:S(2)}, u32[]{:S(2)}) collective-permute-start(bf16[32,7168]{1,0:T(8,128)(2,1)S(1)} %unpack.2.refs_0_), channel_id=1, source_target_pairs={{0,32},{32,64},{64,96},{96,0},{1,33},{33,65},{65,97},{97,1},{2,34}... | collective-permute-start | bytes 1376264 | tf_op jit(solution)/shard_map/ppermute | solution.py:19
  166.2 8.3 %collective-permute-start.21 = (bf16[16,7168]{1,0:T(8,128)(2,1)S(1)}, bf16[16,7168]{1,0:T(8,128)(2,1)S(1)}, u32[]{:S(2)}, u32[]{:S(2)}) collective-permute-start(bf16[16,7168]{1,0:T(8,128)(2,1)S(1)} %slice.38), channel_id=1, source_target_pairs={{0,96},{32,0},{64,32},{96,64},{1,97},{33,1},{65,33},{97,65},{2,98}... | collective-permute-start | bytes 688136 | tf_op jit(solution)/shard_map/ppermute | solution.py:19
  170.0 8.0 %collective-permute-start.19 = (bf16[16,7168]{1,0:T(8,128)(2,1)S(1)}, bf16[16,7168]{1,0:T(8,128)(2,1)S(1)}, u32[]{:S(2)}, u32[]{:S(2)}) collective-permute-start(bf16[16,7168]{1,0:T(8,128)(2,1)S(1)} %slice.37), channel_id=1, source_target_pairs={{0,32},{32,64},{64,96},{96,0},{1,33},{33,65},{65,97},{97,1},{2,34}... | collective-permute-start | bytes 688136 | tf_op jit(solution)/shard_map/ppermute | solution.py:19
  179.1 12.0 %collective-permute-start.23 = (bf16[32,7168]{1,0:T(8,128)(2,1)S(1)}, bf16[32,7168]{1,0:T(8,128)(2,1)S(1)}, u32[]{:S(2)}, u32[]{:S(2)}) collective-permute-start(bf16[32,7168]{1,0:T(8,128)(2,1)S(1)} %unpack.3.refs_0_), channel_id=1, source_target_pairs={{0,32},{32,64},{64,96},{96,0},{1,33},{33,65},{65,97},{97,1},{2,34}... | collective-permute-start | bytes 1376264 | tf_op jit(solution)/shard_map/ppermute | solution.py:19
  179.2 11.9 %collective-permute-start.22 = (bf16[32,7168]{1,0:T(8,128)(2,1)S(1)}, bf16[32,7168]{1,0:T(8,128)(2,1)S(1)}, u32[]{:S(2)}, u32[]{:S(2)}) collective-permute-start(bf16[32,7168]{1,0:T(8,128)(2,1)S(1)} %unpack.3.refs_0_), channel_id=1, source_target_pairs={{0,96},{32,0},{64,32},{96,64},{1,97},{33,1},{65,33},{97,65},{2,98}... | collective-permute-start | bytes 1376264 | tf_op jit(solution)/shard_map/ppermute | solution.py:19
  191.1 6.6 %collective-permute-start.25 = (bf16[16,7168]{1,0:T(8,128)(2,1)S(1)}, bf16[16,7168]{1,0:T(8,128)(2,1)S(1)}, u32[]{:S(2)}, u32[]{:S(2)}) collective-permute-start(bf16[16,7168]{1,0:T(8,128)(2,1)S(1)} %slice.33), channel_id=1, source_target_pairs={{0,96},{32,0},{64,32},{96,64},{1,97},{33,1},{65,33},{97,65},{2,98}... | collective-permute-start | bytes 688136 | tf_op jit(solution)/shard_map/ppermute | solution.py:19
  194.2 7.2 %collective-permute-start.24 = (bf16[16,7168]{1,0:T(8,128)(2,1)S(1)}, bf16[16,7168]{1,0:T(8,128)(2,1)S(1)}, u32[]{:S(2)}, u32[]{:S(2)}) collective-permute-start(bf16[16,7168]{1,0:T(8,128)(2,1)S(1)} %slice.32), channel_id=1, source_target_pairs={{0,32},{32,64},{64,96},{96,0},{1,33},{33,65},{65,97},{97,1},{2,34}... | collective-permute-start | bytes 688136 | tf_op jit(solution)/shard_map/ppermute | solution.py:19
  (4 other events, 12.9 us)

commit v6 on v5

--- a/solution.py
+++ b/solution.py
@@ -41,18 +41,13 @@
     return pltpu.CompilerParams(vmem_limit_bytes=mebibytes * 1024 * 1024)
 
 
-def pack_kernel(index_ref, own_ref, next_ref, prev_ref, out_ref, own, near, far, pieces, in_sems, out_sems):
+def pack_kernel(index_ref, *refs):
+    terms, (out_ref, held, pieces, in_sems, out_sems) = refs[:-5], refs[-5:]
     wide_count, _, block_cols = pieces.shape
-    run_all(
-        [
-            pltpu.make_async_copy(own_ref, own, in_sems.at[0]),
-            pltpu.make_async_copy(next_ref, near, in_sems.at[1]),
-            pltpu.make_async_copy(prev_ref, far, in_sems.at[2]),
-        ]
-    )
+    run_all([pltpu.make_async_copy(term, held.at[i], in_sems.at[i]) for i, term in enumerate(terms)])
     for w in range(wide_count):
         cols = slice(w * block_cols, (w + 1) * block_cols)
-        pieces[w] = add(own[:, cols], near[:, cols], far[:, cols])
+        pieces[w] = add(*(held[i, :, cols] for i in range(len(terms))))
     run_all(
         [
             pltpu.make_async_copy(pieces.at[index_ref[c]], out_ref.at[c], out_sems.at[c])
@@ -61,24 +56,48 @@
     )
 
 
-def pack(index, own, from_next, from_prev, block_cols):
-    rows, width = own.shape
+def pack(index, terms, block_cols):
+    rows, width = terms[0].shape
+    dtype = terms[0].dtype
     dests = index.shape[0]
+    count = len(terms)
     return pl.pallas_call(
         pack_kernel,
-        out_shape=jax.ShapeDtypeStruct((dests, rows, block_cols), own.dtype),
-        in_specs=[SMEM, ANY, ANY, ANY],
+        out_shape=jax.ShapeDtypeStruct((dests, rows, block_cols), dtype),
+        in_specs=[SMEM] + [ANY] * count,
         out_specs=ANY,
-        scratch_shapes=[pltpu.VMEM((rows, width), own.dtype)] * 3
-        + [
-            pltpu.VMEM((width // block_cols, rows, block_cols), own.dtype),
-            pltpu.SemaphoreType.DMA((3,)),
+        scratch_shapes=[
+            pltpu.VMEM((count, rows, width), dtype),
+            pltpu.VMEM((width // block_cols, rows, block_cols), dtype),
+            pltpu.SemaphoreType.DMA((count,)),
             pltpu.SemaphoreType.DMA((dests,)),
         ],
-        cost_estimate=cost(8 * rows * width + 2 * dests * rows * block_cols),
-        compiler_params=vmem(4),
+        cost_estimate=cost(2 * (count + 1) * rows * width + 2 * dests * rows * block_cols),
+        compiler_params=vmem(5),
         name="pack",
-    )(index, own, from_next, from_prev)
+    )(index, *terms)
+
+
+def stage_kernel(left_ref, right_ref, left_out, right_out, left, right, sems):
+    run_all([pltpu.make_async_copy(left_ref, left, sems.at[0]), pltpu.make_async_copy(right_ref, right, sems.at[1])])
+    run_all([pltpu.make_async_copy(left, left_out, sems.at[2]), pltpu.make_async_copy(right, right_out, sems.at[3])])
+
+
+def stage(left, right):
+    return pl.pallas_call(
+        stage_kernel,
+        out_shape=[jax.ShapeDtypeStruct(x.shape, x.dtype) for x in (left, right)],
+        in_specs=[HBM, HBM],
+        out_specs=[ANY, ANY],
+        scratch_shapes=[
+            pltpu.VMEM(left.shape, left.dtype),
+            pltpu.VMEM(right.shape, right.dtype),
+            pltpu.SemaphoreType.DMA((4,)),
+        ],
+        cost_estimate=cost(8 * left.size),
+        compiler_params=vmem(5),
+        name="stage",
+    )(left, right)
 
 
 def run_used(used_ref, copies):
@@ -196,7 +215,7 @@
     grad, *outs = pl.pallas_call(
         functools.partial(precondition_kernel, total),
         out_shape=[jax.ShapeDtypeStruct(layout, dtype)] + [jax.ShapeDtypeStruct(pieces[0].shape, dtype)] * total,
-        in_specs=[SMEM, SMEM] + [ANY] * total + [HBM] * 2,
+        in_specs=[SMEM, SMEM] + [ANY] * (total + 2),
         out_specs=[ANY] * (total + 1),
         scratch_shapes=[
             pltpu.VMEM(layout, dtype),
@@ -323,7 +342,6 @@
     block_count = owner_slot.shape[0]
     chunk_rows = shard_rows // CHUNKS
     quarter = chunk_rows // dp_count
-    half = quarter // 2
     held_count = dp_count * slot_count
 
     my_expert = lax.axis_index("expert")
@@ -353,13 +371,8 @@
         start = chunk * chunk_rows + (my_dp + offset) % dp_count * quarter + down
         return lax.dynamic_slice(grad_parts, (0, start, 0), (1, rows, row_width))[0]
 
-    def toward(chunk, from_next, from_prev):
-        to_prev = add(part(chunk, 3, 0, quarter), jnp.pad(from_next, ((0, half), (0, 0))))
-        to_next = add(part(chunk, 1, 0, quarter), jnp.pad(from_prev, ((half, 0), (0, 0))))
-        return to_prev, to_next
-
-    def packed(chunk, to_prev, to_next):
-        return pack(send_piece, part(chunk, 0, 0, quarter), shift(to_prev, -1), shift(to_next, 1), block_cols)
+    def parts(chunk):
+        return [part(chunk, offset, 0, quarter) for offset in range(dp_count)]
 
     entry = (row_blocks, halves, quarter, block_cols)
 
@@ -369,18 +382,18 @@
     def to_rows(column_parts):
         return from_slots(*rows_behind, column_parts, row_blocks).reshape(expert_count, quarter, block_cols)
 
-    from_next = shift(jnp.concatenate([part(chunk, 2, 0, half) for chunk in range(CHUNKS)]), -1)
-    from_prev = shift(jnp.concatenate([part(chunk, 2, half, half) for chunk in range(CHUNKS)]), 1)
-    first_packed = packed(0, *toward(0, from_next[:half], from_prev[:half]))
-    sends = toward(1, from_next[half:], from_prev[half:])
-    sends, first_packed = lax.optimization_barrier((sends, first_packed))
-    first_in = expert_exchange(first_packed)
-    second_in = expert_exchange(packed(1, *sends))
+    first_terms = replica_exchange(parts(0))
+    second_parts, first_terms = lax.optimization_barrier((parts(1), first_terms))
+    second_terms = replica_exchange(second_parts)
+    first_in = expert_exchange(pack(send_piece, first_terms, block_cols))
+    second_in = expert_exchange(pack(send_piece, second_terms, block_cols))
     first_owned = to_owners(first_in)
-    first_owned, second_in = lax.optimization_barrier((first_owned, second_in))
+    first_owned, second_in, (left, right) = lax.optimization_barrier(
+        (first_owned, second_in, stage(root_left, root_right))
+    )
     second_owned = to_owners(second_in)
 
-    grad, first_out, second_out = precondition(my_used, me, first_owned + second_owned, root_left, root_right)
+    grad, first_out, second_out = precondition(my_used, me, first_owned + second_owned, left, right)
 
     first_back = replica_exchange(first_out)
     left_gram = jnp.einsum("sij,skj->sik", grad, grad, preferred_element_type=jnp.float32)
@@ -396,9 +409,8 @@
     first_own, second_rows = lax.optimization_barrier((unpack(my_column, first_in), second_rows))
     second_in = expert_exchange(second_rows)
 
-    near = spread(first_own)
+    near, second_in = lax.optimization_barrier((spread(first_own), second_in))
     far = spread_far(*near)
-    far, second_in = lax.optimization_barrier((far, second_in))
     second_own = unpack(my_column, second_in)
     updates = place(me, (first_own, *near), far, None, 0, quarter, shard_rows)
     near = spread(second_own)

time: 204 us -> 212 us (1.039)
  local copies, waits for them, and re-layouts: 5.59 us -> 11.4 us
  waiting for transfers between devices: 101 us -> 105 us
  other arithmetic: 3.11 us -> 0.35 us
    unnamed x12 -> x18, local copies, waits for them, and re-layouts: 2.84 us -> 7.92 us
    all_to_all x4, waiting for transfers between devices: 5.23 us -> 8.57 us  [expert_exchange(): return lax.all_to_all(x, 'expert', split_axis=0, concat_axis=0, tiled=True)]
    convert_element_type x1 -> x0, other arithmetic: 2.69 us -> none  [add(): return total.astype(terms[0].dtype)]
  transfers between devices with their start and end apart: 30 -> 30, of which waited for: 21 -> 20; matrix products, arithmetic and copies ran while one was open for 4% -> 3% of each run, Pallas kernels for 5% -> 5%
where the time goes in v6:
time: 212 us; the launch traced here: 211 us
  waiting for transfers between devices  105 us (50%)
  starting transfers between devices  61.4 us (29%)
  Pallas kernels  26.1 us (12%)
  local copies, waits for them, and re-layouts  11.4 us (5%)
  matrix products  5.67 us (3%)
    ppermute x26, waiting for transfers between devices, shift(): lax.ppermute(x, 'dp', [(i, (i + step) % count) for i in range(count)])  96.3 us
    ppermute x26, starting transfers between devices, shift(): lax.ppermute(x, 'dp', [(i, (i + step) % count) for i in range(count)])  37.8 us
    all_to_all x4, starting transfers between devices, expert_exchange(): return lax.all_to_all(x, 'expert', split_axis=0, concat_axis=0, tiled=True)  23.6 us
    all_to_all x4, waiting for transfers between devices, expert_exchange(): return lax.all_to_all(x, 'expert', split_axis=0, concat_axis=0, tiled=True)  8.57 us
    unnamed x18, local copies, waits for them, and re-layouts  7.92 us
    pallas_call x2, Pallas kernels, pack(): pl.pallas_call(pack_kernel, out_shape=jax.ShapeDtypeStruct((dests, rows,...  6.23 us
    pallas_call x3, Pallas kernels, place(): pl.pallas_call(functools.partial(place_kernel, base, quarter, places), ou...  5.99 us
    pallas_call x1, Pallas kernels, precondition(): pl.pallas_call(functools.partial(precondition_kernel, total), out_shape=[...  5.55 us
  transfers between devices with their start and end apart: 30, of which 20 were waited for; matrix products, arithmetic and copies ran while one was open for 3% of the time, Pallas kernels for 5%

profile of v6, /device:TPU:0, one launch (start us, length us, event | category | flops | bytes accessed | tf_op | source)
XLA Modules:
  0.0 210.9 jit_solution(13820332137938277939)
XLA Ops:
  0.7 3.4 %dynamic-slice_bitcast_fusion = (bf16[32,7168]{1,0:T(8,128)(2,1)}, bf16[32,7168]{1,0:T(8,128)(2,1)S(1)}, bf16[32,7168]{1,0:T(8,128)(2,1)S(1)}, bf16[32,7168]{1,0...) fusion(bf16[1,256,7168]{2,1,0:T(8,128)(2,1)} %param.6, ...), kind=kLoop, calls=%fused_computation.2 | loop fusion | bytes 7340064 | tf_op jit(solution)/shard_map/squeeze | solution.py:372
  4.1 4.1 %collective-permute-start.2 = (bf16[32,7168]{1,0:T(8,128)(2,1)}, bf16[32,7168]{1,0:T(8,128)(2,1)S(1)}, u32[]{:S(2)}, u32[]{:S(2)}) collective-permute-start(bf16[32,7168]{1,0:T(8,128)(2,1)} %get-tuple-element.123), channel_id=1, source_target_pairs={{0,96},{32,0},{64,32},{96,64},{1,97},{33,1},{65,33},{97,65},{2,98}... | collective-permute-start | bytes 1376264 | tf_op jit(solution)/shard_map/ppermute | solution.py:19
  10.3 17.9 %collective-permute-done.2.refs_3_ = bf16[32,7168]{1,0:T(8,128)(2,1)S(1)} collective-permute-done((bf16[32,7168]{1,0:T(8,128)(2,1)}, bf16[32,7168]{1,0:T(8,128)(2,1)S(1)}, u32[]{:S(2)}, u32[]{:S(2)}) %collective-permute-start.2) | collective-permute-done | bytes 458784 | tf_op jit(solution)/shard_map/ppermute | solution.py:19
  28.1 3.1 %collective-permute-done.refs_1_ = bf16[32,7168]{1,0:T(8,128)(2,1)S(1)} collective-permute-done((bf16[32,7168]{1,0:T(8,128)(2,1)S(1)}, bf16[32,7168]{1,0:T(8,128)(2,1)S(1)}, u32[]{:S(2)}, u32[]{:S(2)}) %collective-permute-start) | collective-permute-done | bytes 458784 | tf_op jit(solution)/shard_map/ppermute | solution.py:19
  31.2 3.1 %pack.2 = bf16[32,32,512]{2,1,0:T(8,128)(2,1)} custom-call(s32[32]{0:T(128)S(1)} %select_reduce_fusion.index_ref, bf16[32,7168]{1,0:T(8,128)(2,1)S(1)} %get-tuple-element.61.refs_0_, bf16[32,7168]{1,0:T(8,128)(2,1)S(1)} %collective-permute-done.refs_1_, bf16[32,7168]{1,0:T(8,128)(2,1)S(1)} %collective-permute-done.1.refs_2_, ...), custom_call_target="tpu_custom_call" | custom-call | bytes 3342336 | tf_op jit(solution)/shard_map/pack/pallas_call | solution.py:64
  34.3 7.3 %all-to-all-start = ((bf16[32,32,512]{2,1,0:T(8,128)(2,1)}), bf16[32,32,512]{2,1,0:T(8,128)(2,1)S(1)}, u32[]{:S(2)}, u32[]{:S(2)}) async-start(bf16[32,32,512]{2,1,0:T(8,128)(2,1)} %pack.2), calls=%async_computation | async-start | bytes 2097152 | tf_op jit(solution)/shard_map/all_to_all | solution.py:326
  45.0 20.7 %collective-permute-done.6.refs_1_ = bf16[32,7168]{1,0:T(8,128)(2,1)S(1)} collective-permute-done((bf16[32,7168]{1,0:T(8,128)(2,1)}, bf16[32,7168]{1,0:T(8,128)(2,1)S(1)}, u32[]{:S(2)}, u32[]{:S(2)}) %collective-permute-start.6) | collective-permute-done | bytes 458784 | tf_op jit(solution)/shard_map/ppermute | solution.py:19
  66.3 3.1 %pack.3 = bf16[32,32,512]{2,1,0:T(8,128)(2,1)} custom-call(s32[32]{0:T(128)S(1)} %select_reduce_fusion.index_ref, bf16[32,7168]{1,0:T(8,128)(2,1)S(1)} %get-tuple-element.69.refs_0_, bf16[32,7168]{1,0:T(8,128)(2,1)S(1)} %collective-permute-done.6.refs_1_, bf16[32,7168]{1,0:T(8,128)(2,1)S(1)} %collective-permute-done.7.refs_2_, ...), custom_call_target="tpu_custom_call" | custom-call | bytes 3342336 | tf_op jit(solution)/shard_map/pack/pallas_call | solution.py:64
  69.5 7.3 %all-to-all-start.1 = ((bf16[32,32,512]{2,1,0:T(8,128)(2,1)}), bf16[32,32,512]{2,1,0:T(8,128)(2,1)S(1)}, u32[]{:S(2)}, u32[]{:S(2)}) async-start(bf16[32,32,512]{2,1,0:T(8,128)(2,1)} %pack.3), calls=%async_computation.1 | async-start | bytes 2097152 | tf_op jit(solution)/shard_map/all_to_all | solution.py:326
  78.7 3.6 %collective-permute-start.4 = (bf16[3,2,32,512]{3,2,1,0:T(8,128)(2,1)S(1)}, bf16[3,2,32,512]{3,2,1,0:T(8,128)(2,1)S(1)}, u32[]{:S(2)}, u32[]{:S(2)}) collective-permute-start(bf16[3,2,32,512]{3,2,1,0:T(8,128)(2,1)S(1)} %get-tuple-element.67), channel_id=1, source_target_pairs={{0,64},{32,96},{64,0},{96,32},{1,65},{33,97},{65,1},{97,33},{2,66}... | collective-permute-start | bytes 589832 | tf_op jit(solution)/shard_map/ppermute | solution.py:19
  87.8 3.7 %collective-permute-done.4.refs_2_ = bf16[3,2,32,512]{3,2,1,0:T(8,128)(2,1)S(1)} collective-permute-done((bf16[3,2,32,512]{3,2,1,0:T(8,128)(2,1)S(1)}, bf16[3,2,32,512]{3,2,1,0:T(8,128)(2,1)S(1)}, u32[]{:S(2)}, u32[]{:S(2)}) %collective-permute-start.4) | collective-permute-done | bytes 196640 | tf_op jit(solution)/shard_map/ppermute | solution.py:19
  95.8 3.6 %collective-permute-start.10 = (bf16[3,2,32,512]{3,2,1,0:T(8,128)(2,1)S(1)}, bf16[3,2,32,512]{3,2,1,0:T(8,128)(2,1)S(1)}, u32[]{:S(2)}, u32[]{:S(2)}) collective-permute-start(bf16[3,2,32,512]{3,2,1,0:T(8,128)(2,1)S(1)} %get-tuple-element.82), channel_id=1, source_target_pairs={{0,64},{32,96},{64,0},{96,32},{1,65},{33,97},{65,1},{97,33},{2,66}... | collective-permute-start | bytes 589832 | tf_op jit(solution)/shard_map/ppermute | solution.py:19
  99.3 4.6 %collective-permute-done.9.refs_5_ = bf16[3,2,32,512]{3,2,1,0:T(8,128)(2,1)S(1)} collective-permute-done((bf16[3,2,32,512]{3,2,1,0:T(8,128)(2,1)S(1)}, bf16[3,2,32,512]{3,2,1,0:T(8,128)(2,1)S(1)}, u32[]{:S(2)}, u32[]{:S(2)}) %collective-permute-start.9) | collective-permute-done | bytes 196640 | tf_op jit(solution)/shard_map/ppermute | solution.py:19
  103.9 4.5 %collective-permute-done.10.refs_6_ = bf16[3,2,32,512]{3,2,1,0:T(8,128)(2,1)S(1)} collective-permute-done((bf16[3,2,32,512]{3,2,1,0:T(8,128)(2,1)S(1)}, bf16[3,2,32,512]{3,2,1,0:T(8,128)(2,1)S(1)}, u32[]{:S(2)}, u32[]{:S(2)}) %collective-permute-start.10) | collective-permute-done | bytes 196640 | tf_op jit(solution)/shard_map/ppermute | solution.py:19
  111.3 5.5 %precondition.1 = (bf16[3,2,2,4,32,512]{5,4,3,2,1,0:T(8,128)(2,1)S(1)}, bf16[3,2,32,512]{3,2,1,0:T(8,128)(2,1)S(1)}, bf16[3,2,32,512]{3,2,1,0:T(8,128)(2,1)S(1)}...) custom-call(s32[3]{0:T(128)S(1)} %bitcast.31, ...), custom_call_target="tpu_custom_call" | custom-call | flops 1610612736 | bytes 7864320 | tf_op jit(solution)/shard_map/precondition/pallas_call | solution.py:215
  117.2 3.9 %collective-permute-start.13 = (bf16[3,2,32,512]{3,2,1,0:T(8,128)(2,1)S(1)}, bf16[3,2,32,512]{3,2,1,0:T(8,128)(2,1)S(1)}, u32[]{:S(2)}, u32[]{:S(2)}) collective-permute-start(bf16[3,2,32,512]{3,2,1,0:T(8,128)(2,1)S(1)} %get-tuple-element.88), channel_id=1, source_target_pairs={{0,64},{32,96},{64,0},{96,32},{1,65},{33,97},{65,1},{97,33},{2,66}... | collective-permute-start | bytes 589832 | tf_op jit(solution)/shard_map/ppermute | solution.py:19
  121.0 2.9 %multiply_add_fusion = f32[3,512,512]{2,1,0:T(8,128)} fusion(f32[3,512,512]{2,1,0:T(8,128)S(1)} %copy-done.6, bf16[3,512,512]{2,1,0:T(8,128)(2,1)S(1)} %bitcast.27), kind=kOutput, calls=%fused_computation | convolution fusion | flops 807665664 | bytes 7864320 | tf_op jit(solution)/shard_map/sji,sjk->sik/dot_general | solution.py:400
  123.9 2.8 %multiply_add_fusion.1 = f32[3,512,512]{2,1,0:T(8,128)} fusion(f32[3,512,512]{2,1,0:T(8,128)S(1)} %copy-done.7, bf16[3,512,512]{2,1,0:T(8,128)(2,1)S(1)} %bitcast.28), kind=kOutput, calls=%fused_computation.1 | convolution fusion | flops 807665664 | bytes 7864320 | tf_op jit(solution)/shard_map/sij,skj->sik/dot_general | solution.py:399
  126.7 3.3 %collective-permute-done.13.refs_2_ = bf16[3,2,32,512]{3,2,1,0:T(8,128)(2,1)S(1)} collective-permute-done((bf16[3,2,32,512]{3,2,1,0:T(8,128)(2,1)S(1)}, bf16[3,2,32,512]{3,2,1,0:T(8,128)(2,1)S(1)}, u32[]{:S(2)}, u32[]{:S(2)}) %collective-permute-start.13) | collective-permute-done | bytes 196640 | tf_op jit(solution)/shard_map/ppermute | solution.py:19
  131.5 4.5 %all-to-all-start.2 = ((bf16[32,32,512]{2,1,0:T(8,128)(2,1)}), bf16[32,32,512]{2,1,0:T(8,128)(2,1)S(1)}, u32[]{:S(2)}, u32[]{:S(2)}) async-start(bf16[32,32,512]{2,1,0:T(8,128)(2,1)} %bitcast.12), calls=%async_computation.2 | async-start | bytes 2097152 | tf_op jit(solution)/shard_map/all_to_all | solution.py:326
  136.1 3.6 %collective-permute-start.16 = (bf16[3,2,32,512]{3,2,1,0:T(8,128)(2,1)S(1)}, bf16[3,2,32,512]{3,2,1,0:T(8,128)(2,1)S(1)}, u32[]{:S(2)}, u32[]{:S(2)}) collective-permute-start(bf16[3,2,32,512]{3,2,1,0:T(8,128)(2,1)S(1)} %get-tuple-element.104), channel_id=1, source_target_pairs={{0,64},{32,96},{64,0},{96,32},{1,65},{33,97},{65,1},{97,33},{2,66}... | collective-permute-start | bytes 589832 | tf_op jit(solution)/shard_map/ppermute | solution.py:19
  139.6 5.0 %collective-permute-done.15.refs_1_ = bf16[3,2,32,512]{3,2,1,0:T(8,128)(2,1)S(1)} collective-permute-done((bf16[3,2,32,512]{3,2,1,0:T(8,128)(2,1)S(1)}, bf16[3,2,32,512]{3,2,1,0:T(8,128)(2,1)S(1)}, u32[]{:S(2)}, u32[]{:S(2)}) %collective-permute-start.15) | collective-permute-done | bytes 196640 | tf_op jit(solution)/shard_map/ppermute | solution.py:19
  144.6 4.3 %collective-permute-done.16.refs_2_ = bf16[3,2,32,512]{3,2,1,0:T(8,128)(2,1)S(1)} collective-permute-done((bf16[3,2,32,512]{3,2,1,0:T(8,128)(2,1)S(1)}, bf16[3,2,32,512]{3,2,1,0:T(8,128)(2,1)S(1)}, u32[]{:S(2)}, u32[]{:S(2)}) %collective-permute-start.16) | collective-permute-done | bytes 196640 | tf_op jit(solution)/shard_map/ppermute | solution.py:19
  154.4 4.6 %all-to-all-start.3 = ((bf16[32,32,512]{2,1,0:T(8,128)(2,1)}), bf16[32,32,512]{2,1,0:T(8,128)(2,1)S(1)}, u32[]{:S(2)}, u32[]{:S(2)}) async-start(bf16[32,32,512]{2,1,0:T(8,128)(2,1)} %bitcast.13), calls=%async_computation.3 | async-start | bytes 2097152 | tf_op jit(solution)/shard_map/all_to_all | solution.py:326
  159.3 3.0 %collective-permute-start.18 = (bf16[32,7168]{1,0:T(8,128)(2,1)S(1)}, bf16[32,7168]{1,0:T(8,128)(2,1)S(1)}, u32[]{:S(2)}, u32[]{:S(2)}) collective-permute-start(bf16[32,7168]{1,0:T(8,128)(2,1)S(1)} %unpack.2.refs_0_), channel_id=1, source_target_pairs={{0,96},{32,0},{64,32},{96,64},{1,97},{33,1},{65,33},{97,65},{2,98}... | collective-permute-start | bytes 1376264 | tf_op jit(solution)/shard_map/ppermute | solution.py:19
  162.3 10.7 %collective-permute-done.19.refs_2_ = bf16[32,7168]{1,0:T(8,128)(2,1)S(1)} collective-permute-done((bf16[32,7168]{1,0:T(8,128)(2,1)S(1)}, bf16[32,7168]{1,0:T(8,128)(2,1)S(1)}, u32[]{:S(2)}, u32[]{:S(2)}) %collective-permute-start.19) | collective-permute-done | bytes 458784 | tf_op jit(solution)/shard_map/ppermute | solution.py:19
  173.0 3.4 %all-to-all-done.3.pieces_ref = bf16[32,32,512]{2,1,0:T(8,128)(2,1)S(1)} async-done(((bf16[32,32,512]{2,1,0:T(8,128)(2,1)}), bf16[32,32,512]{2,1,0:T(8,128)(2,1)S(1)}, u32[]{:S(2)}, u32[]{:S(2)}) %all-to-all-start.3) | async-done | bytes 1048608 | tf_op jit(solution)/shard_map/all_to_all | solution.py:326
  177.8 3.0 %collective-permute-start.20 = (bf16[32,7168]{1,0:T(8,128)(2,1)S(1)}, bf16[32,7168]{1,0:T(8,128)(2,1)S(1)}, u32[]{:S(2)}, u32[]{:S(2)}) collective-permute-start(bf16[32,7168]{1,0:T(8,128)(2,1)S(1)} %unpack.3.refs_0_), channel_id=1, source_target_pairs={{0,96},{32,0},{64,32},{96,64},{1,97},{33,1},{65,33},{97,65},{2,98}... | collective-permute-start | bytes 1376264 | tf_op jit(solution)/shard_map/ppermute | solution.py:19
  180.9 3.2 %collective-permute-start.23 = (bf16[16,7168]{1,0:T(8,128)(2,1)S(1)}, bf16[16,7168]{1,0:T(8,128)(2,1)S(1)}, u32[]{:S(2)}, u32[]{:S(2)}) collective-permute-start(bf16[16,7168]{1,0:T(8,128)(2,1)S(1)} %slice.17), channel_id=1, source_target_pairs={{0,96},{32,0},{64,32},{96,64},{1,97},{33,1},{65,33},{97,65},{2,98}... | collective-permute-start | bytes 688136 | tf_op jit(solution)/shard_map/ppermute | solution.py:19
  184.1 12.1 %collective-permute-done.22.refs_3_ = bf16[16,7168]{1,0:T(8,128)(2,1)S(1)} collective-permute-done((bf16[16,7168]{1,0:T(8,128)(2,1)S(1)}, bf16[16,7168]{1,0:T(8,128)(2,1)S(1)}, u32[]{:S(2)}, u32[]{:S(2)}) %collective-permute-start.22) | collective-permute-done | bytes 229408 | tf_op jit(solution)/shard_map/ppermute | solution.py:19
  199.0 3.0 %collective-permute-start.25 = (bf16[16,7168]{1,0:T(8,128)(2,1)S(1)}, bf16[16,7168]{1,0:T(8,128)(2,1)S(1)}, u32[]{:S(2)}, u32[]{:S(2)}) collective-permute-start(bf16[16,7168]{1,0:T(8,128)(2,1)S(1)} %slice.19), channel_id=1, source_target_pairs={{0,96},{32,0},{64,32},{96,64},{1,97},{33,1},{65,33},{97,65},{2,98}... | collective-permute-start | bytes 688136 | tf_op jit(solution)/shard_map/ppermute | solution.py:19
  206.0 3.4 %collective-permute-done.24.refs_0_ = bf16[16,7168]{1,0:T(8,128)(2,1)S(1)} collective-permute-done((bf16[16,7168]{1,0:T(8,128)(2,1)S(1)}, bf16[16,7168]{1,0:T(8,128)(2,1)S(1)}, u32[]{:S(2)}, u32[]{:S(2)}) %collective-permute-start.24) | collective-permute-done | bytes 229408 | tf_op jit(solution)/shard_map/ppermute | solution.py:19
  (71 shorter events, 37.9 us)
Async XLA Ops:
  0.7 9.4 %copy-start.8 = (s32[224]{0:T(256)S(1)}, s32[224]{0:T(256)}, u32[]{:S(2)}) copy-start(s32[224]{0:T(256)} %param.7) | copy-start | bytes 2692
  4.1 24.0 %collective-permute-start.2 = (bf16[32,7168]{1,0:T(8,128)(2,1)}, bf16[32,7168]{1,0:T(8,128)(2,1)S(1)}, u32[]{:S(2)}, u32[]{:S(2)}) collective-permute-start(bf16[32,7168]{1,0:T(8,128)(2,1)} %get-tuple-element.123), channel_id=1, source_target_pairs={{0,96},{32,0},{64,32},{96,64},{1,97},{33,1},{65,33},{97,65},{2,98}... | collective-permute-start | bytes 1376264 | tf_op jit(solution)/shard_map/ppermute | solution.py:19
  8.2 23.0 %collective-permute-start = (bf16[32,7168]{1,0:T(8,128)(2,1)S(1)}, bf16[32,7168]{1,0:T(8,128)(2,1)S(1)}, u32[]{:S(2)}, u32[]{:S(2)}) collective-permute-start(bf16[32,7168]{1,0:T(8,128)(2,1)S(1)} %get-tuple-element.124), channel_id=1, source_target_pairs={{0,32},{32,64},{64,96},{96,0},{1,33},{33,65},{65,97},{97,1},{2,34}... | collective-permute-start | bytes 1376264 | tf_op jit(solution)/shard_map/ppermute | solution.py:19
  8.2 23.0 %collective-permute-start.1 = (bf16[32,7168]{1,0:T(8,128)(2,1)S(1)}, bf16[32,7168]{1,0:T(8,128)(2,1)S(1)}, u32[]{:S(2)}, u32[]{:S(2)}) collective-permute-start(bf16[32,7168]{1,0:T(8,128)(2,1)S(1)} %get-tuple-element.130), channel_id=1, source_target_pairs={{0,64},{32,96},{64,0},{96,32},{1,65},{33,97},{65,1},{97,33},{2,66}... | collective-permute-start | bytes 1376264 | tf_op jit(solution)/shard_map/ppermute | solution.py:19
  34.3 35.1 %all-to-all-start = ((bf16[32,32,512]{2,1,0:T(8,128)(2,1)}), bf16[32,32,512]{2,1,0:T(8,128)(2,1)S(1)}, u32[]{:S(2)}, u32[]{:S(2)}) async-start(bf16[32,32,512]{2,1,0:T(8,128)(2,1)} %pack.2), calls=%async_computation | async-start | bytes 2097152 | tf_op jit(solution)/shard_map/all_to_all | solution.py:326
  41.7 24.0 %collective-permute-start.6 = (bf16[32,7168]{1,0:T(8,128)(2,1)}, bf16[32,7168]{1,0:T(8,128)(2,1)S(1)}, u32[]{:S(2)}, u32[]{:S(2)}) collective-permute-start(bf16[32,7168]{1,0:T(8,128)(2,1)} %get-tuple-element.70), channel_id=1, source_target_pairs={{0,32},{32,64},{64,96},{96,0},{1,33},{33,65},{65,97},{97,1},{2,34}... | collective-permute-start | bytes 1376264 | tf_op jit(solution)/shard_map/ppermute | solution.py:19
  41.8 23.9 %collective-permute-start.7 = (bf16[32,7168]{1,0:T(8,128)(2,1)}, bf16[32,7168]{1,0:T(8,128)(2,1)S(1)}, u32[]{:S(2)}, u32[]{:S(2)}) collective-permute-start(bf16[32,7168]{1,0:T(8,128)(2,1)} %get-tuple-element.71), channel_id=1, source_target_pairs={{0,64},{32,96},{64,0},{96,32},{1,65},{33,97},{65,1},{97,33},{2,66}... | collective-permute-start | bytes 1376264 | tf_op jit(solution)/shard_map/ppermute | solution.py:19
  43.7 22.6 %collective-permute-start.8 = (bf16[32,7168]{1,0:T(8,128)(2,1)}, bf16[32,7168]{1,0:T(8,128)(2,1)S(1)}, u32[]{:S(2)}, u32[]{:S(2)}) collective-permute-start(bf16[32,7168]{1,0:T(8,128)(2,1)} %get-tuple-element.72), channel_id=1, source_target_pairs={{0,96},{32,0},{64,32},{96,64},{1,97},{33,1},{65,33},{97,65},{2,98}... | collective-permute-start | bytes 1376264 | tf_op jit(solution)/shard_map/ppermute | solution.py:19
  69.5 24.6 %all-to-all-start.1 = ((bf16[32,32,512]{2,1,0:T(8,128)(2,1)}), bf16[32,32,512]{2,1,0:T(8,128)(2,1)S(1)}, u32[]{:S(2)}, u32[]{:S(2)}) async-start(bf16[32,32,512]{2,1,0:T(8,128)(2,1)} %pack.3), calls=%async_computation.1 | async-start | bytes 2097152 | tf_op jit(solution)/shard_map/all_to_all | solution.py:326
  78.4 9.5 %collective-permute-start.3 = (bf16[3,2,32,512]{3,2,1,0:T(8,128)(2,1)S(1)}, bf16[3,2,32,512]{3,2,1,0:T(8,128)(2,1)S(1)}, u32[]{:S(2)}, u32[]{:S(2)}) collective-permute-start(bf16[3,2,32,512]{3,2,1,0:T(8,128)(2,1)S(1)} %get-tuple-element.66), channel_id=1, source_target_pairs={{0,32},{32,64},{64,96},{96,0},{1,33},{33,65},{65,97},{97,1},{2,34}... | collective-permute-start | bytes 589832 | tf_op jit(solution)/shard_map/ppermute | solution.py:19
  78.7 12.8 %collective-permute-start.4 = (bf16[3,2,32,512]{3,2,1,0:T(8,128)(2,1)S(1)}, bf16[3,2,32,512]{3,2,1,0:T(8,128)(2,1)S(1)}, u32[]{:S(2)}, u32[]{:S(2)}) collective-permute-start(bf16[3,2,32,512]{3,2,1,0:T(8,128)(2,1)S(1)} %get-tuple-element.67), channel_id=1, source_target_pairs={{0,64},{32,96},{64,0},{96,32},{1,65},{33,97},{65,1},{97,33},{2,66}... | collective-permute-start | bytes 589832 | tf_op jit(solution)/shard_map/ppermute | solution.py:19
  82.2 9.3 %collective-permute-start.5 = (bf16[3,2,32,512]{3,2,1,0:T(8,128)(2,1)S(1)}, bf16[3,2,32,512]{3,2,1,0:T(8,128)(2,1)S(1)}, u32[]{:S(2)}, u32[]{:S(2)}) collective-permute-start(bf16[3,2,32,512]{3,2,1,0:T(8,128)(2,1)S(1)} %get-tuple-element.68), channel_id=1, source_target_pairs={{0,96},{32,0},{64,32},{96,64},{1,97},{33,1},{65,33},{97,65},{2,98}... | collective-permute-start | bytes 589832 | tf_op jit(solution)/shard_map/ppermute | solution.py:19
  95.5 8.5 %collective-permute-start.9 = (bf16[3,2,32,512]{3,2,1,0:T(8,128)(2,1)S(1)}, bf16[3,2,32,512]{3,2,1,0:T(8,128)(2,1)S(1)}, u32[]{:S(2)}, u32[]{:S(2)}) collective-permute-start(bf16[3,2,32,512]{3,2,1,0:T(8,128)(2,1)S(1)} %get-tuple-element.81), channel_id=1, source_target_pairs={{0,32},{32,64},{64,96},{96,0},{1,33},{33,65},{65,97},{97,1},{2,34}... | collective-permute-start | bytes 589832 | tf_op jit(solution)/shard_map/ppermute | solution.py:19
  95.8 12.7 %collective-permute-start.10 = (bf16[3,2,32,512]{3,2,1,0:T(8,128)(2,1)S(1)}, bf16[3,2,32,512]{3,2,1,0:T(8,128)(2,1)S(1)}, u32[]{:S(2)}, u32[]{:S(2)}) collective-permute-start(bf16[3,2,32,512]{3,2,1,0:T(8,128)(2,1)S(1)} %get-tuple-element.82), channel_id=1, source_target_pairs={{0,64},{32,96},{64,0},{96,32},{1,65},{33,97},{65,1},{97,33},{2,66}... | collective-permute-start | bytes 589832 | tf_op jit(solution)/shard_map/ppermute | solution.py:19
  99.3 9.2 %collective-permute-start.11 = (bf16[3,2,32,512]{3,2,1,0:T(8,128)(2,1)S(1)}, bf16[3,2,32,512]{3,2,1,0:T(8,128)(2,1)S(1)}, u32[]{:S(2)}, u32[]{:S(2)}) collective-permute-start(bf16[3,2,32,512]{3,2,1,0:T(8,128)(2,1)S(1)} %get-tuple-element.83), channel_id=1, source_target_pairs={{0,96},{32,0},{64,32},{96,64},{1,97},{33,1},{65,33},{97,65},{2,98}... | collective-permute-start | bytes 589832 | tf_op jit(solution)/shard_map/ppermute | solution.py:19
  111.3 9.7 %copy-start.6 = (f32[3,512,512]{2,1,0:T(8,128)S(1)}, f32[3,512,512]{2,1,0:T(8,128)}, u32[]{:S(2)}) copy-start(f32[3,512,512]{2,1,0:T(8,128)} %param.9) | copy-start | bytes 9437188
  116.9 9.8 %collective-permute-start.12 = (bf16[3,2,32,512]{3,2,1,0:T(8,128)(2,1)S(1)}, bf16[3,2,32,512]{3,2,1,0:T(8,128)(2,1)S(1)}, u32[]{:S(2)}, u32[]{:S(2)}) collective-permute-start(bf16[3,2,32,512]{3,2,1,0:T(8,128)(2,1)S(1)} %get-tuple-element.87), channel_id=1, source_target_pairs={{0,32},{32,64},{64,96},{96,0},{1,33},{33,65},{65,97},{97,1},{2,34}... | collective-permute-start | bytes 589832 | tf_op jit(solution)/shard_map/ppermute | solution.py:19
  117.2 12.9 %collective-permute-start.13 = (bf16[3,2,32,512]{3,2,1,0:T(8,128)(2,1)S(1)}, bf16[3,2,32,512]{3,2,1,0:T(8,128)(2,1)S(1)}, u32[]{:S(2)}, u32[]{:S(2)}) collective-permute-start(bf16[3,2,32,512]{3,2,1,0:T(8,128)(2,1)S(1)} %get-tuple-element.88), channel_id=1, source_target_pairs={{0,64},{32,96},{64,0},{96,32},{1,65},{33,97},{65,1},{97,33},{2,66}... | collective-permute-start | bytes 589832 | tf_op jit(solution)/shard_map/ppermute | solution.py:19
  121.0 9.0 %collective-permute-start.14 = (bf16[3,2,32,512]{3,2,1,0:T(8,128)(2,1)S(1)}, bf16[3,2,32,512]{3,2,1,0:T(8,128)(2,1)S(1)}, u32[]{:S(2)}, u32[]{:S(2)}) collective-permute-start(bf16[3,2,32,512]{3,2,1,0:T(8,128)(2,1)S(1)} %get-tuple-element.89), channel_id=1, source_target_pairs={{0,96},{32,0},{64,32},{96,64},{1,97},{33,1},{65,33},{97,65},{2,98}... | collective-permute-start | bytes 589832 | tf_op jit(solution)/shard_map/ppermute | solution.py:19
  131.5 21.8 %all-to-all-start.2 = ((bf16[32,32,512]{2,1,0:T(8,128)(2,1)}), bf16[32,32,512]{2,1,0:T(8,128)(2,1)S(1)}, u32[]{:S(2)}, u32[]{:S(2)}) async-start(bf16[32,32,512]{2,1,0:T(8,128)(2,1)} %bitcast.12), calls=%async_computation.2 | async-start | bytes 2097152 | tf_op jit(solution)/shard_map/all_to_all | solution.py:326
  136.0 8.6 %collective-permute-start.15 = (bf16[3,2,32,512]{3,2,1,0:T(8,128)(2,1)S(1)}, bf16[3,2,32,512]{3,2,1,0:T(8,128)(2,1)S(1)}, u32[]{:S(2)}, u32[]{:S(2)}) collective-permute-start(bf16[3,2,32,512]{3,2,1,0:T(8,128)(2,1)S(1)} %get-tuple-element.103), channel_id=1, source_target_pairs={{0,32},{32,64},{64,96},{96,0},{1,33},{33,65},{65,97},{97,1},{2,34}... | collective-permute-start | bytes 589832 | tf_op jit(solution)/shard_map/ppermute | solution.py:19
  136.1 12.9 %collective-permute-start.16 = (bf16[3,2,32,512]{3,2,1,0:T(8,128)(2,1)S(1)}, bf16[3,2,32,512]{3,2,1,0:T(8,128)(2,1)S(1)}, u32[]{:S(2)}, u32[]{:S(2)}) collective-permute-start(bf16[3,2,32,512]{3,2,1,0:T(8,128)(2,1)S(1)} %get-tuple-element.104), channel_id=1, source_target_pairs={{0,64},{32,96},{64,0},{96,32},{1,65},{33,97},{65,1},{97,33},{2,66}... | collective-permute-start | bytes 589832 | tf_op jit(solution)/shard_map/ppermute | solution.py:19
  139.6 9.5 %collective-permute-start.17 = (bf16[3,2,32,512]{3,2,1,0:T(8,128)(2,1)S(1)}, bf16[3,2,32,512]{3,2,1,0:T(8,128)(2,1)S(1)}, u32[]{:S(2)}, u32[]{:S(2)}) collective-permute-start(bf16[3,2,32,512]{3,2,1,0:T(8,128)(2,1)S(1)} %get-tuple-element.105), channel_id=1, source_target_pairs={{0,96},{32,0},{64,32},{96,64},{1,97},{33,1},{65,33},{97,65},{2,98}... | collective-permute-start | bytes 589832 | tf_op jit(solution)/shard_map/ppermute | solution.py:19
  154.4 21.9 %all-to-all-start.3 = ((bf16[32,32,512]{2,1,0:T(8,128)(2,1)}), bf16[32,32,512]{2,1,0:T(8,128)(2,1)S(1)}, u32[]{:S(2)}, u32[]{:S(2)}) async-start(bf16[32,32,512]{2,1,0:T(8,128)(2,1)} %bitcast.13), calls=%async_computation.3 | async-start | bytes 2097152 | tf_op jit(solution)/shard_map/all_to_all | solution.py:326
  159.0 14.0 %collective-permute-start.19 = (bf16[32,7168]{1,0:T(8,128)(2,1)S(1)}, bf16[32,7168]{1,0:T(8,128)(2,1)S(1)}, u32[]{:S(2)}, u32[]{:S(2)}) collective-permute-start(bf16[32,7168]{1,0:T(8,128)(2,1)S(1)} %unpack.2.refs_0_), channel_id=1, source_target_pairs={{0,32},{32,64},{64,96},{96,0},{1,33},{33,65},{65,97},{97,1},{2,34}... | collective-permute-start | bytes 1376264 | tf_op jit(solution)/shard_map/ppermute | solution.py:19
  159.3 13.7 %collective-permute-start.18 = (bf16[32,7168]{1,0:T(8,128)(2,1)S(1)}, bf16[32,7168]{1,0:T(8,128)(2,1)S(1)}, u32[]{:S(2)}, u32[]{:S(2)}) collective-permute-start(bf16[32,7168]{1,0:T(8,128)(2,1)S(1)} %unpack.2.refs_0_), channel_id=1, source_target_pairs={{0,96},{32,0},{64,32},{96,64},{1,97},{33,1},{65,33},{97,65},{2,98}... | collective-permute-start | bytes 1376264 | tf_op jit(solution)/shard_map/ppermute | solution.py:19
  177.5 21.5 %collective-permute-start.21 = (bf16[32,7168]{1,0:T(8,128)(2,1)S(1)}, bf16[32,7168]{1,0:T(8,128)(2,1)S(1)}, u32[]{:S(2)}, u32[]{:S(2)}) collective-permute-start(bf16[32,7168]{1,0:T(8,128)(2,1)S(1)} %unpack.3.refs_0_), channel_id=1, source_target_pairs={{0,32},{32,64},{64,96},{96,0},{1,33},{33,65},{65,97},{97,1},{2,34}... | collective-permute-start | bytes 1376264 | tf_op jit(solution)/shard_map/ppermute | solution.py:19
  177.8 21.2 %collective-permute-start.20 = (bf16[32,7168]{1,0:T(8,128)(2,1)S(1)}, bf16[32,7168]{1,0:T(8,128)(2,1)S(1)}, u32[]{:S(2)}, u32[]{:S(2)}) collective-permute-start(bf16[32,7168]{1,0:T(8,128)(2,1)S(1)} %unpack.3.refs_0_), channel_id=1, source_target_pairs={{0,96},{32,0},{64,32},{96,64},{1,97},{33,1},{65,33},{97,65},{2,98}... | collective-permute-start | bytes 1376264 | tf_op jit(solution)/shard_map/ppermute | solution.py:19
  180.8 15.4 %collective-permute-start.22 = (bf16[16,7168]{1,0:T(8,128)(2,1)S(1)}, bf16[16,7168]{1,0:T(8,128)(2,1)S(1)}, u32[]{:S(2)}, u32[]{:S(2)}) collective-permute-start(bf16[16,7168]{1,0:T(8,128)(2,1)S(1)} %slice.16), channel_id=1, source_target_pairs={{0,32},{32,64},{64,96},{96,0},{1,33},{33,65},{65,97},{97,1},{2,34}... | collective-permute-start | bytes 688136 | tf_op jit(solution)/shard_map/ppermute | solution.py:19
  180.9 15.3 %collective-permute-start.23 = (bf16[16,7168]{1,0:T(8,128)(2,1)S(1)}, bf16[16,7168]{1,0:T(8,128)(2,1)S(1)}, u32[]{:S(2)}, u32[]{:S(2)}) collective-permute-start(bf16[16,7168]{1,0:T(8,128)(2,1)S(1)} %slice.17), channel_id=1, source_target_pairs={{0,96},{32,0},{64,32},{96,64},{1,97},{33,1},{65,33},{97,65},{2,98}... | collective-permute-start | bytes 688136 | tf_op jit(solution)/shard_map/ppermute | solution.py:19
  199.0 7.0 %collective-permute-start.25 = (bf16[16,7168]{1,0:T(8,128)(2,1)S(1)}, bf16[16,7168]{1,0:T(8,128)(2,1)S(1)}, u32[]{:S(2)}, u32[]{:S(2)}) collective-permute-start(bf16[16,7168]{1,0:T(8,128)(2,1)S(1)} %slice.19), channel_id=1, source_target_pairs={{0,96},{32,0},{64,32},{96,64},{1,97},{33,1},{65,33},{97,65},{2,98}... | collective-permute-start | bytes 688136 | tf_op jit(solution)/shard_map/ppermute | solution.py:19
  202.0 7.4 %collective-permute-start.24 = (bf16[16,7168]{1,0:T(8,128)(2,1)S(1)}, bf16[16,7168]{1,0:T(8,128)(2,1)S(1)}, u32[]{:S(2)}, u32[]{:S(2)}) collective-permute-start(bf16[16,7168]{1,0:T(8,128)(2,1)S(1)} %slice.18), channel_id=1, source_target_pairs={{0,32},{32,64},{64,96},{96,0},{1,33},{33,65},{65,97},{97,1},{2,34}... | collective-permute-start | bytes 688136 | tf_op jit(solution)/shard_map/ppermute | solution.py:19
  (7 other events, 10.8 us)

commit v7 on v5

--- a/solution.py
+++ b/solution.py
@@ -12,6 +12,7 @@
 ANY = pl.BlockSpec(memory_space=pl.ANY)
 SMEM = pl.BlockSpec(memory_space=pltpu.SMEM)
 HBM = pl.BlockSpec(memory_space=pltpu.HBM)
+VMEM = pl.BlockSpec(memory_space=pltpu.VMEM)
 
 
 def shift(x, step):
@@ -145,9 +146,9 @@
 
 
 def precondition_kernel(chunk_pieces, used_ref, me_ref, *refs):
-    pieces, (left_ref, right_ref, grad_ref) = refs[:chunk_pieces], refs[chunk_pieces : chunk_pieces + 3]
+    pieces, (left, right, grad_ref) = refs[:chunk_pieces], refs[chunk_pieces : chunk_pieces + 3]
     outs = refs[chunk_pieces + 3 : 2 * chunk_pieces + 3]
-    grad, left, right, update, in_sems, root_sems, grad_sems, out_sems = refs[2 * chunk_pieces + 3 :]
+    grad, update, in_sems, grad_sems, out_sems = refs[2 * chunk_pieces + 3 :]
     slots, _, _, count = grad.shape[:4]
     block = left.shape[1]
     me = me_ref[0]
@@ -155,25 +156,13 @@
         pltpu.make_async_copy(piece, grad.at[:, :, i // count, (me + count - i % count) % count], in_sems.at[i])
         for i, piece in enumerate(pieces)
     ]
-    roots = [
-        (
-            pltpu.make_async_copy(left_ref.at[s], left.at[s], root_sems.at[0, s]),
-            pltpu.make_async_copy(right_ref.at[s], right.at[s], root_sems.at[1, s]),
-        )
-        for s in range(slots)
-    ]
-    for pair in roots:
-        for copy in pair:
-            copy.start()
     run_all(loads)
     stores = []
     for s in range(slots):
         whole = grad[s].reshape(block, block)
         whole = jnp.where(used_ref[s] > 0, whole, jnp.zeros_like(whole))
         grad[s] = whole.reshape(grad.shape[1:])
-        roots[s][0].wait()
         part = jnp.dot(left[s], whole, preferred_element_type=jnp.float32).astype(whole.dtype)
-        roots[s][1].wait()
         result = jnp.dot(part, right[s], preferred_element_type=jnp.float32).astype(whole.dtype)
         update[s] = result.reshape(update.shape[1:])
         sends = [pltpu.make_async_copy(grad.at[s], grad_ref.at[s], grad_sems.at[s])] + [
@@ -196,15 +185,12 @@
     grad, *outs = pl.pallas_call(
         functools.partial(precondition_kernel, total),
         out_shape=[jax.ShapeDtypeStruct(layout, dtype)] + [jax.ShapeDtypeStruct(pieces[0].shape, dtype)] * total,
-        in_specs=[SMEM, SMEM] + [ANY] * total + [HBM] * 2,
+        in_specs=[SMEM, SMEM] + [ANY] * total + [VMEM] * 2,
         out_specs=[ANY] * (total + 1),
         scratch_shapes=[
             pltpu.VMEM(layout, dtype),
-            pltpu.VMEM(root_left.shape, dtype),
-            pltpu.VMEM(root_right.shape, dtype),
             pltpu.VMEM(layout, dtype),
             pltpu.SemaphoreType.DMA((total,)),
-            pltpu.SemaphoreType.DMA((2, slots)),
             pltpu.SemaphoreType.DMA((slots,)),
             pltpu.SemaphoreType.DMA((slots, total)),
         ],
@@ -398,8 +384,7 @@
 
     near = spread(first_own)
     far = spread_far(*near)
-    far, second_in = lax.optimization_barrier((far, second_in))
-    second_own = unpack(my_column, second_in)
+    far, second_own = lax.optimization_barrier((far, unpack(my_column, second_in)))
     updates = place(me, (first_own, *near), far, None, 0, quarter, shard_rows)
     near = spread(second_own)
     near, updates = lax.optimization_barrier((near, updates))

time: 204 us -> 201 us (0.985)
  transfers between devices with their start and end apart: 30 -> 30, of which waited for: 21 -> 22; matrix products, arithmetic and copies ran while one was open for 4% -> 4% of each run, Pallas kernels for 5% -> 6%
where the time goes in v7:
time: 201 us
  waiting for transfers between devices  100 us (50%)
  starting transfers between devices  61.1 us (30%)
  Pallas kernels  24 us (12%)
  matrix products  5.66 us (3%)
  local copies, waits for them, and re-layouts  5.59 us (3%)
  other arithmetic  3.11 us (2%)
    ppermute x26, waiting for transfers between devices, shift(): lax.ppermute(x, 'dp', [(i, (i + step) % count) for i in range(count)])  94.4 us
    ppermute x26, starting transfers between devices, shift(): lax.ppermute(x, 'dp', [(i, (i + step) % count) for i in range(count)])  37.5 us
    all_to_all x4, starting transfers between devices, expert_exchange(): return lax.all_to_all(x, 'expert', split_axis=0, concat_axis=0, tiled=True)  23.6 us
    pallas_call x3, Pallas kernels, place(): pl.pallas_call(functools.partial(place_kernel, base, quarter, places), ou...  5.99 us
    all_to_all x4, waiting for transfers between devices, expert_exchange(): return lax.all_to_all(x, 'expert', split_axis=0, concat_axis=0, tiled=True)  5.75 us
    pallas_call x2, Pallas kernels, pack(): pl.pallas_call(pack_kernel, out_shape=jax.ShapeDtypeStruct((dests, rows,...  5.55 us
    pallas_call x1, Pallas kernels, precondition(): pl.pallas_call(functools.partial(precondition_kernel, total), out_shape=[...  4.64 us
  transfers between devices with their start and end apart: 30, of which 22 were waited for; matrix products, arithmetic and copies ran while one was open for 4% of the time, Pallas kernels for 6%

profile of v7, /device:TPU:0, one launch (start us, length us, event | category | flops | bytes accessed | tf_op | source)
XLA Modules:
  0.0 200.8 jit_solution(11842088453982208673)
XLA Ops:
  2.1 4.2 %collective-permute-start = (bf16[32,7168]{1,0:T(8,128)(2,1)S(1)}, bf16[32,7168]{1,0:T(8,128)(2,1)S(1)}, u32[]{:S(2)}, u32[]{:S(2)}) collective-permute-start(bf16[32,7168]{1,0:T(8,128)(2,1)S(1)} %pad_maximum_fusion), channel_id=1, source_target_pairs={{0,96},{32,0},{64,32},{96,64},{1,97},{33,1},{65,33},{97,65},{2,98}... | collective-permute-start | bytes 1376264 | tf_op jit(solution)/shard_map/ppermute | solution.py:20
  6.4 9.6 %collective-permute-done = bf16[32,7168]{1,0:T(8,128)(2,1)S(1)} collective-permute-done((bf16[32,7168]{1,0:T(8,128)(2,1)S(1)}, bf16[32,7168]{1,0:T(8,128)(2,1)S(1)}, u32[]{:S(2)}, u32[]{:S(2)}) %collective-permute-start) | collective-permute-done | bytes 458784 | tf_op jit(solution)/shard_map/ppermute | solution.py:20
  16.1 3.5 %collective-permute-done.1 = bf16[32,7168]{1,0:T(8,128)(2,1)S(1)} collective-permute-done((bf16[32,7168]{1,0:T(8,128)(2,1)S(1)}, bf16[32,7168]{1,0:T(8,128)(2,1)S(1)}, u32[]{:S(2)}, u32[]{:S(2)}) %collective-permute-start.1) | collective-permute-done | bytes 458784 | tf_op jit(solution)/shard_map/ppermute | solution.py:20
  22.3 3.2 %collective-permute-start.2 = (bf16[32,7168]{1,0:T(8,128)(2,1)S(1)}, bf16[32,7168]{1,0:T(8,128)(2,1)S(1)}, u32[]{:S(2)}, u32[]{:S(2)}) collective-permute-start(bf16[32,7168]{1,0:T(8,128)(2,1)S(1)} %get-tuple-element.108), channel_id=1, source_target_pairs={{0,96},{32,0},{64,32},{96,64},{1,97},{33,1},{65,33},{97,65},{2,98}... | collective-permute-start | bytes 1376264 | tf_op jit(solution)/shard_map/ppermute | solution.py:20
  27.0 7.6 %collective-permute-done.3.prev_ref = bf16[32,7168]{1,0:T(8,128)(2,1)S(1)} collective-permute-done((bf16[32,7168]{1,0:T(8,128)(2,1)S(1)}, bf16[32,7168]{1,0:T(8,128)(2,1)S(1)}, u32[]{:S(2)}, u32[]{:S(2)}) %collective-permute-start.3) | collective-permute-done | bytes 458784 | tf_op jit(solution)/shard_map/ppermute | solution.py:20
  34.6 2.8 %pack.2 = bf16[32,32,512]{2,1,0:T(8,128)(2,1)} custom-call(s32[32]{0:T(128)S(1)} %select_reduce_fusion.index_ref, bf16[32,7168]{1,0:T(8,128)(2,1)S(1)} %get-tuple-element.106.own_ref, bf16[32,7168]{1,0:T(8,128)(2,1)S(1)} %collective-permute-done.2.next_ref, bf16[32,7168]{1,0:T(8,128)(2,1)S(1)} %collective-permute-done.3.prev_ref), custom_call_target="tpu_custom_call" | custom-call | bytes 2883584 | tf_op jit(solution)/shard_map/pack/pallas_call | solution.py:68
  37.4 7.3 %all-to-all-start = ((bf16[32,32,512]{2,1,0:T(8,128)(2,1)}), bf16[32,32,512]{2,1,0:T(8,128)(2,1)S(1)}, u32[]{:S(2)}, u32[]{:S(2)}) async-start(bf16[32,32,512]{2,1,0:T(8,128)(2,1)} %pack.2), calls=%async_computation | async-start | bytes 2097152 | tf_op jit(solution)/shard_map/all_to_all | solution.py:293
  44.7 3.0 %collective-permute-start.7 = (bf16[32,7168]{1,0:T(8,128)(2,1)}, bf16[32,7168]{1,0:T(8,128)(2,1)S(1)}, u32[]{:S(2)}, u32[]{:S(2)}) collective-permute-start(bf16[32,7168]{1,0:T(8,128)(2,1)} %get-tuple-element.57), channel_id=1, source_target_pairs={{0,96},{32,0},{64,32},{96,64},{1,97},{33,1},{65,33},{97,65},{2,98}... | collective-permute-start | bytes 1376264 | tf_op jit(solution)/shard_map/ppermute | solution.py:20
  47.7 10.5 %collective-permute-done.7.next_ref = bf16[32,7168]{1,0:T(8,128)(2,1)S(1)} collective-permute-done((bf16[32,7168]{1,0:T(8,128)(2,1)}, bf16[32,7168]{1,0:T(8,128)(2,1)S(1)}, u32[]{:S(2)}, u32[]{:S(2)}) %collective-permute-start.7) | collective-permute-done | bytes 458784 | tf_op jit(solution)/shard_map/ppermute | solution.py:20
  58.3 3.3 %collective-permute-done.8.prev_ref = bf16[32,7168]{1,0:T(8,128)(2,1)S(1)} collective-permute-done((bf16[32,7168]{1,0:T(8,128)(2,1)}, bf16[32,7168]{1,0:T(8,128)(2,1)S(1)}, u32[]{:S(2)}, u32[]{:S(2)}) %collective-permute-start.8) | collective-permute-done | bytes 458784 | tf_op jit(solution)/shard_map/ppermute | solution.py:20
  61.6 2.8 %pack.3 = bf16[32,32,512]{2,1,0:T(8,128)(2,1)} custom-call(s32[32]{0:T(128)S(1)} %select_reduce_fusion.index_ref, bf16[32,7168]{1,0:T(8,128)(2,1)S(1)} %get-tuple-element.105.own_ref, bf16[32,7168]{1,0:T(8,128)(2,1)S(1)} %collective-permute-done.7.next_ref, bf16[32,7168]{1,0:T(8,128)(2,1)S(1)} %collective-permute-done.8.prev_ref), custom_call_target="tpu_custom_call" | custom-call | bytes 2883584 | tf_op jit(solution)/shard_map/pack/pallas_call | solution.py:68
  64.4 7.3 %all-to-all-start.1 = ((bf16[32,32,512]{2,1,0:T(8,128)(2,1)}), bf16[32,32,512]{2,1,0:T(8,128)(2,1)S(1)}, u32[]{:S(2)}, u32[]{:S(2)}) async-start(bf16[32,32,512]{2,1,0:T(8,128)(2,1)} %pack.3), calls=%async_computation.1 | async-start | bytes 2097152 | tf_op jit(solution)/shard_map/all_to_all | solution.py:293
  76.6 9.3 %collective-permute-done.4.refs_1_ = bf16[3,2,32,512]{3,2,1,0:T(8,128)(2,1)S(1)} collective-permute-done((bf16[3,2,32,512]{3,2,1,0:T(8,128)(2,1)S(1)}, bf16[3,2,32,512]{3,2,1,0:T(8,128)(2,1)S(1)}, u32[]{:S(2)}, u32[]{:S(2)}) %collective-permute-start.4) | collective-permute-done | bytes 196640 | tf_op jit(solution)/shard_map/ppermute | solution.py:20
  93.7 9.1 %collective-permute-done.9.refs_5_ = bf16[3,2,32,512]{3,2,1,0:T(8,128)(2,1)S(1)} collective-permute-done((bf16[3,2,32,512]{3,2,1,0:T(8,128)(2,1)S(1)}, bf16[3,2,32,512]{3,2,1,0:T(8,128)(2,1)S(1)}, u32[]{:S(2)}, u32[]{:S(2)}) %collective-permute-start.9) | collective-permute-done | bytes 196640 | tf_op jit(solution)/shard_map/ppermute | solution.py:20
  106.2 4.6 %precondition.1 = (bf16[3,2,2,4,32,512]{5,4,3,2,1,0:T(8,128)(2,1)S(1)}, bf16[3,2,32,512]{3,2,1,0:T(8,128)(2,1)S(1)}, bf16[3,2,32,512]{3,2,1,0:T(8,128)(2,1)S(1)}...) custom-call(s32[3]{0:T(128)S(1)} %bitcast.39, ...), custom_call_target="tpu_custom_call" | custom-call | flops 1610612736 | bytes 7864320 | tf_op jit(solution)/shard_map/precondition/pallas_call | solution.py:185
  111.2 3.6 %collective-permute-start.13 = (bf16[3,2,32,512]{3,2,1,0:T(8,128)(2,1)S(1)}, bf16[3,2,32,512]{3,2,1,0:T(8,128)(2,1)S(1)}, u32[]{:S(2)}, u32[]{:S(2)}) collective-permute-start(bf16[3,2,32,512]{3,2,1,0:T(8,128)(2,1)S(1)} %get-tuple-element.70), channel_id=1, source_target_pairs={{0,64},{32,96},{64,0},{96,32},{1,65},{33,97},{65,1},{97,33},{2,66}... | collective-permute-start | bytes 589832 | tf_op jit(solution)/shard_map/ppermute | solution.py:20
  114.7 2.9 %multiply_add_fusion = f32[3,512,512]{2,1,0:T(8,128)} fusion(f32[3,512,512]{2,1,0:T(8,128)S(1)} %copy-done.2, bf16[3,512,512]{2,1,0:T(8,128)(2,1)S(1)} %bitcast.35), kind=kOutput, calls=%fused_computation | convolution fusion | flops 807665664 | bytes 7864320 | tf_op jit(solution)/shard_map/sji,sjk->sik/dot_general | solution.py:373
  117.6 2.8 %multiply_add_fusion.1 = f32[3,512,512]{2,1,0:T(8,128)} fusion(f32[3,512,512]{2,1,0:T(8,128)S(1)} %copy-done.3, bf16[3,512,512]{2,1,0:T(8,128)(2,1)S(1)} %bitcast.36), kind=kOutput, calls=%fused_computation.1 | convolution fusion | flops 807665664 | bytes 7864320 | tf_op jit(solution)/shard_map/sij,skj->sik/dot_general | solution.py:372
  120.4 3.0 %collective-permute-done.13.refs_2_ = bf16[3,2,32,512]{3,2,1,0:T(8,128)(2,1)S(1)} collective-permute-done((bf16[3,2,32,512]{3,2,1,0:T(8,128)(2,1)S(1)}, bf16[3,2,32,512]{3,2,1,0:T(8,128)(2,1)S(1)}, u32[]{:S(2)}, u32[]{:S(2)}) %collective-permute-start.13) | collective-permute-done | bytes 196640 | tf_op jit(solution)/shard_map/ppermute | solution.py:20
  124.9 4.5 %all-to-all-start.2 = ((bf16[32,32,512]{2,1,0:T(8,128)(2,1)}), bf16[32,32,512]{2,1,0:T(8,128)(2,1)S(1)}, u32[]{:S(2)}, u32[]{:S(2)}) async-start(bf16[32,32,512]{2,1,0:T(8,128)(2,1)} %bitcast.14), calls=%async_computation.2 | async-start | bytes 2097152 | tf_op jit(solution)/shard_map/all_to_all | solution.py:293
  129.6 3.4 %collective-permute-start.16 = (bf16[3,2,32,512]{3,2,1,0:T(8,128)(2,1)S(1)}, bf16[3,2,32,512]{3,2,1,0:T(8,128)(2,1)S(1)}, u32[]{:S(2)}, u32[]{:S(2)}) collective-permute-start(bf16[3,2,32,512]{3,2,1,0:T(8,128)(2,1)S(1)} %get-tuple-element.86), channel_id=1, source_target_pairs={{0,64},{32,96},{64,0},{96,32},{1,65},{33,97},{65,1},{97,33},{2,66}... | collective-permute-start | bytes 589832 | tf_op jit(solution)/shard_map/ppermute | solution.py:20
  133.0 4.9 %collective-permute-done.15.refs_1_ = bf16[3,2,32,512]{3,2,1,0:T(8,128)(2,1)S(1)} collective-permute-done((bf16[3,2,32,512]{3,2,1,0:T(8,128)(2,1)S(1)}, bf16[3,2,32,512]{3,2,1,0:T(8,128)(2,1)S(1)}, u32[]{:S(2)}, u32[]{:S(2)}) %collective-permute-start.15) | collective-permute-done | bytes 196640 | tf_op jit(solution)/shard_map/ppermute | solution.py:20
  138.0 4.3 %collective-permute-done.16.refs_2_ = bf16[3,2,32,512]{3,2,1,0:T(8,128)(2,1)S(1)} collective-permute-done((bf16[3,2,32,512]{3,2,1,0:T(8,128)(2,1)S(1)}, bf16[3,2,32,512]{3,2,1,0:T(8,128)(2,1)S(1)}, u32[]{:S(2)}, u32[]{:S(2)}) %collective-permute-start.16) | collective-permute-done | bytes 196640 | tf_op jit(solution)/shard_map/ppermute | solution.py:20
  144.0 2.7 %all-to-all-done.2.pieces_ref = bf16[32,32,512]{2,1,0:T(8,128)(2,1)S(1)} async-done(((bf16[32,32,512]{2,1,0:T(8,128)(2,1)}), bf16[32,32,512]{2,1,0:T(8,128)(2,1)S(1)}, u32[]{:S(2)}, u32[]{:S(2)}) %all-to-all-start.2) | async-done | bytes 1048608 | tf_op jit(solution)/shard_map/all_to_all | solution.py:293
  147.8 4.6 %all-to-all-start.3 = ((bf16[32,32,512]{2,1,0:T(8,128)(2,1)}), bf16[32,32,512]{2,1,0:T(8,128)(2,1)S(1)}, u32[]{:S(2)}, u32[]{:S(2)}) async-start(bf16[32,32,512]{2,1,0:T(8,128)(2,1)} %bitcast.15), calls=%async_computation.3 | async-start | bytes 2097152 | tf_op jit(solution)/shard_map/all_to_all | solution.py:293
  155.1 10.2 %collective-permute-done.20.refs_1_ = bf16[32,7168]{1,0:T(8,128)(2,1)S(1)} collective-permute-done((bf16[32,7168]{1,0:T(8,128)(2,1)S(1)}, bf16[32,7168]{1,0:T(8,128)(2,1)S(1)}, u32[]{:S(2)}, u32[]{:S(2)}) %collective-permute-start.20) | collective-permute-done | bytes 458784 | tf_op jit(solution)/shard_map/ppermute | solution.py:20
  165.3 3.8 %collective-permute-start.21 = (bf16[16,7168]{1,0:T(8,128)(2,1)S(1)}, bf16[16,7168]{1,0:T(8,128)(2,1)S(1)}, u32[]{:S(2)}, u32[]{:S(2)}) collective-permute-start(bf16[16,7168]{1,0:T(8,128)(2,1)S(1)} %slice.38), channel_id=1, source_target_pairs={{0,96},{32,0},{64,32},{96,64},{1,97},{33,1},{65,33},{97,65},{2,98}... | collective-permute-start | bytes 688136 | tf_op jit(solution)/shard_map/ppermute | solution.py:20
  173.6 3.5 %collective-permute-done.19.refs_3_ = bf16[16,7168]{1,0:T(8,128)(2,1)S(1)} collective-permute-done((bf16[16,7168]{1,0:T(8,128)(2,1)S(1)}, bf16[16,7168]{1,0:T(8,128)(2,1)S(1)}, u32[]{:S(2)}, u32[]{:S(2)}) %collective-permute-start.19) | collective-permute-done | bytes 229408 | tf_op jit(solution)/shard_map/ppermute | solution.py:20
  177.1 3.2 %collective-permute-start.22 = (bf16[32,7168]{1,0:T(8,128)(2,1)S(1)}, bf16[32,7168]{1,0:T(8,128)(2,1)S(1)}, u32[]{:S(2)}, u32[]{:S(2)}) collective-permute-start(bf16[32,7168]{1,0:T(8,128)(2,1)S(1)} %unpack.3.refs_0_), channel_id=1, source_target_pairs={{0,96},{32,0},{64,32},{96,64},{1,97},{33,1},{65,33},{97,65},{2,98}... | collective-permute-start | bytes 1376264 | tf_op jit(solution)/shard_map/ppermute | solution.py:20
  183.0 6.0 %collective-permute-done.23.refs_2_ = bf16[32,7168]{1,0:T(8,128)(2,1)S(1)} collective-permute-done((bf16[32,7168]{1,0:T(8,128)(2,1)S(1)}, bf16[32,7168]{1,0:T(8,128)(2,1)S(1)}, u32[]{:S(2)}, u32[]{:S(2)}) %collective-permute-start.23) | collective-permute-done | bytes 458784 | tf_op jit(solution)/shard_map/ppermute | solution.py:20
  189.0 3.0 %collective-permute-start.25 = (bf16[16,7168]{1,0:T(8,128)(2,1)S(1)}, bf16[16,7168]{1,0:T(8,128)(2,1)S(1)}, u32[]{:S(2)}, u32[]{:S(2)}) collective-permute-start(bf16[16,7168]{1,0:T(8,128)(2,1)S(1)} %slice.33), channel_id=1, source_target_pairs={{0,96},{32,0},{64,32},{96,64},{1,97},{33,1},{65,33},{97,65},{2,98}... | collective-permute-start | bytes 688136 | tf_op jit(solution)/shard_map/ppermute | solution.py:20
  195.6 3.7 %collective-permute-done.24.refs_0_ = bf16[16,7168]{1,0:T(8,128)(2,1)S(1)} collective-permute-done((bf16[16,7168]{1,0:T(8,128)(2,1)S(1)}, bf16[16,7168]{1,0:T(8,128)(2,1)S(1)}, u32[]{:S(2)}, u32[]{:S(2)}) %collective-permute-start.24) | collective-permute-done | bytes 229408 | tf_op jit(solution)/shard_map/ppermute | solution.py:20
  (70 shorter events, 41.4 us)
Async XLA Ops:
  0.6 19.0 %copy-start.5 = (pred[32]{0:T(512)(128)(4,1)S(1)}, pred[32]{0:T(512)(128)(4,1)}, u32[]{:S(2)}) copy-start(pred[32]{0:T(512)(128)(4,1)} %constant.146.clone.1) | copy-start | bytes 100
  2.1 14.0 %collective-permute-start = (bf16[32,7168]{1,0:T(8,128)(2,1)S(1)}, bf16[32,7168]{1,0:T(8,128)(2,1)S(1)}, u32[]{:S(2)}, u32[]{:S(2)}) collective-permute-start(bf16[32,7168]{1,0:T(8,128)(2,1)S(1)} %pad_maximum_fusion), channel_id=1, source_target_pairs={{0,96},{32,0},{64,32},{96,64},{1,97},{33,1},{65,33},{97,65},{2,98}... | collective-permute-start | bytes 1376264 | tf_op jit(solution)/shard_map/ppermute | solution.py:20
  6.3 13.3 %collective-permute-start.1 = (bf16[32,7168]{1,0:T(8,128)(2,1)S(1)}, bf16[32,7168]{1,0:T(8,128)(2,1)S(1)}, u32[]{:S(2)}, u32[]{:S(2)}) collective-permute-start(bf16[32,7168]{1,0:T(8,128)(2,1)S(1)} %pad_maximum_fusion.1), channel_id=1, source_target_pairs={{0,32},{32,64},{64,96},{96,0},{1,33},{33,65},{65,97},{97,1},{2,34}... | collective-permute-start | bytes 1376264 | tf_op jit(solution)/shard_map/ppermute | solution.py:20
  22.3 12.3 %collective-permute-start.3 = (bf16[32,7168]{1,0:T(8,128)(2,1)S(1)}, bf16[32,7168]{1,0:T(8,128)(2,1)S(1)}, u32[]{:S(2)}, u32[]{:S(2)}) collective-permute-start(bf16[32,7168]{1,0:T(8,128)(2,1)S(1)} %get-tuple-element.107), channel_id=1, source_target_pairs={{0,32},{32,64},{64,96},{96,0},{1,33},{33,65},{65,97},{97,1},{2,34}... | collective-permute-start | bytes 1376264 | tf_op jit(solution)/shard_map/ppermute | solution.py:20
  22.3 12.3 %collective-permute-start.2 = (bf16[32,7168]{1,0:T(8,128)(2,1)S(1)}, bf16[32,7168]{1,0:T(8,128)(2,1)S(1)}, u32[]{:S(2)}, u32[]{:S(2)}) collective-permute-start(bf16[32,7168]{1,0:T(8,128)(2,1)S(1)} %get-tuple-element.108), channel_id=1, source_target_pairs={{0,96},{32,0},{64,32},{96,64},{1,97},{33,1},{65,33},{97,65},{2,98}... | collective-permute-start | bytes 1376264 | tf_op jit(solution)/shard_map/ppermute | solution.py:20
  37.4 27.0 %all-to-all-start = ((bf16[32,32,512]{2,1,0:T(8,128)(2,1)}), bf16[32,32,512]{2,1,0:T(8,128)(2,1)S(1)}, u32[]{:S(2)}, u32[]{:S(2)}) async-start(bf16[32,32,512]{2,1,0:T(8,128)(2,1)} %pack.2), calls=%async_computation | async-start | bytes 2097152 | tf_op jit(solution)/shard_map/all_to_all | solution.py:293
  44.7 13.6 %collective-permute-start.7 = (bf16[32,7168]{1,0:T(8,128)(2,1)}, bf16[32,7168]{1,0:T(8,128)(2,1)S(1)}, u32[]{:S(2)}, u32[]{:S(2)}) collective-permute-start(bf16[32,7168]{1,0:T(8,128)(2,1)} %get-tuple-element.57), channel_id=1, source_target_pairs={{0,96},{32,0},{64,32},{96,64},{1,97},{33,1},{65,33},{97,65},{2,98}... | collective-permute-start | bytes 1376264 | tf_op jit(solution)/shard_map/ppermute | solution.py:20
  47.7 13.8 %collective-permute-start.8 = (bf16[32,7168]{1,0:T(8,128)(2,1)}, bf16[32,7168]{1,0:T(8,128)(2,1)S(1)}, u32[]{:S(2)}, u32[]{:S(2)}) collective-permute-start(bf16[32,7168]{1,0:T(8,128)(2,1)} %get-tuple-element.58), channel_id=1, source_target_pairs={{0,32},{32,64},{64,96},{96,0},{1,33},{33,65},{65,97},{97,1},{2,34}... | collective-permute-start | bytes 1376264 | tf_op jit(solution)/shard_map/ppermute | solution.py:20
  64.4 24.6 %all-to-all-start.1 = ((bf16[32,32,512]{2,1,0:T(8,128)(2,1)}), bf16[32,32,512]{2,1,0:T(8,128)(2,1)S(1)}, u32[]{:S(2)}, u32[]{:S(2)}) async-start(bf16[32,32,512]{2,1,0:T(8,128)(2,1)} %pack.3), calls=%async_computation.1 | async-start | bytes 2097152 | tf_op jit(solution)/shard_map/all_to_all | solution.py:293
  73.3 12.6 %collective-permute-start.4 = (bf16[3,2,32,512]{3,2,1,0:T(8,128)(2,1)S(1)}, bf16[3,2,32,512]{3,2,1,0:T(8,128)(2,1)S(1)}, u32[]{:S(2)}, u32[]{:S(2)}) collective-permute-start(bf16[3,2,32,512]{3,2,1,0:T(8,128)(2,1)S(1)} %get-tuple-element.54), channel_id=1, source_target_pairs={{0,32},{32,64},{64,96},{96,0},{1,33},{33,65},{65,97},{97,1},{2,34}... | collective-permute-start | bytes 589832 | tf_op jit(solution)/shard_map/ppermute | solution.py:20
  73.4 12.5 %collective-permute-start.5 = (bf16[3,2,32,512]{3,2,1,0:T(8,128)(2,1)S(1)}, bf16[3,2,32,512]{3,2,1,0:T(8,128)(2,1)S(1)}, u32[]{:S(2)}, u32[]{:S(2)}) collective-permute-start(bf16[3,2,32,512]{3,2,1,0:T(8,128)(2,1)S(1)} %get-tuple-element.55), channel_id=1, source_target_pairs={{0,64},{32,96},{64,0},{96,32},{1,65},{33,97},{65,1},{97,33},{2,66}... | collective-permute-start | bytes 589832 | tf_op jit(solution)/shard_map/ppermute | solution.py:20
  75.1 11.4 %collective-permute-start.6 = (bf16[3,2,32,512]{3,2,1,0:T(8,128)(2,1)S(1)}, bf16[3,2,32,512]{3,2,1,0:T(8,128)(2,1)S(1)}, u32[]{:S(2)}, u32[]{:S(2)}) collective-permute-start(bf16[3,2,32,512]{3,2,1,0:T(8,128)(2,1)S(1)} %get-tuple-element.56), channel_id=1, source_target_pairs={{0,96},{32,0},{64,32},{96,64},{1,97},{33,1},{65,33},{97,65},{2,98}... | collective-permute-start | bytes 589832 | tf_op jit(solution)/shard_map/ppermute | solution.py:20
  90.4 12.4 %collective-permute-start.9 = (bf16[3,2,32,512]{3,2,1,0:T(8,128)(2,1)S(1)}, bf16[3,2,32,512]{3,2,1,0:T(8,128)(2,1)S(1)}, u32[]{:S(2)}, u32[]{:S(2)}) collective-permute-start(bf16[3,2,32,512]{3,2,1,0:T(8,128)(2,1)S(1)} %get-tuple-element.65), channel_id=1, source_target_pairs={{0,32},{32,64},{64,96},{96,0},{1,33},{33,65},{65,97},{97,1},{2,34}... | collective-permute-start | bytes 589832 | tf_op jit(solution)/shard_map/ppermute | solution.py:20
  90.4 12.3 %collective-permute-start.10 = (bf16[3,2,32,512]{3,2,1,0:T(8,128)(2,1)S(1)}, bf16[3,2,32,512]{3,2,1,0:T(8,128)(2,1)S(1)}, u32[]{:S(2)}, u32[]{:S(2)}) collective-permute-start(bf16[3,2,32,512]{3,2,1,0:T(8,128)(2,1)S(1)} %get-tuple-element.66), channel_id=1, source_target_pairs={{0,64},{32,96},{64,0},{96,32},{1,65},{33,97},{65,1},{97,33},{2,66}... | collective-permute-start | bytes 589832 | tf_op jit(solution)/shard_map/ppermute | solution.py:20
  92.2 11.2 %collective-permute-start.11 = (bf16[3,2,32,512]{3,2,1,0:T(8,128)(2,1)S(1)}, bf16[3,2,32,512]{3,2,1,0:T(8,128)(2,1)S(1)}, u32[]{:S(2)}, u32[]{:S(2)}) collective-permute-start(bf16[3,2,32,512]{3,2,1,0:T(8,128)(2,1)S(1)} %get-tuple-element.67), channel_id=1, source_target_pairs={{0,96},{32,0},{64,32},{96,64},{1,97},{33,1},{65,33},{97,65},{2,98}... | collective-permute-start | bytes 589832 | tf_op jit(solution)/shard_map/ppermute | solution.py:20
  106.2 8.5 %copy-start.2 = (f32[3,512,512]{2,1,0:T(8,128)S(1)}, f32[3,512,512]{2,1,0:T(8,128)}, u32[]{:S(2)}) copy-start(f32[3,512,512]{2,1,0:T(8,128)} %param.9) | copy-start | bytes 9437188
  110.9 9.6 %collective-permute-start.12 = (bf16[3,2,32,512]{3,2,1,0:T(8,128)(2,1)S(1)}, bf16[3,2,32,512]{3,2,1,0:T(8,128)(2,1)S(1)}, u32[]{:S(2)}, u32[]{:S(2)}) collective-permute-start(bf16[3,2,32,512]{3,2,1,0:T(8,128)(2,1)S(1)} %get-tuple-element.69), channel_id=1, source_target_pairs={{0,32},{32,64},{64,96},{96,0},{1,33},{33,65},{65,97},{97,1},{2,34}... | collective-permute-start | bytes 589832 | tf_op jit(solution)/shard_map/ppermute | solution.py:20
  111.2 12.3 %collective-permute-start.13 = (bf16[3,2,32,512]{3,2,1,0:T(8,128)(2,1)S(1)}, bf16[3,2,32,512]{3,2,1,0:T(8,128)(2,1)S(1)}, u32[]{:S(2)}, u32[]{:S(2)}) collective-permute-start(bf16[3,2,32,512]{3,2,1,0:T(8,128)(2,1)S(1)} %get-tuple-element.70), channel_id=1, source_target_pairs={{0,64},{32,96},{64,0},{96,32},{1,65},{33,97},{65,1},{97,33},{2,66}... | collective-permute-start | bytes 589832 | tf_op jit(solution)/shard_map/ppermute | solution.py:20
  114.7 8.7 %collective-permute-start.14 = (bf16[3,2,32,512]{3,2,1,0:T(8,128)(2,1)S(1)}, bf16[3,2,32,512]{3,2,1,0:T(8,128)(2,1)S(1)}, u32[]{:S(2)}, u32[]{:S(2)}) collective-permute-start(bf16[3,2,32,512]{3,2,1,0:T(8,128)(2,1)S(1)} %get-tuple-element.71), channel_id=1, source_target_pairs={{0,96},{32,0},{64,32},{96,64},{1,97},{33,1},{65,33},{97,65},{2,98}... | collective-permute-start | bytes 589832 | tf_op jit(solution)/shard_map/ppermute | solution.py:20
  124.9 21.8 %all-to-all-start.2 = ((bf16[32,32,512]{2,1,0:T(8,128)(2,1)}), bf16[32,32,512]{2,1,0:T(8,128)(2,1)S(1)}, u32[]{:S(2)}, u32[]{:S(2)}) async-start(bf16[32,32,512]{2,1,0:T(8,128)(2,1)} %bitcast.14), calls=%async_computation.2 | async-start | bytes 2097152 | tf_op jit(solution)/shard_map/all_to_all | solution.py:293
  129.3 8.6 %collective-permute-start.15 = (bf16[3,2,32,512]{3,2,1,0:T(8,128)(2,1)S(1)}, bf16[3,2,32,512]{3,2,1,0:T(8,128)(2,1)S(1)}, u32[]{:S(2)}, u32[]{:S(2)}) collective-permute-start(bf16[3,2,32,512]{3,2,1,0:T(8,128)(2,1)S(1)} %get-tuple-element.85), channel_id=1, source_target_pairs={{0,32},{32,64},{64,96},{96,0},{1,33},{33,65},{65,97},{97,1},{2,34}... | collective-permute-start | bytes 589832 | tf_op jit(solution)/shard_map/ppermute | solution.py:20
  129.6 12.7 %collective-permute-start.16 = (bf16[3,2,32,512]{3,2,1,0:T(8,128)(2,1)S(1)}, bf16[3,2,32,512]{3,2,1,0:T(8,128)(2,1)S(1)}, u32[]{:S(2)}, u32[]{:S(2)}) collective-permute-start(bf16[3,2,32,512]{3,2,1,0:T(8,128)(2,1)S(1)} %get-tuple-element.86), channel_id=1, source_target_pairs={{0,64},{32,96},{64,0},{96,32},{1,65},{33,97},{65,1},{97,33},{2,66}... | collective-permute-start | bytes 589832 | tf_op jit(solution)/shard_map/ppermute | solution.py:20
  133.0 9.5 %collective-permute-start.17 = (bf16[3,2,32,512]{3,2,1,0:T(8,128)(2,1)S(1)}, bf16[3,2,32,512]{3,2,1,0:T(8,128)(2,1)S(1)}, u32[]{:S(2)}, u32[]{:S(2)}) collective-permute-start(bf16[3,2,32,512]{3,2,1,0:T(8,128)(2,1)S(1)} %get-tuple-element.87), channel_id=1, source_target_pairs={{0,96},{32,0},{64,32},{96,64},{1,97},{33,1},{65,33},{97,65},{2,98}... | collective-permute-start | bytes 589832 | tf_op jit(solution)/shard_map/ppermute | solution.py:20
  147.8 21.9 %all-to-all-start.3 = ((bf16[32,32,512]{2,1,0:T(8,128)(2,1)}), bf16[32,32,512]{2,1,0:T(8,128)(2,1)S(1)}, u32[]{:S(2)}, u32[]{:S(2)}) async-start(bf16[32,32,512]{2,1,0:T(8,128)(2,1)} %bitcast.15), calls=%async_computation.3 | async-start | bytes 2097152 | tf_op jit(solution)/shard_map/all_to_all | solution.py:293
  152.4 12.9 %collective-permute-start.20 = (bf16[32,7168]{1,0:T(8,128)(2,1)S(1)}, bf16[32,7168]{1,0:T(8,128)(2,1)S(1)}, u32[]{:S(2)}, u32[]{:S(2)}) collective-permute-start(bf16[32,7168]{1,0:T(8,128)(2,1)S(1)} %unpack.2.refs_0_), channel_id=1, source_target_pairs={{0,96},{32,0},{64,32},{96,64},{1,97},{33,1},{65,33},{97,65},{2,98}... | collective-permute-start | bytes 1376264 | tf_op jit(solution)/shard_map/ppermute | solution.py:20
  155.1 14.0 %collective-permute-start.18 = (bf16[32,7168]{1,0:T(8,128)(2,1)S(1)}, bf16[32,7168]{1,0:T(8,128)(2,1)S(1)}, u32[]{:S(2)}, u32[]{:S(2)}) collective-permute-start(bf16[32,7168]{1,0:T(8,128)(2,1)S(1)} %unpack.2.refs_0_), channel_id=1, source_target_pairs={{0,32},{32,64},{64,96},{96,0},{1,33},{33,65},{65,97},{97,1},{2,34}... | collective-permute-start | bytes 1376264 | tf_op jit(solution)/shard_map/ppermute | solution.py:20
  165.3 8.3 %collective-permute-start.21 = (bf16[16,7168]{1,0:T(8,128)(2,1)S(1)}, bf16[16,7168]{1,0:T(8,128)(2,1)S(1)}, u32[]{:S(2)}, u32[]{:S(2)}) collective-permute-start(bf16[16,7168]{1,0:T(8,128)(2,1)S(1)} %slice.38), channel_id=1, source_target_pairs={{0,96},{32,0},{64,32},{96,64},{1,97},{33,1},{65,33},{97,65},{2,98}... | collective-permute-start | bytes 688136 | tf_op jit(solution)/shard_map/ppermute | solution.py:20
  169.1 8.0 %collective-permute-start.19 = (bf16[16,7168]{1,0:T(8,128)(2,1)S(1)}, bf16[16,7168]{1,0:T(8,128)(2,1)S(1)}, u32[]{:S(2)}, u32[]{:S(2)}) collective-permute-start(bf16[16,7168]{1,0:T(8,128)(2,1)S(1)} %slice.37), channel_id=1, source_target_pairs={{0,32},{32,64},{64,96},{96,0},{1,33},{33,65},{65,97},{97,1},{2,34}... | collective-permute-start | bytes 688136 | tf_op jit(solution)/shard_map/ppermute | solution.py:20
  177.1 11.9 %collective-permute-start.23 = (bf16[32,7168]{1,0:T(8,128)(2,1)S(1)}, bf16[32,7168]{1,0:T(8,128)(2,1)S(1)}, u32[]{:S(2)}, u32[]{:S(2)}) collective-permute-start(bf16[32,7168]{1,0:T(8,128)(2,1)S(1)} %unpack.3.refs_0_), channel_id=1, source_target_pairs={{0,32},{32,64},{64,96},{96,0},{1,33},{33,65},{65,97},{97,1},{2,34}... | collective-permute-start | bytes 1376264 | tf_op jit(solution)/shard_map/ppermute | solution.py:20
  177.1 11.9 %collective-permute-start.22 = (bf16[32,7168]{1,0:T(8,128)(2,1)S(1)}, bf16[32,7168]{1,0:T(8,128)(2,1)S(1)}, u32[]{:S(2)}, u32[]{:S(2)}) collective-permute-start(bf16[32,7168]{1,0:T(8,128)(2,1)S(1)} %unpack.3.refs_0_), channel_id=1, source_target_pairs={{0,96},{32,0},{64,32},{96,64},{1,97},{33,1},{65,33},{97,65},{2,98}... | collective-permute-start | bytes 1376264 | tf_op jit(solution)/shard_map/ppermute | solution.py:20
  189.0 6.6 %collective-permute-start.25 = (bf16[16,7168]{1,0:T(8,128)(2,1)S(1)}, bf16[16,7168]{1,0:T(8,128)(2,1)S(1)}, u32[]{:S(2)}, u32[]{:S(2)}) collective-permute-start(bf16[16,7168]{1,0:T(8,128)(2,1)S(1)} %slice.33), channel_id=1, source_target_pairs={{0,96},{32,0},{64,32},{96,64},{1,97},{33,1},{65,33},{97,65},{2,98}... | collective-permute-start | bytes 688136 | tf_op jit(solution)/shard_map/ppermute | solution.py:20
  192.0 7.2 %collective-permute-start.24 = (bf16[16,7168]{1,0:T(8,128)(2,1)S(1)}, bf16[16,7168]{1,0:T(8,128)(2,1)S(1)}, u32[]{:S(2)}, u32[]{:S(2)}) collective-permute-start(bf16[16,7168]{1,0:T(8,128)(2,1)S(1)} %slice.32), channel_id=1, source_target_pairs={{0,32},{32,64},{64,96},{96,0},{1,33},{33,65},{65,97},{97,1},{2,34}... | collective-permute-start | bytes 688136 | tf_op jit(solution)/shard_map/ppermute | solution.py:20
  (4 other events, 12.9 us)
